TPU v7x, 256 devices: a whole 4x4x8 slice. The times are simulated.
256 devices in a mesh: inst: 16 (over z_hi, y), ep: 16 (over x, z_lo, core).
Axes of the slice: x: 4, y: 4, z: 8 (z_hi: 4, z_lo: 2; z = z_hi * 2 + z_lo), core: 2. Of those that a mesh axis runs over, the one named last changes fastest.
Arguments:
- queries: bfloat16 [16, 16, 4, 8192], P('inst', 'ep'), may hold values from -120 to 120
- kv_cache: bfloat16 [16, 16, 2, 16, 64, 512], P('inst', 'ep'), may hold values from -6 to 6
- ctx_len: int32 [16, 16, 4], P('inst', 'ep'), may hold values from 1 to 512, 768 in all within a row
- page_order: int32 [16, 16, 16], P('inst', 'ep'), may hold values from 0 to 15, each once within a row
- hidden_in: bfloat16 [32768, 4096], P(('inst', 'ep')), may hold values from -6 to 6
- routes: int32 [32768, 1], P(('inst', 'ep')), may hold values from 0 to 3; in each aligned block of 128 rows (0 to 127, 128 to 255, ...) at most 64 rows name the same one
- w_gate: bfloat16 [16, 4096, 384], P('ep'), may hold values from -0.09375 to 0.09375
- w_up: bfloat16 [16, 4096, 384], P('ep'), may hold values from -0.09375 to 0.09375
- w_down: bfloat16 [16, 384, 4096], P('ep'), may hold values from -0.15625 to 0.15625
Outputs:
- attn_out: bfloat16 [16, 16, 4, 8192], P('inst', 'ep')
- moe_out: bfloat16 [32768, 4096], P(('inst', 'ep'))
- moved_pages: bfloat16 [16, 16, 2, 8, 64, 512], P('inst', 'ep')
Inputs may be any that keep to these rules, and one draw needn't show every extreme that they name: `ctx_len`: the lengths of one device's requests sum to 768, and one of them is 512. `page_order`: each device's list holds each of its pages once. `routes`: the 128 tokens of one device name each expert at most 64 times, a bound that some block reaches.
All inputs are finite; a program needn't handle non-finite values.
Results may differ from a plain program's by a relative error of at most 0.011.
Values may be sent and summed in bfloat16 or wider, within the bound.
No kernel may reach another device: no remote copies, remote signals or barrier semaphores. Data moves between devices by JAX's collectives and lax.ppermute only.
A program may use at most 128 MiB of HBM per device.

v0:
```python
import jax
import jax.numpy as jnp
from jax import lax
from jax.sharding import PartitionSpec as P

HEADS = 64
KV_HEADS = 4
HEAD_DIM = 128
FF_SPLIT = 4
PAGE = 64
MAXP = 8


def from_behind(block, axis, distance):
    devices = range(lax.axis_size(axis))
    route = [(i - distance, i) for i in devices if i - distance in devices]
    return lax.ppermute(block, axis, route)


def gather_pages(kv_cache, ctx_len, page_order):
    pages = (ctx_len + PAGE - 1) // PAGE
    start = jnp.cumsum(pages) - pages
    slots = jnp.minimum(
        start[:, None] + jnp.arange(MAXP, dtype=jnp.int32)[None, :], page_order.shape[0] - 1
    )
    return (kv_cache[:, page_order[slots]], pages)


def attend(queries, kv_pages, ctx_len):
    reqs = queries.shape[0]
    group = HEADS // KV_HEADS
    keys = kv_pages[0].reshape(reqs, MAXP * PAGE, KV_HEADS, HEAD_DIM)
    values = kv_pages[1].reshape(reqs, MAXP * PAGE, KV_HEADS, HEAD_DIM)
    query = queries.reshape(reqs, KV_HEADS, group, HEAD_DIM)
    scores = jnp.einsum(
        "rkgd,rtkd->rkgt", query, keys, preferred_element_type=jnp.float32
    ) * HEAD_DIM ** (-0.5)
    inside = (jnp.arange(MAXP * PAGE, dtype=jnp.int32)[None, :] < ctx_len[:, None])[
        :, None, None, :
    ]
    scores = jnp.where(inside, scores, -1e30)
    top = jnp.max(scores, axis=-1, keepdims=True)
    expo = jnp.exp(scores - top)
    probs = (expo / jnp.sum(expo, axis=-1, keepdims=True)).astype(jnp.bfloat16)
    mixed = jnp.einsum("rkgt,rtkd->rkgd", probs, values, preferred_element_type=jnp.float32)
    return mixed.reshape(reqs, HEADS * HEAD_DIM).astype(jnp.bfloat16)


def expert_part(rows, gate_w, up_w, down_w):
    gate = jnp.dot(rows, gate_w, preferred_element_type=jnp.float32)
    upper = jnp.dot(rows, up_w, preferred_element_type=jnp.float32)
    hidden = (jax.nn.silu(gate) * upper).astype(jnp.bfloat16)
    return jnp.dot(hidden, down_w, preferred_element_type=jnp.float32).astype(jnp.bfloat16)


def local(queries, kv_cache, ctx_len, page_order, hidden_in, routes, w_gate, w_up, w_down):
    lengths = ctx_len[0, 0]
    kv_pages, pages = gather_pages(kv_cache[0, 0], lengths, page_order[0, 0])
    keep = (jnp.arange(MAXP, dtype=jnp.int32) < pages[0])[None, :, None, None]
    leaving = jnp.where(keep, kv_pages[:, 0], jnp.zeros_like(kv_pages[:, 0]))
    arrived = from_behind(leaving, "inst", lax.axis_size("inst") // 2)
    attn_out = attend(queries[0, 0], kv_pages, lengths)
    devices = lax.axis_size("ep")
    groups = devices // FF_SPLIT
    tokens = hidden_in.shape[0]
    width = hidden_in.shape[1]
    cap = min(tokens, 8 * tokens // devices)
    gate_w, up_w, down_w = (w_gate[0], w_up[0], w_down[0])
    expert = routes[:, 0]
    match = (expert[:, None] == jnp.arange(groups, dtype=jnp.int32)[None, :]).astype(jnp.int32)
    rank = jnp.cumsum(match, axis=0) - match
    slot = jnp.sum(rank * match, axis=1)
    target = expert * cap + slot
    onehot = (target[None, :] == jnp.arange(groups * cap, dtype=jnp.int32)[:, None]).astype(
        jnp.bfloat16
    )
    buffer = jnp.dot(onehot, hidden_in, preferred_element_type=jnp.float32).astype(jnp.bfloat16)
    sending = jnp.repeat(buffer.reshape(groups, cap, width), FF_SPLIT, axis=0)
    rows = lax.all_to_all(sending, "ep", split_axis=0, concat_axis=0, tiled=True)
    count = rows.shape[1]
    partial_value = expert_part(rows.reshape(devices * count, width), gate_w, up_w, down_w)
    back = lax.all_to_all(
        partial_value.reshape(devices, count, width), "ep", split_axis=0, concat_axis=0, tiled=True
    )
    summed = (
        back.reshape(groups, FF_SPLIT, cap, width)
        .astype(jnp.float32)
        .sum(axis=1)
        .astype(jnp.bfloat16)
    )
    moe_out = summed.reshape(groups * cap, width)[target]
    return (attn_out[None, None], moe_out, arrived[None, None])


def solution(mesh):
    placed = (
        P("inst", "ep", None, None),
        P("inst", "ep", None, None, None, None),
        P("inst", "ep", None),
        P("inst", "ep", None),
        P(("inst", "ep"), None),
        P(("inst", "ep"), None),
        P("ep", None, None),
        P("ep", None, None),
        P("ep", None, None),
    )
    return jax.shard_map(
        local,
        mesh=mesh,
        in_specs=placed,
        out_specs=(
            P("inst", "ep", None, None),
            P(("inst", "ep"), None),
            P("inst", "ep", None, None, None, None),
        ),
        check_vma=False,
    )
```

profile of v0, /device:TPU:216, one launch (start us, length us, event | category | flops | bytes accessed | tf_op | source)
XLA Modules:
  0.0 280.5 jit_solution(10894787974428327088)
XLA Ops:
  0.6 0.0 copy-start
  0.6 0.9 fusion.29
  1.5 0.2 reduce_window_sum.18
  1.7 0.8 select_reduce_fusion
  2.5 0.7 multiply_add_fusion
  3.2 1.9 convolution_convert_fusion.1
  5.1 1.0 broadcast_in_dim.28
  6.2 0.0 copy-start.9
  6.2 100.1 %all_to_all.10 = bf16[16,64,4096]{2,1,0:T(8,128)(2,1)S(1)} all-to-all(bf16[16,64,4096]{2,1,0:T(8,128)(2,1)S(1)} %bitcast.80), channel_id=1, replica_groups=mesh['inst'=16,'ep'=16] {'ep'}, dimensions={0} | all-to-all | bytes 16777216 | tf_op jit(solution)/shard_map/all_to_all | solution.py:79
  106.3 0.0 copy-done.9
  106.3 0.0 copy-start.10
  106.3 4.5 %fusion.4 = f32[1024,384]{1,0:T(8,128)S(1)} fusion(bf16[1024,4096]{1,0:T(8,128)(2,1)S(1)} %bitcast.86, bf16[1,4096,384]{2,1,0:T(8,128)(2,1)S(1)} %copy-done.9), kind=kOutput, calls=%fused_computation.10 | convolution fusion | flops 3221225472 | bytes 13107200 | tf_op jit(solution)/shard_map/dot_general | solution.py:50
  110.7 0.0 copy-done.10
  110.8 4.6 %multiply_convert_fusion = bf16[1024,384]{1,0:T(8,128)(2,1)S(1)} fusion(f32[1024,384]{1,0:T(8,128)S(1)} %fusion.4, bf16[1024,4096]{1,0:T(8,128)(2,1)S(1)} %bitcast.87, bf16[1,4096,384]{2,1,0:T(8,128)(2,1)S(1)} %copy-done.10), kind=kOutput, calls=%fused_computation.16 | convolution fusion | flops 3223584768 | bytes 13893632 | tf_op jit(solution)/shard_map/dot_general | solution.py:51
  115.3 0.0 copy-done
  115.3 6.7 %convolution_convert_fusion = bf16[1024,4096]{1,0:T(8,128)(2,1)} fusion(bf16[1024,384]{1,0:T(8,128)(2,1)S(1)} %multiply_convert_fusion, bf16[1,384,4096]{2,1,0:T(8,128)(2,1)S(1)} %copy-done), kind=kOutput, calls=%fused_computation.5 | convolution fusion | flops 3225419776 | bytes 12320768 | tf_op jit(solution)/shard_map/dot_general | solution.py:53
  122.0 4.9 %all-to-all-start.1 = ((bf16[16,64,4096]{2,1,0:T(8,128)(2,1)}), bf16[16,64,4096]{2,1,0:T(8,128)(2,1)}, u32[]{:S(2)}, u32[]{:S(2)}) async-start(bf16[16,64,4096]{2,1,0:T(8,128)(2,1)} %bitcast.85), calls=%async_computation.1 | async-start | bytes 16777216 | tf_op jit(solution)/shard_map/all_to_all | solution.py:82
  126.9 0.0 copy-done.8
  126.9 0.0 copy-start.3
  126.9 0.2 reduce-window.8
  127.1 0.1 compare_select_fusion.1
  127.2 0.1 reshape.214
  127.3 0.0 copy-done.2
  127.3 0.7 gather_fusion
  128.0 0.1 gather.12
  128.1 0.1 reshape.222
  128.2 0.3 copy-done.3
  128.5 2.7 gather_fusion.1
  131.3 1.4 fusion.26
  132.6 1.5 collective-permute-start
  134.1 4.1 %fusion.32 = (bf16[1,4,8,64,512]{4,3,0,2,1:T(8,128)(2,1)}, bf16[1,4,8,64,512]{4,3,0,2,1:T(8,128)(2,1)S(1)}) fusion(bf16[2,4,8,64,512]{4,3,0,2,1:T(8,128)(2,1)} %bitcast.82), kind=kLoop, calls=%fused_computation.54 | loop fusion | bytes 8388608 | tf_op jit(solution)/shard_map/slice | solution.py:32
  138.2 0.1 iota_compare_fusion.3
  138.2 4.0 %reshape_squeeze.9 = bf16[4,512,4,128]{3,2,1,0:T(4,128)(2,1)} reshape(bf16[1,4,8,64,512]{4,3,0,2,1:T(8,128)(2,1)} %get-tuple-element.8) | data formatting | bytes 4194304 | tf_op jit(solution)/shard_map/reshape;squeeze | solution.py:32
  142.2 0.0 copy-done.6
  142.2 2.1 reshape_squeeze.11
  144.3 2.4 fusion.20
  146.7 0.8 copy-done.5
  147.5 0.2 fusion.33
  147.8 0.0 copy-done.4
  147.8 1.8 fusion.23
  149.6 0.7 convert_element_type.33
  150.3 0.0 copy-done.7
  150.3 115.6 %collective-permute-done = bf16[2,8,64,512]{3,2,0,1:T(8,128)(2,1)} collective-permute-done((bf16[2,8,64,512]{3,2,0,1:T(8,128)(2,1)S(1)}, bf16[2,8,64,512]{3,2,0,1:T(8,128)(2,1)}, u32[]{:S(2)}, u32[]{:S(2)}) %collective-permute-start) | collective-permute-done | bytes 1048608 | tf_op jit(solution)/shard_map/ppermute | solution.py:17
  265.9 2.3 copy.14
  268.2 0.0 all-to-all-done.1
  268.2 7.1 %bitcast_reduce_fusion = bf16[4,64,4096]{2,1,0:T(8,128)(2,1)} fusion(bf16[16,64,4096]{2,1,0:T(8,128)(2,1)} %all-to-all-done.1), kind=kLoop, calls=%fused_computation.4 | loop fusion | flops 3145728 | bytes 10485760 | tf_op jit(solution)/shard_map/reduce_sum | solution.py:88
  275.3 5.2 %gather_fusion.2 = bf16[128,4096]{1,0:T(8,128)(2,1)} fusion(bf16[256,4096]{1,0:T(8,128)(2,1)} %bitcast.79, s32[1024]{0:T(1024)S(1)} %pad_clamp_fusion), kind=kCustom, calls=%fused_computation.2 | custom fusion | bytes 2097664 | tf_op jit(solution)/shard_map/gather | solution.py:91
  280.5 0.0 copy-done.1
  (16 shorter events, 0.1 us)
Async XLA Ops:
  0.6 114.7 %copy-start = (bf16[1,384,4096]{2,1,0:T(8,128)(2,1)S(1)}, bf16[1,384,4096]{2,1,0:T(8,128)(2,1)}, u32[]{:S(2)}) copy-start(bf16[1,384,4096]{2,1,0:T(8,128)(2,1)} %param.17) | copy-start | bytes 9437188
  6.2 100.1 %copy-start.9 = (bf16[1,4096,384]{2,1,0:T(8,128)(2,1)S(1)}, bf16[1,4096,384]{2,1,0:T(8,128)(2,1)}, u32[]{:S(2)}) copy-start(bf16[1,4096,384]{2,1,0:T(8,128)(2,1)} %param.15) | copy-start | bytes 9437188
  106.3 4.5 %copy-start.10 = (bf16[1,4096,384]{2,1,0:T(8,128)(2,1)S(1)}, bf16[1,4096,384]{2,1,0:T(8,128)(2,1)}, u32[]{:S(2)}) copy-start(bf16[1,4096,384]{2,1,0:T(8,128)(2,1)} %param.16) | copy-start | bytes 9437188
  122.0 4.9 %copy-start.8 = (s32[1,1,4]{2,1,0:T(1,128)S(1)}, s32[1,1,4]{2,1,0:T(1,128)}, u32[]{:S(2)}) copy-start(s32[1,1,4]{2,1,0:T(1,128)} %param.11) | copy-start | bytes 52
  122.0 5.3 %copy-start.2 = (s32[1,1,16]{2,1,0:T(1,128)S(1)}, s32[1,1,16]{2,1,0:T(1,128)}, u32[]{:S(2)}) copy-start(s32[1,1,16]{2,1,0:T(1,128)} %param.12) | copy-start | bytes 196
  122.0 146.2 %all-to-all-start.1 = ((bf16[16,64,4096]{2,1,0:T(8,128)(2,1)}), bf16[16,64,4096]{2,1,0:T(8,128)(2,1)}, u32[]{:S(2)}, u32[]{:S(2)}) async-start(bf16[16,64,4096]{2,1,0:T(8,128)(2,1)} %bitcast.85), calls=%async_computation.1 | async-start | bytes 16777216 | tf_op jit(solution)/shard_map/all_to_all | solution.py:82
  126.9 1.6 copy-start.3
  132.6 133.3 %collective-permute-start = (bf16[2,8,64,512]{3,2,0,1:T(8,128)(2,1)S(1)}, bf16[2,8,64,512]{3,2,0,1:T(8,128)(2,1)}, u32[]{:S(2)}, u32[]{:S(2)}) collective-permute-start(bf16[2,8,64,512]{3,2,0,1:T(8,128)(2,1)S(1)} %fusion.26), channel_id=1, source_target_pairs={{0,128},{16,144},{32,160},{48,176},{64,192},{80,208},{96,224},{112... | collective-permute-start | bytes 3145736 | tf_op jit(solution)/shard_map/ppermute | solution.py:17
  138.2 4.1 %copy-start.6 = (bf16[1,1,4,8192]{3,2,1,0:T(4,128)(2,1)S(1)}, bf16[1,1,4,8192]{3,2,1,0:T(4,128)(2,1)}, u32[]{:S(2)}) copy-start(bf16[1,1,4,8192]{3,2,1,0:T(4,128)(2,1)} %param.9) | copy-start | bytes 196612
  144.3 3.4 %copy-start.4 = (bf16[4,512,4,128]{3,2,1,0:T(4,128)(2,1)S(1)}, bf16[4,512,4,128]{3,2,1,0:T(4,128)(2,1)}, u32[]{:S(2)}) copy-start(bf16[4,512,4,128]{3,2,1,0:T(4,128)(2,1)} %reshape_squeeze.11) | copy-start | bytes 6291460
  146.7 0.8 copy-start.5
  147.5 2.7 copy-start.7
  275.3 5.2 %copy-start.1 = (bf16[1,384,4096]{2,1,0:T(8,128)(2,1)S(1)}, bf16[1,384,4096]{2,1,0:T(8,128)(2,1)}, u32[]{:S(2)}) copy-start(bf16[1,384,4096]{2,1,0:T(8,128)(2,1)} %param.17) | copy-start | bytes 9437188
where the time goes:
time: 281 us; the launch traced here: 280 us
  waiting for transfers between devices  116 us (41%)
  blocking collectives  100 us (36%)
  local copies, waits for them, and re-layouts  24.2 us (9%)
  matrix products  21.8 us (8%)
  other arithmetic  11.7 us (4%)
  starting transfers between devices  6.34 us (2%)
    ppermute x1, waiting for transfers between devices, from_behind(): return lax.ppermute(block, axis, route)  116 us
    all_to_all x1, blocking collectives, local(): lax.all_to_all(sending, 'ep', split_axis=0, concat_axis=0, tiled=True)  100 us
    reduce_sum x1, other arithmetic, local(): summed = back.reshape(groups, FF_SPLIT, cap, width).astype(jnp.float32).s...  7.09 us
    dot_general x1, matrix products, expert_part(): jnp.dot(hidden, down_w, preferred_element_type=jnp.float32)  6.65 us
  transfers between devices with their start and end apart: 2, of which 1 were waited for; matrix products, arithmetic and copies ran while one was open for 8% of the time, Pallas kernels for 0%

commit v1 on v0

--- a/solution.py
+++ b/solution.py
@@ -6,15 +6,27 @@
 HEADS = 64
 KV_HEADS = 4
 HEAD_DIM = 128
-FF_SPLIT = 4
 PAGE = 64
 MAXP = 8
+CAP = 64
+HALF = 32
+NX, NY, NZ, NC = 4, 4, 8, 2
 
 
-def from_behind(block, axis, distance):
-    devices = range(lax.axis_size(axis))
-    route = [(i - distance, i) for i in devices if i - distance in devices]
-    return lax.ppermute(block, axis, route)
+def device_id(x, y, z, c):
+    x, y, z = x % NX, y % NY, z % NZ
+    return ((z // 2) * NY + y) * 16 + x * 4 + (z % 2) * 2 + c
+
+
+def shifted(block, dx=0, dz=0, dc=0):
+    route = [
+        (device_id(x, y, z, c), device_id(x + dx, y, z + dz, c ^ dc))
+        for x in range(NX)
+        for y in range(NY)
+        for z in range(NZ)
+        for c in range(NC)
+    ]
+    return lax.ppermute(block, ("inst", "ep"), route)
 
 
 def gather_pages(kv_cache, ctx_len, page_order):
@@ -23,7 +35,7 @@
     slots = jnp.minimum(
         start[:, None] + jnp.arange(MAXP, dtype=jnp.int32)[None, :], page_order.shape[0] - 1
     )
-    return (kv_cache[:, page_order[slots]], pages)
+    return kv_cache[:, page_order[slots]], pages
 
 
 def attend(queries, kv_pages, ctx_len):
@@ -53,43 +65,61 @@
     return jnp.dot(hidden, down_w, preferred_element_type=jnp.float32).astype(jnp.bfloat16)
 
 
+def add(a, b):
+    return (a.astype(jnp.float32) + b.astype(jnp.float32)).astype(jnp.bfloat16)
+
+
+def spread(pieces):
+    size = CAP * len(pieces)
+    own = pieces[0] if len(pieces) == 1 else jnp.concatenate(pieces, 0)
+    above = shifted(own[: size // 2], dz=1)
+    below = shifted(own[size // 2 :], dz=-1)
+    mine = jnp.concatenate([own, above, below], 0)
+    return jnp.concatenate([mine, shifted(mine, dc=1)], 0)
+
+
+def collect(part):
+    size = part.shape[0] // 4
+    mine = add(part[: 2 * size], shifted(part[2 * size :], dc=1))
+    first = shifted(mine[size : size + size // 2], dz=-1)
+    second = shifted(mine[size + size // 2 :], dz=1)
+    own = add(mine[:size], jnp.concatenate([first, second], 0))
+    return [own[i : i + CAP] for i in range(0, size, CAP)]
+
+
 def local(queries, kv_cache, ctx_len, page_order, hidden_in, routes, w_gate, w_up, w_down):
     lengths = ctx_len[0, 0]
     kv_pages, pages = gather_pages(kv_cache[0, 0], lengths, page_order[0, 0])
     keep = (jnp.arange(MAXP, dtype=jnp.int32) < pages[0])[None, :, None, None]
     leaving = jnp.where(keep, kv_pages[:, 0], jnp.zeros_like(kv_pages[:, 0]))
-    arrived = from_behind(leaving, "inst", lax.axis_size("inst") // 2)
+    arrived = lax.ppermute(leaving, "inst", [(i, i + 8) for i in range(8)])
     attn_out = attend(queries[0, 0], kv_pages, lengths)
-    devices = lax.axis_size("ep")
-    groups = devices // FF_SPLIT
-    tokens = hidden_in.shape[0]
-    width = hidden_in.shape[1]
-    cap = min(tokens, 8 * tokens // devices)
-    gate_w, up_w, down_w = (w_gate[0], w_up[0], w_down[0])
-    expert = routes[:, 0]
-    match = (expert[:, None] == jnp.arange(groups, dtype=jnp.int32)[None, :]).astype(jnp.int32)
+
+    x = lax.axis_index("ep") // 4
+    weights = (w_gate[0], w_up[0], w_down[0])
+    rel = jnp.bitwise_and(routes[:, 0] - x, 3)
+    match = (rel[:, None] == jnp.arange(NX, dtype=jnp.int32)[None, :]).astype(jnp.int32)
     rank = jnp.cumsum(match, axis=0) - match
     slot = jnp.sum(rank * match, axis=1)
-    target = expert * cap + slot
-    onehot = (target[None, :] == jnp.arange(groups * cap, dtype=jnp.int32)[:, None]).astype(
+    target = rel * CAP + slot
+    onehot = (target[None, :] == jnp.arange(NX * CAP, dtype=jnp.int32)[:, None]).astype(
         jnp.bfloat16
     )
     buffer = jnp.dot(onehot, hidden_in, preferred_element_type=jnp.float32).astype(jnp.bfloat16)
-    sending = jnp.repeat(buffer.reshape(groups, cap, width), FF_SPLIT, axis=0)
-    rows = lax.all_to_all(sending, "ep", split_axis=0, concat_axis=0, tiled=True)
-    count = rows.shape[1]
-    partial_value = expert_part(rows.reshape(devices * count, width), gate_w, up_w, down_w)
-    back = lax.all_to_all(
-        partial_value.reshape(devices, count, width), "ep", split_axis=0, concat_axis=0, tiled=True
-    )
-    summed = (
-        back.reshape(groups, FF_SPLIT, cap, width)
-        .astype(jnp.float32)
-        .sum(axis=1)
-        .astype(jnp.bfloat16)
-    )
-    moe_out = summed.reshape(groups * cap, width)[target]
-    return (attn_out[None, None], moe_out, arrived[None, None])
+    piece = [buffer[i * CAP : (i + 1) * CAP] for i in range(NX)]
+    got = [piece[0]] + [shifted(piece[d], dx=d) for d in (1, 3, 2)]
+    groups = [[got[0]], [got[1], got[2]], [got[3]]]
+    back = []
+    for g in groups:
+        back += collect(expert_part(spread(g), *weights))
+    home = [back[0], shifted(back[1], dx=-1), shifted(back[3], dx=-2), shifted(back[2], dx=-3)]
+    moe_out = lax.dot_general(
+        onehot,
+        jnp.concatenate(home, 0),
+        (((0,), (0,)), ((), ())),
+        preferred_element_type=jnp.float32,
+    ).astype(jnp.bfloat16)
+    return attn_out[None, None], moe_out, arrived[None, None]
 
 
 def solution(mesh):

time: 281 us -> 219 us (0.78)
  the two profiles are of different devices: /device:TPU:216 before, /device:TPU:80 now
where the time goes in v1:
time: 219 us; the launch traced here: 218 us
  waiting for transfers between devices  81.3 us (37%)
  matrix products  43.2 us (20%)
  local copies, waits for them, and re-layouts  43.1 us (20%)
  starting transfers between devices  32.8 us (15%)
  other arithmetic  16.3 us (7%)
    ppermute x24, waiting for transfers between devices, shifted(): return lax.ppermute(block, ('inst', 'ep'), route)  81.3 us
    ppermute x24, starting transfers between devices, shifted(): return lax.ppermute(block, ('inst', 'ep'), route)  25.5 us
    dot_general x3, matrix products, expert_part(): jnp.dot(hidden, down_w, preferred_element_type=jnp.float32)  22.6 us
    unnamed x43, local copies, waits for them, and re-layouts  9.5 us
    dot_general x2, matrix products, expert_part(): upper = jnp.dot(rows, up_w, preferred_element_type=jnp.float32)  9.36 us
    ppermute x1, starting transfers between devices, local(): arrived = lax.ppermute(leaving, 'inst', [(i, i + 8) for i in range(8)])  7.35 us
    slice x3, local copies, waits for them, and re-layouts, collect(): mine = add(part[:2 * size], shifted(part[2 * size:], dc=1))  6.76 us
    concatenate x3, other arithmetic, spread(): mine = jnp.concatenate([own, above, below], 0)  6.17 us
  transfers between devices with their start and end apart: 25, of which 9 were waited for; matrix products, arithmetic and copies ran while one was open for 42% of the time, Pallas kernels for 0%

profile of v1, /device:TPU:80, one launch (start us, length us, event | category | flops | bytes accessed | tf_op | source)
XLA Modules:
  0.0 217.7 jit_solution(5104614449296107128)
XLA Ops:
  2.6 1.9 convolution_convert_fusion.1
  5.3 1.9 collective-permute-start
  7.3 1.3 fusion.71
  8.6 3.0 %collective-permute-start.15 = (bf16[64,4096]{1,0:T(8,128)(2,1)}, bf16[64,4096]{1,0:T(8,128)(2,1)}, u32[]{:S(2)}, u32[]{:S(2)}) collective-permute-start(bf16[64,4096]{1,0:T(8,128)(2,1)} %get-tuple-element.11), channel_id=1, source_target_pairs={{0,8},{1,9},{2,10},{3,11},{64,72},{65,73},{66,74},{67,75},{128,136... | collective-permute-start | bytes 1572872 | tf_op jit(solution)/shard_map/ppermute | solution.py:29
  12.2 2.6 %collective-permute-start.7 = (bf16[64,4096]{1,0:T(8,128)(2,1)}, bf16[64,4096]{1,0:T(8,128)(2,1)}, u32[]{:S(2)}, u32[]{:S(2)}) collective-permute-start(bf16[64,4096]{1,0:T(8,128)(2,1)} %get-tuple-element.12), channel_id=1, source_target_pairs={{0,12},{1,13},{2,14},{3,15},{64,76},{65,77},{66,78},{67,79},{128,1... | collective-permute-start | bytes 1572872 | tf_op jit(solution)/shard_map/ppermute | solution.py:29
  16.1 4.4 %gather_fusion.1 = bf16[32,2,64,512]{3,2,1,0:T(8,128)(2,1)} fusion(bf16[2,16,64,512]{3,2,1,0:T(8,128)(2,1)} %bitcast.93, s32[1024]{0:T(1024)S(1)} %pad_clamp_fusion), kind=kCustom, calls=%fused_computation.1 | custom fusion | bytes 8388736 | tf_op jit(solution)/shard_map/gather | solution.py:38
  20.5 4.8 %fusion.70 = (bf16[1,4,8,64,512]{4,3,0,2,1:T(8,128)(2,1)}, bf16[1,4,8,64,512]{4,3,0,2,1:T(8,128)(2,1)}) fusion(bf16[2,4,8,64,512]{4,3,0,2,1:T(8,128)(2,1)} %bitcast.91), kind=kLoop, calls=%fused_computation.101 | loop fusion | bytes 8388608 | tf_op jit(solution)/shard_map/slice | solution.py:44
  25.3 4.1 %reshape_squeeze.9 = bf16[4,512,4,128]{3,2,1,0:T(4,128)(2,1)} reshape(bf16[1,4,8,64,512]{4,3,0,2,1:T(8,128)(2,1)} %get-tuple-element.8) | data formatting | bytes 4194304 | tf_op jit(solution)/shard_map/reshape;squeeze | solution.py:44
  29.4 2.2 %fusion.35 = f32[4,4,16,512]{3,2,1,0:T(8,128)S(1)} fusion(bf16[4,4,16,128]{3,2,1,0:T(8,128)(2,1)S(1)} %bitcast.96, bf16[4,512,4,128]{3,2,1,0:T(4,128)(2,1)} %reshape_squeeze.9, pred[4,512]{1,0:T(4,128)(4,1)S(1)} %iota_compare_fusion.4), kind=kOutput, calls=%fused_computation.44 | convolution fusion | flops 33816576 | bytes 2689024 | tf_op jit(solution)/shard_map/rkgd,rtkd->rkgt/dot_general | solution.py:47
  32.7 4.0 %reshape_squeeze.11 = bf16[4,512,4,128]{3,2,1,0:T(4,128)(2,1)} reshape(bf16[1,4,8,64,512]{4,3,0,2,1:T(8,128)(2,1)} %get-tuple-element.9) | data formatting | bytes 4194304 | tf_op jit(solution)/shard_map/reshape;squeeze | solution.py:45
  36.8 2.5 %fusion.38 = bf16[4,4,16,128]{3,2,1,0:T(8,128)(2,1)S(1)} fusion(bf16[4,512,4,128]{3,2,1,0:T(4,128)(2,1)} %reshape_squeeze.11, f32[4,4,16]{2,1,0:T(4,128)S(1)} %fusion.78, f32[4,4,16,512]{3,2,1,0:T(8,128)} %copy-done.7), kind=kOutput, calls=%fused_computation.45 | convolution fusion | flops 33981184 | bytes 2688000 | tf_op jit(solution)/shard_map/rkgt,rtkd->rkgd/dot_general | solution.py:57
  39.3 2.3 %fusion.41 = bf16[2,8,64,512]{3,2,0,1:T(8,128)(2,1)} fusion(bf16[2,4,8,64,512]{4,3,0,2,1:T(8,128)(2,1)} %bitcast.92, pred[8]{0:T(512)(128)(4,1)S(1)} %iota_compare_fusion.5), kind=kLoop, calls=%fused_computation.47 | loop fusion | flops 524288 | bytes 2097160 | tf_op jit(solution)/shard_map/jit(_where)/select_n | solution.py:94
  42.3 7.4 %collective-permute-start.24 = (bf16[2,8,64,512]{3,2,0,1:T(8,128)(2,1)}, bf16[2,8,64,512]{3,2,0,1:T(8,128)(2,1)S(1)}, u32[]{:S(2)}, u32[]{:S(2)}) collective-permute-start(bf16[2,8,64,512]{3,2,0,1:T(8,128)(2,1)} %fusion.41), channel_id=1, source_target_pairs={{0,128},{16,144},{32,160},{48,176},{64,192},{80,208},{96,224},{112... | collective-permute-start | bytes 3145736 | tf_op jit(solution)/shard_map/ppermute | solution.py:95
  49.7 1.3 pad_maximum_fusion.2
  52.2 1.1 collective-permute-start.16
  54.4 1.1 collective-permute-start.17
  56.5 1.1 collective-permute-start.8
  58.7 42.5 %collective-permute-done.16 = bf16[32,4096]{1,0:T(8,128)(2,1)S(1)} collective-permute-done((bf16[32,4096]{1,0:T(8,128)(2,1)S(1)}, bf16[32,4096]{1,0:T(8,128)(2,1)S(1)}, u32[]{:S(2)}, u32[]{:S(2)}) %collective-permute-start.16) | collective-permute-done | bytes 262176 | tf_op jit(solution)/shard_map/ppermute | solution.py:29
  101.2 2.1 pad_maximum_fusion.3
  103.4 6.9 %collective-permute-done.8 = bf16[64,4096]{1,0:T(8,128)(2,1)S(1)} collective-permute-done((bf16[64,4096]{1,0:T(8,128)(2,1)}, bf16[64,4096]{1,0:T(8,128)(2,1)S(1)}, u32[]{:S(2)}, u32[]{:S(2)}) %collective-permute-start.8) | collective-permute-done | bytes 524320 | tf_op jit(solution)/shard_map/ppermute | solution.py:29
  110.3 2.5 %collective-permute-done.9 = bf16[64,4096]{1,0:T(8,128)(2,1)S(1)} collective-permute-done((bf16[64,4096]{1,0:T(8,128)(2,1)}, bf16[64,4096]{1,0:T(8,128)(2,1)S(1)}, u32[]{:S(2)}, u32[]{:S(2)}) %collective-permute-start.9) | collective-permute-done | bytes 524320 | tf_op jit(solution)/shard_map/ppermute | solution.py:29
  112.8 2.8 %pad_maximum_fusion.1 = bf16[256,4096]{1,0:T(8,128)(2,1)} fusion(bf16[64,4096]{1,0:T(8,128)(2,1)S(1)} %collective-permute-done.9, bf16[64,4096]{1,0:T(8,128)(2,1)S(1)} %collective-permute-done.8, bf16[64,4096]{1,0:T(8,128)(2,1)} %collective-permute-done.7, bf16[64,4096]{1,0:T(8,128)(2,1)} %collective-permute-done.6), kind=kLoop, calls=%fused_computation.25 | loop fusion | flops 8388608 | bytes 4194304 | tf_op jit(solution)/shard_map/concatenate | solution.py:77
  116.8 1.9 copy-done.11
  119.7 3.1 %fusion.14 = f32[256,384]{1,0:T(8,128)} fusion(bf16[1,4096,384]{2,1,0:T(8,128)(2,1)S(1)} %copy-done.15, bf16[128,4096]{1,0:T(8,128)(2,1)S(1)} %collective-permute-done.2, bf16[32,4096]{1,0:T(8,128)(2,1)} %collective-permute-done.1, bf16[32,4096]{1,0:T(8,128)(2,1)} %collective-permute-done, bf16[64,4096]{1,0:T(8,128)(2,1)S(1)} %copy-done.6), kind=kOutput, calls=%fused_computation.22 | convolution fusion | flops 813694976 | bytes 5636096 | tf_op jit(solution)/shard_map/dot_general | solution.py:62
  122.8 6.4 %convolution_convert_fusion.3 = bf16[256,4096]{1,0:T(8,128)(2,1)} fusion(bf16[1,384,4096]{2,1,0:T(8,128)(2,1)S(1)} %copy-done, f32[256,384]{1,0:T(8,128)} %fusion.14, bf16[1,4096,384]{2,1,0:T(8,128)(2,1)} %param.16, bf16[128,4096]{1,0:T(8,128)(2,1)} %copy-done.16, bf16[32,4096]{1,0:T(8,128)(2,1)} %collective-permute-done.1, ...), kind=kOutput, calls=%fused_computation.6 | convolution fusion | flops 1620639744 | bytes 10878976 | tf_op jit(solution)/shard_map/dot_general | solution.py:65
  129.2 2.4 %slice.128 = bf16[128,4096]{1,0:T(8,128)(2,1)} slice(bf16[256,4096]{1,0:T(8,128)(2,1)} %convolution_convert_fusion.3), slice={[128:256], [0:4096]} | slice | bytes 2097152 | tf_op jit(solution)/shard_map/slice | solution.py:83
  132.1 1.3 constant_dynamic-update-slice_fusion.5
  133.4 1.3 copy-done.10
  134.7 3.9 %fusion.4 = f32[256,384]{1,0:T(8,128)} fusion(bf16[256,4096]{1,0:T(8,128)(2,1)S(1)} %constant_dynamic-update-slice_fusion.5, bf16[1,4096,384]{2,1,0:T(8,128)(2,1)} %param.16), kind=kOutput, calls=%fused_computation.12 | convolution fusion | flops 805306368 | bytes 5636096 | tf_op jit(solution)/shard_map/dot_general | solution.py:63
  138.7 6.4 %convolution_convert_fusion.2 = bf16[256,4096]{1,0:T(8,128)(2,1)} fusion(bf16[1,384,4096]{2,1,0:T(8,128)(2,1)S(1)} %copy-done, f32[256,384]{1,0:T(8,128)} %fusion.4, bf16[256,4096]{1,0:T(8,128)(2,1)} %copy-done.10, bf16[1,4096,384]{2,1,0:T(8,128)(2,1)} %param.15), kind=kOutput, calls=%fused_computation.5 | convolution fusion | flops 1612251136 | bytes 10878976 | tf_op jit(solution)/shard_map/dot_general | solution.py:65
  145.1 2.4 %slice.144 = bf16[128,4096]{1,0:T(8,128)(2,1)} slice(bf16[256,4096]{1,0:T(8,128)(2,1)} %convolution_convert_fusion.2), slice={[128:256], [0:4096]} | slice | bytes 2097152 | tf_op jit(solution)/shard_map/slice | solution.py:83
  147.5 2.5 %add_convert_fusion.3 = bf16[128,4096]{1,0:T(8,128)(2,1)} fusion(bf16[128,4096]{1,0:T(8,128)(2,1)} %collective-permute-done.3, bf16[256,4096]{1,0:T(8,128)(2,1)S(1)} %copy-done.5), kind=kLoop, calls=%fused_computation.39 | loop fusion | flops 2097152 | bytes 3145728 | tf_op jit(solution)/shard_map/convert_element_type | solution.py:69
  150.0 3.3 %constant_dynamic-update-slice_fusion = bf16[512,4096]{1,0:T(8,128)(2,1)} fusion(bf16[512,4096]{1,0:T(8,128)(2,1)} %copy-done.11, bf16[256,4096]{1,0:T(8,128)(2,1)} %collective-permute-done.10), kind=kLoop, calls=%fused_computation.66 | loop fusion | bytes 4194304 | tf_op jit(solution)/shard_map/concatenate | solution.py:78
  153.3 5.4 %fusion.6 = f32[512,384]{1,0:T(8,128)} fusion(bf16[512,4096]{1,0:T(8,128)(2,1)} %constant_dynamic-update-slice_fusion, bf16[1,4096,384]{2,1,0:T(8,128)(2,1)S(1)} %copy-done.14), kind=kOutput, calls=%fused_computation.14 | convolution fusion | flops 1610612736 | bytes 8126464 | tf_op jit(solution)/shard_map/dot_general | solution.py:63
  158.7 9.9 %convolution_convert_fusion = bf16[512,4096]{1,0:T(8,128)(2,1)} fusion(bf16[1,384,4096]{2,1,0:T(8,128)(2,1)S(1)} %copy-done, f32[512,384]{1,0:T(8,128)} %fusion.6, bf16[512,4096]{1,0:T(8,128)(2,1)} %constant_dynamic-update-slice_fusion, bf16[1,4096,384]{2,1,0:T(8,128)(2,1)} %param.15), kind=kOutput, calls=%fused_computation.3 | convolution fusion | flops 3224502272 | bytes 15466496 | tf_op jit(solution)/shard_map/dot_general | solution.py:65
  168.6 1.9 slice.135
  171.2 3.8 %collective-permute-start.5 = (bf16[32,4096]{1,0:T(8,128)(2,1)S(1)}, bf16[32,4096]{1,0:T(8,128)(2,1)S(1)}, u32[]{:S(2)}, u32[]{:S(2)}) collective-permute-start(bf16[32,4096]{1,0:T(8,128)(2,1)S(1)} %get-tuple-element.19), channel_id=1, source_target_pairs={{0,2},{1,3},{2,64},{3,65},{64,66},{65,67},{66,128},{67,129},{128,1... | collective-permute-start | bytes 786440 | tf_op jit(solution)/shard_map/ppermute | solution.py:29
  175.0 1.5 add_convert_fusion.1
  176.6 3.2 %collective-permute-start.21 = (bf16[32,4096]{1,0:T(8,128)(2,1)S(1)}, bf16[32,4096]{1,0:T(8,128)(2,1)S(1)}, u32[]{:S(2)}, u32[]{:S(2)}) collective-permute-start(bf16[32,4096]{1,0:T(8,128)(2,1)S(1)} %get-tuple-element.23), channel_id=1, source_target_pairs={{0,2},{1,3},{2,64},{3,65},{64,66},{65,67},{66,128},{67,129},{128,1... | collective-permute-start | bytes 786440 | tf_op jit(solution)/shard_map/ppermute | solution.py:29
  180.8 6.8 %collective-permute-done.20 = bf16[32,4096]{1,0:T(8,128)(2,1)S(1)} collective-permute-done((bf16[32,4096]{1,0:T(8,128)(2,1)S(1)}, bf16[32,4096]{1,0:T(8,128)(2,1)S(1)}, u32[]{:S(2)}, u32[]{:S(2)}) %collective-permute-start.20) | collective-permute-done | bytes 262176 | tf_op jit(solution)/shard_map/ppermute | solution.py:29
  187.6 3.3 %collective-permute-start.13 = (bf16[64,4096]{1,0:T(8,128)(2,1)S(1)}, bf16[64,4096]{1,0:T(8,128)(2,1)S(1)}, u32[]{:S(2)}, u32[]{:S(2)}) collective-permute-start(bf16[64,4096]{1,0:T(8,128)(2,1)S(1)} %get-tuple-element.17), channel_id=1, source_target_pairs={{0,2},{1,3},{2,64},{3,65},{64,66},{65,67},{66,128},{67,129},{128,1... | collective-permute-start | bytes 1572872 | tf_op jit(solution)/shard_map/ppermute | solution.py:29
  191.1 7.1 %collective-permute-done.12 = bf16[64,4096]{1,0:T(8,128)(2,1)S(1)} collective-permute-done((bf16[64,4096]{1,0:T(8,128)(2,1)S(1)}, bf16[64,4096]{1,0:T(8,128)(2,1)S(1)}, u32[]{:S(2)}, u32[]{:S(2)}) %collective-permute-start.12) | collective-permute-done | bytes 524320 | tf_op jit(solution)/shard_map/ppermute | solution.py:29
  198.2 2.2 %collective-permute-done.13 = bf16[64,4096]{1,0:T(8,128)(2,1)S(1)} collective-permute-done((bf16[64,4096]{1,0:T(8,128)(2,1)S(1)}, bf16[64,4096]{1,0:T(8,128)(2,1)S(1)}, u32[]{:S(2)}, u32[]{:S(2)}) %collective-permute-start.13) | collective-permute-done | bytes 524320 | tf_op jit(solution)/shard_map/ppermute | solution.py:29
  201.2 1.7 collective-permute-start.23
  203.1 4.4 %collective-permute-done.22 = bf16[64,4096]{1,0:T(8,128)(2,1)S(1)} collective-permute-done((bf16[64,4096]{1,0:T(8,128)(2,1)S(1)}, bf16[64,4096]{1,0:T(8,128)(2,1)S(1)}, u32[]{:S(2)}, u32[]{:S(2)}) %collective-permute-start.22) | collective-permute-done | bytes 524320 | tf_op jit(solution)/shard_map/ppermute | solution.py:29
  207.5 5.8 %collective-permute-done.14 = bf16[64,4096]{1,0:T(8,128)(2,1)S(1)} collective-permute-done((bf16[64,4096]{1,0:T(8,128)(2,1)S(1)}, bf16[64,4096]{1,0:T(8,128)(2,1)S(1)}, u32[]{:S(2)}, u32[]{:S(2)}) %collective-permute-start.14) | collective-permute-done | bytes 524320 | tf_op jit(solution)/shard_map/ppermute | solution.py:29
  213.2 3.0 %collective-permute-done.23 = bf16[64,4096]{1,0:T(8,128)(2,1)S(1)} collective-permute-done((bf16[64,4096]{1,0:T(8,128)(2,1)S(1)}, bf16[64,4096]{1,0:T(8,128)(2,1)S(1)}, u32[]{:S(2)}, u32[]{:S(2)}) %collective-permute-start.23) | collective-permute-done | bytes 524320 | tf_op jit(solution)/shard_map/ppermute | solution.py:29
  216.3 1.5 convolution_convert_fusion.4
  (101 shorter events, 16.4 us)
Async XLA Ops:
  0.6 122.2 %copy-start = (bf16[1,384,4096]{2,1,0:T(8,128)(2,1)S(1)}, bf16[1,384,4096]{2,1,0:T(8,128)(2,1)}, u32[]{:S(2)}) copy-start(bf16[1,384,4096]{2,1,0:T(8,128)(2,1)} %param.17) | copy-start | bytes 9437188
  5.3 37.1 %collective-permute-start = (bf16[32,4096]{1,0:T(8,128)(2,1)}, bf16[32,4096]{1,0:T(8,128)(2,1)}, u32[]{:S(2)}, u32[]{:S(2)}) collective-permute-start(bf16[32,4096]{1,0:T(8,128)(2,1)} %get-tuple-element.14), channel_id=1, source_target_pairs={{0,2},{1,3},{2,64},{3,65},{64,66},{65,67},{66,128},{67,129},{128,1... | collective-permute-start | bytes 786440 | tf_op jit(solution)/shard_map/ppermute | solution.py:29
  7.2 7.7 %copy-start.13 = (s32[1,1,4]{2,1,0:T(1,128)S(1)}, s32[1,1,4]{2,1,0:T(1,128)}, u32[]{:S(2)}) copy-start(s32[1,1,4]{2,1,0:T(1,128)} %param.11) | copy-start | bytes 52
  7.2 8.1 %copy-start.1 = (s32[1,1,16]{2,1,0:T(1,128)S(1)}, s32[1,1,16]{2,1,0:T(1,128)}, u32[]{:S(2)}) copy-start(s32[1,1,16]{2,1,0:T(1,128)} %param.12) | copy-start | bytes 196
  7.2 42.5 %collective-permute-start.1 = (bf16[32,4096]{1,0:T(8,128)(2,1)S(1)}, bf16[32,4096]{1,0:T(8,128)(2,1)}, u32[]{:S(2)}, u32[]{:S(2)}) collective-permute-start(bf16[32,4096]{1,0:T(8,128)(2,1)S(1)} %get-tuple-element.15), channel_id=1, source_target_pairs={{0,194},{1,195},{2,0},{3,1},{64,2},{65,3},{66,64},{67,65},{128,66}... | collective-permute-start | bytes 786440 | tf_op jit(solution)/shard_map/ppermute | solution.py:29
  8.6 42.5 %collective-permute-start.15 = (bf16[64,4096]{1,0:T(8,128)(2,1)}, bf16[64,4096]{1,0:T(8,128)(2,1)}, u32[]{:S(2)}, u32[]{:S(2)}) collective-permute-start(bf16[64,4096]{1,0:T(8,128)(2,1)} %get-tuple-element.11), channel_id=1, source_target_pairs={{0,8},{1,9},{2,10},{3,11},{64,72},{65,73},{66,74},{67,75},{128,136... | collective-permute-start | bytes 1572872 | tf_op jit(solution)/shard_map/ppermute | solution.py:29
  11.6 42.7 %collective-permute-start.6 = (bf16[64,4096]{1,0:T(8,128)(2,1)}, bf16[64,4096]{1,0:T(8,128)(2,1)}, u32[]{:S(2)}, u32[]{:S(2)}) collective-permute-start(bf16[64,4096]{1,0:T(8,128)(2,1)} %get-tuple-element.13), channel_id=1, source_target_pairs={{0,4},{1,5},{2,6},{3,7},{64,68},{65,69},{66,70},{67,71},{128,132},... | collective-permute-start | bytes 1572872 | tf_op jit(solution)/shard_map/ppermute | solution.py:29
  12.2 44.3 %collective-permute-start.7 = (bf16[64,4096]{1,0:T(8,128)(2,1)}, bf16[64,4096]{1,0:T(8,128)(2,1)}, u32[]{:S(2)}, u32[]{:S(2)}) collective-permute-start(bf16[64,4096]{1,0:T(8,128)(2,1)} %get-tuple-element.12), channel_id=1, source_target_pairs={{0,12},{1,13},{2,14},{3,15},{64,76},{65,77},{66,78},{67,79},{128,1... | collective-permute-start | bytes 1572872 | tf_op jit(solution)/shard_map/ppermute | solution.py:29
  25.3 4.1 %copy-start.12 = (bf16[1,1,4,8192]{3,2,1,0:T(4,128)(2,1)S(1)}, bf16[1,1,4,8192]{3,2,1,0:T(4,128)(2,1)}, u32[]{:S(2)}) copy-start(bf16[1,1,4,8192]{3,2,1,0:T(4,128)(2,1)} %param.9) | copy-start | bytes 196612
  31.7 0.8 copy-start.7
  42.3 73.3 %collective-permute-start.24 = (bf16[2,8,64,512]{3,2,0,1:T(8,128)(2,1)}, bf16[2,8,64,512]{3,2,0,1:T(8,128)(2,1)S(1)}, u32[]{:S(2)}, u32[]{:S(2)}) collective-permute-start(bf16[2,8,64,512]{3,2,0,1:T(8,128)(2,1)} %fusion.41), channel_id=1, source_target_pairs={{0,128},{16,144},{32,160},{48,176},{64,192},{80,208},{96,224},{112... | collective-permute-start | bytes 3145736 | tf_op jit(solution)/shard_map/ppermute | solution.py:95
  51.0 65.8 %collective-permute-start.2 = (bf16[128,4096]{1,0:T(8,128)(2,1)S(1)}, bf16[128,4096]{1,0:T(8,128)(2,1)S(1)}, u32[]{:S(2)}, u32[]{:S(2)}) collective-permute-start(bf16[128,4096]{1,0:T(8,128)(2,1)S(1)} %pad_maximum_fusion.2), channel_id=1, source_target_pairs={{0,1},{1,0},{2,3},{3,2},{64,65},{65,64},{66,67},{67,66},{128,129},... | collective-permute-start | bytes 3145736 | tf_op jit(solution)/shard_map/ppermute | solution.py:29
  52.2 49.0 %collective-permute-start.16 = (bf16[32,4096]{1,0:T(8,128)(2,1)S(1)}, bf16[32,4096]{1,0:T(8,128)(2,1)S(1)}, u32[]{:S(2)}, u32[]{:S(2)}) collective-permute-start(bf16[32,4096]{1,0:T(8,128)(2,1)S(1)} %get-tuple-element.25), channel_id=1, source_target_pairs={{0,2},{1,3},{2,64},{3,65},{64,66},{65,67},{66,128},{67,129},{128,1... | collective-permute-start | bytes 786440 | tf_op jit(solution)/shard_map/ppermute | solution.py:29
  54.4 46.9 %collective-permute-start.17 = (bf16[32,4096]{1,0:T(8,128)(2,1)S(1)}, bf16[32,4096]{1,0:T(8,128)(2,1)S(1)}, u32[]{:S(2)}, u32[]{:S(2)}) collective-permute-start(bf16[32,4096]{1,0:T(8,128)(2,1)S(1)} %get-tuple-element.24), channel_id=1, source_target_pairs={{0,194},{1,195},{2,0},{3,1},{64,2},{65,3},{66,64},{67,65},{128,66}... | collective-permute-start | bytes 786440 | tf_op jit(solution)/shard_map/ppermute | solution.py:29
  56.5 53.8 %collective-permute-start.8 = (bf16[64,4096]{1,0:T(8,128)(2,1)}, bf16[64,4096]{1,0:T(8,128)(2,1)S(1)}, u32[]{:S(2)}, u32[]{:S(2)}) collective-permute-start(bf16[64,4096]{1,0:T(8,128)(2,1)} %collective-permute-done.6), channel_id=1, source_target_pairs={{0,2},{1,3},{2,64},{3,65},{64,66},{65,67},{66,128},{67,129},{128,1... | collective-permute-start | bytes 1572872 | tf_op jit(solution)/shard_map/ppermute | solution.py:29
  101.2 11.6 %collective-permute-start.9 = (bf16[64,4096]{1,0:T(8,128)(2,1)}, bf16[64,4096]{1,0:T(8,128)(2,1)S(1)}, u32[]{:S(2)}, u32[]{:S(2)}) collective-permute-start(bf16[64,4096]{1,0:T(8,128)(2,1)} %collective-permute-done.7), channel_id=1, source_target_pairs={{0,194},{1,195},{2,0},{3,1},{64,2},{65,3},{66,64},{67,65},{128,66}... | collective-permute-start | bytes 1572872 | tf_op jit(solution)/shard_map/ppermute | solution.py:29
  103.3 28.8 %collective-permute-start.18 = (bf16[128,4096]{1,0:T(8,128)(2,1)}, bf16[128,4096]{1,0:T(8,128)(2,1)}, u32[]{:S(2)}, u32[]{:S(2)}) collective-permute-start(bf16[128,4096]{1,0:T(8,128)(2,1)} %pad_maximum_fusion.3), channel_id=1, source_target_pairs={{0,1},{1,0},{2,3},{3,2},{64,65},{65,64},{66,67},{67,66},{128,129},... | collective-permute-start | bytes 3145736 | tf_op jit(solution)/shard_map/ppermute | solution.py:29
  103.4 6.9 %copy-start.8 = (bf16[256,4096]{1,0:T(8,128)(2,1)}, bf16[256,4096]{1,0:T(8,128)(2,1)S(1)}, u32[]{:S(2)}) copy-start(bf16[256,4096]{1,0:T(8,128)(2,1)S(1)} %constant_dynamic-update-slice_fusion.6) | copy-start | bytes 6291460
  115.6 34.4 %collective-permute-start.10 = (bf16[256,4096]{1,0:T(8,128)(2,1)}, bf16[256,4096]{1,0:T(8,128)(2,1)}, u32[]{:S(2)}, u32[]{:S(2)}) collective-permute-start(bf16[256,4096]{1,0:T(8,128)(2,1)} %pad_maximum_fusion.1), channel_id=1, source_target_pairs={{0,1},{1,0},{2,3},{3,2},{64,65},{65,64},{66,67},{67,66},{128,129},... | collective-permute-start | bytes 6291464 | tf_op jit(solution)/shard_map/ppermute | solution.py:29
  115.6 4.1 %copy-start.6 = (bf16[64,4096]{1,0:T(8,128)(2,1)S(1)}, bf16[64,4096]{1,0:T(8,128)(2,1)}, u32[]{:S(2)}) copy-start(bf16[64,4096]{1,0:T(8,128)(2,1)} %get-tuple-element.10) | copy-start | bytes 1572868
  115.6 4.1 %copy-start.15 = (bf16[1,4096,384]{2,1,0:T(8,128)(2,1)S(1)}, bf16[1,4096,384]{2,1,0:T(8,128)(2,1)}, u32[]{:S(2)}) copy-start(bf16[1,4096,384]{2,1,0:T(8,128)(2,1)} %param.15) | copy-start | bytes 9437188
  116.8 2.0 copy-start.11
  118.7 1.0 copy-start.16
  129.2 2.9 %copy-start.9 = (bf16[256,4096]{1,0:T(8,128)(2,1)S(1)}, bf16[256,4096]{1,0:T(8,128)(2,1)}, u32[]{:S(2)}) copy-start(bf16[256,4096]{1,0:T(8,128)(2,1)} %copy-done.8) | copy-start | bytes 6291460
  131.6 15.9 %collective-permute-start.3 = (bf16[128,4096]{1,0:T(8,128)(2,1)}, bf16[128,4096]{1,0:T(8,128)(2,1)}, u32[]{:S(2)}, u32[]{:S(2)}) collective-permute-start(bf16[128,4096]{1,0:T(8,128)(2,1)} %slice.128), channel_id=1, source_target_pairs={{0,1},{1,0},{2,3},{3,2},{64,65},{65,64},{66,67},{67,66},{128,129},... | collective-permute-start | bytes 3145736 | tf_op jit(solution)/shard_map/ppermute | solution.py:29
  133.4 1.3 copy-start.10
  145.1 2.5 %copy-start.5 = (bf16[256,4096]{1,0:T(8,128)(2,1)S(1)}, bf16[256,4096]{1,0:T(8,128)(2,1)}, u32[]{:S(2)}) copy-start(bf16[256,4096]{1,0:T(8,128)(2,1)} %convolution_convert_fusion.3) | copy-start | bytes 6291460
  147.5 27.5 %collective-permute-start.19 = (bf16[128,4096]{1,0:T(8,128)(2,1)}, bf16[128,4096]{1,0:T(8,128)(2,1)}, u32[]{:S(2)}, u32[]{:S(2)}) collective-permute-start(bf16[128,4096]{1,0:T(8,128)(2,1)} %slice.144), channel_id=1, source_target_pairs={{0,1},{1,0},{2,3},{3,2},{64,65},{65,64},{66,67},{67,66},{128,129},... | collective-permute-start | bytes 3145736 | tf_op jit(solution)/shard_map/ppermute | solution.py:29
  150.0 3.3 %copy-start.14 = (bf16[1,4096,384]{2,1,0:T(8,128)(2,1)S(1)}, bf16[1,4096,384]{2,1,0:T(8,128)(2,1)}, u32[]{:S(2)}) copy-start(bf16[1,4096,384]{2,1,0:T(8,128)(2,1)} %param.16) | copy-start | bytes 9437188
  168.6 2.5 %copy-start.2 = (bf16[128,4096]{1,0:T(8,128)(2,1)S(1)}, bf16[128,4096]{1,0:T(8,128)(2,1)}, u32[]{:S(2)}) copy-start(bf16[128,4096]{1,0:T(8,128)(2,1)} %add_convert_fusion.3) | copy-start | bytes 3145732
  168.6 6.4 %copy-start.4 = (bf16[256,4096]{1,0:T(8,128)(2,1)S(1)}, bf16[256,4096]{1,0:T(8,128)(2,1)}, u32[]{:S(2)}) copy-start(bf16[256,4096]{1,0:T(8,128)(2,1)} %convolution_convert_fusion.2) | copy-start | bytes 6291460
  170.5 9.3 %collective-permute-start.11 = (bf16[256,4096]{1,0:T(8,128)(2,1)S(1)}, bf16[256,4096]{1,0:T(8,128)(2,1)S(1)}, u32[]{:S(2)}, u32[]{:S(2)}) collective-permute-start(bf16[256,4096]{1,0:T(8,128)(2,1)S(1)} %slice.135), channel_id=1, source_target_pairs={{0,1},{1,0},{2,3},{3,2},{64,65},{65,64},{66,67},{67,66},{128,129},... | collective-permute-start | bytes 6291464 | tf_op jit(solution)/shard_map/ppermute | solution.py:29
  171.1 31.8 %collective-permute-start.4 = (bf16[32,4096]{1,0:T(8,128)(2,1)S(1)}, bf16[32,4096]{1,0:T(8,128)(2,1)S(1)}, u32[]{:S(2)}, u32[]{:S(2)}) collective-permute-start(bf16[32,4096]{1,0:T(8,128)(2,1)S(1)} %get-tuple-element.18), channel_id=1, source_target_pairs={{0,194},{1,195},{2,0},{3,1},{64,2},{65,3},{66,64},{67,65},{128,66}... | collective-permute-start | bytes 786440 | tf_op jit(solution)/shard_map/ppermute | solution.py:29
  171.2 8.6 %copy-start.3 = (bf16[512,4096]{1,0:T(8,128)(2,1)S(1)}, bf16[512,4096]{1,0:T(8,128)(2,1)}, u32[]{:S(2)}) copy-start(bf16[512,4096]{1,0:T(8,128)(2,1)} %convolution_convert_fusion) | copy-start | bytes 12582916
  171.2 31.7 %collective-permute-start.5 = (bf16[32,4096]{1,0:T(8,128)(2,1)S(1)}, bf16[32,4096]{1,0:T(8,128)(2,1)S(1)}, u32[]{:S(2)}, u32[]{:S(2)}) collective-permute-start(bf16[32,4096]{1,0:T(8,128)(2,1)S(1)} %get-tuple-element.19), channel_id=1, source_target_pairs={{0,2},{1,3},{2,64},{3,65},{64,66},{65,67},{66,128},{67,129},{128,1... | collective-permute-start | bytes 786440 | tf_op jit(solution)/shard_map/ppermute | solution.py:29
  176.5 11.1 %collective-permute-start.20 = (bf16[32,4096]{1,0:T(8,128)(2,1)S(1)}, bf16[32,4096]{1,0:T(8,128)(2,1)S(1)}, u32[]{:S(2)}, u32[]{:S(2)}) collective-permute-start(bf16[32,4096]{1,0:T(8,128)(2,1)S(1)} %get-tuple-element.22), channel_id=1, source_target_pairs={{0,194},{1,195},{2,0},{3,1},{64,2},{65,3},{66,64},{67,65},{128,66}... | collective-permute-start | bytes 786440 | tf_op jit(solution)/shard_map/ppermute | solution.py:29
  176.6 14.3 %collective-permute-start.21 = (bf16[32,4096]{1,0:T(8,128)(2,1)S(1)}, bf16[32,4096]{1,0:T(8,128)(2,1)S(1)}, u32[]{:S(2)}, u32[]{:S(2)}) collective-permute-start(bf16[32,4096]{1,0:T(8,128)(2,1)S(1)} %get-tuple-element.23), channel_id=1, source_target_pairs={{0,2},{1,3},{2,64},{3,65},{64,66},{65,67},{66,128},{67,129},{128,1... | collective-permute-start | bytes 786440 | tf_op jit(solution)/shard_map/ppermute | solution.py:29
  180.7 17.5 %collective-permute-start.12 = (bf16[64,4096]{1,0:T(8,128)(2,1)S(1)}, bf16[64,4096]{1,0:T(8,128)(2,1)S(1)}, u32[]{:S(2)}, u32[]{:S(2)}) collective-permute-start(bf16[64,4096]{1,0:T(8,128)(2,1)S(1)} %get-tuple-element.16), channel_id=1, source_target_pairs={{0,194},{1,195},{2,0},{3,1},{64,2},{65,3},{66,64},{67,65},{128,66}... | collective-permute-start | bytes 1572872 | tf_op jit(solution)/shard_map/ppermute | solution.py:29
  187.6 12.9 %collective-permute-start.13 = (bf16[64,4096]{1,0:T(8,128)(2,1)S(1)}, bf16[64,4096]{1,0:T(8,128)(2,1)S(1)}, u32[]{:S(2)}, u32[]{:S(2)}) collective-permute-start(bf16[64,4096]{1,0:T(8,128)(2,1)S(1)} %get-tuple-element.17), channel_id=1, source_target_pairs={{0,2},{1,3},{2,64},{3,65},{64,66},{65,67},{66,128},{67,129},{128,1... | collective-permute-start | bytes 1572872 | tf_op jit(solution)/shard_map/ppermute | solution.py:29
  191.0 16.5 %collective-permute-start.22 = (bf16[64,4096]{1,0:T(8,128)(2,1)S(1)}, bf16[64,4096]{1,0:T(8,128)(2,1)S(1)}, u32[]{:S(2)}, u32[]{:S(2)}) collective-permute-start(bf16[64,4096]{1,0:T(8,128)(2,1)S(1)} %add_convert_fusion.4), channel_id=1, source_target_pairs={{0,8},{1,9},{2,10},{3,11},{64,72},{65,73},{66,74},{67,75},{128,136... | collective-permute-start | bytes 1572872 | tf_op jit(solution)/shard_map/ppermute | solution.py:29
  200.8 12.4 %collective-permute-start.14 = (bf16[64,4096]{1,0:T(8,128)(2,1)S(1)}, bf16[64,4096]{1,0:T(8,128)(2,1)S(1)}, u32[]{:S(2)}, u32[]{:S(2)}) collective-permute-start(bf16[64,4096]{1,0:T(8,128)(2,1)S(1)} %get-tuple-element.20), channel_id=1, source_target_pairs={{0,12},{1,13},{2,14},{3,15},{64,76},{65,77},{66,78},{67,79},{128,1... | collective-permute-start | bytes 1572872 | tf_op jit(solution)/shard_map/ppermute | solution.py:29
  201.2 15.1 %collective-permute-start.23 = (bf16[64,4096]{1,0:T(8,128)(2,1)S(1)}, bf16[64,4096]{1,0:T(8,128)(2,1)S(1)}, u32[]{:S(2)}, u32[]{:S(2)}) collective-permute-start(bf16[64,4096]{1,0:T(8,128)(2,1)S(1)} %get-tuple-element.21), channel_id=1, source_target_pairs={{0,4},{1,5},{2,6},{3,7},{64,68},{65,69},{66,70},{67,71},{128,132},... | collective-permute-start | bytes 1572872 | tf_op jit(solution)/shard_map/ppermute | solution.py:29

commit v2 on v1

v2 whole, which is shorter than its diff:
```python
import functools

import jax
import jax.numpy as jnp
from jax import lax
from jax.experimental import pallas as pl
from jax.experimental.pallas import tpu as pltpu
from jax.sharding import PartitionSpec as P

HEADS = 64
KV_HEADS = 4
HEAD_DIM = 128
GROUP = HEADS // KV_HEADS
PAGE = 64
MAXP = 8
PAGES = 16
REQS = 4
CAP = 64
TOK = 128
D = 4096
FQ = 384
NX, NY, NZ, NC = 4, 4, 8, 2
K_STEPS, N_STEPS = 4, 4
MIB = 1 << 20
VMEM = pltpu.VMEM
SMEM = pltpu.SMEM


def device_id(x, y, z, c):
    x, y, z = x % NX, y % NY, z % NZ
    return ((z // 2) * NY + y) * 16 + x * 4 + (z % 2) * 2 + c


def move(block, to):
    route = [
        (device_id(x, y, z, c), device_id(*to(x, y, z, c)))
        for x in range(NX)
        for y in range(NY)
        for z in range(NZ)
        for c in range(NC)
    ]
    return lax.ppermute(block, ("inst", "ep"), route)


def over_x(block, dx):
    return move(block, lambda x, y, z, c: (x + dx, y, z, c))


def over_z(block):
    return move(block, lambda x, y, z, c: (x, y, z + 1 - 2 * c, c))


def back_over_z(block):
    return move(block, lambda x, y, z, c: (x, y, z - 1 + 2 * c, c))


def other_core(block):
    return move(block, lambda x, y, z, c: (x, y, z, 1 - c))


def pack_kernel(routes, hidden, onehot, *pieces):
    x = lax.axis_index("ep") // 4
    rel = jnp.bitwise_and(routes[...] - x, NX - 1)
    match = (rel == lax.broadcasted_iota(jnp.int32, (8, TOK), 0)).astype(jnp.float32)
    earlier = lax.broadcasted_iota(jnp.int32, (TOK, TOK), 0) < lax.broadcasted_iota(
        jnp.int32, (TOK, TOK), 1
    )
    rank = jnp.dot(
        match.astype(jnp.bfloat16),
        earlier.astype(jnp.float32).astype(jnp.bfloat16),
        preferred_element_type=jnp.float32,
    )
    slot = jnp.sum(rank * match, axis=0, keepdims=True).astype(jnp.int32)
    target = rel * CAP + slot
    chosen = (lax.broadcasted_iota(jnp.int32, (NX * CAP, TOK), 0) == target).astype(jnp.float32)
    onehot[...] = chosen.astype(jnp.bfloat16)
    for d in (2, 1, 3, 0):
        pieces[d][...] = jnp.dot(
            onehot[d * CAP : (d + 1) * CAP, :], hidden[...], preferred_element_type=jnp.float32
        ).astype(jnp.bfloat16)


def pack(routes, hidden):
    return pl.pallas_call(
        pack_kernel,
        out_shape=[jax.ShapeDtypeStruct((NX * CAP, TOK), jnp.bfloat16)]
        + [jax.ShapeDtypeStruct((CAP, D), jnp.bfloat16)] * NX,
        in_specs=[pl.BlockSpec(memory_space=VMEM)] * 2,
        out_specs=[pl.BlockSpec(memory_space=VMEM)] * (1 + NX),
        compiler_params=pltpu.CompilerParams(vmem_limit_bytes=12 * MIB),
        cost_estimate=pl.CostEstimate(
            flops=2 * NX * CAP * TOK * D, bytes_accessed=3 * MIB, transcendentals=0
        ),
        name="pack",
    )(routes.reshape(1, TOK), hidden)


def leave_kernel(ctx, order, kv, out):
    pages = (ctx[0] + (PAGE - 1)) // PAGE
    for j in range(MAXP):
        page = kv[:, order[j]]
        out[:, j] = jnp.where(j < pages, page, jnp.zeros_like(page))


def leave(ctx, order, kv):
    return pl.pallas_call(
        leave_kernel,
        out_shape=jax.ShapeDtypeStruct((2, MAXP, PAGE, KV_HEADS * HEAD_DIM), jnp.bfloat16),
        in_specs=[pl.BlockSpec(memory_space=SMEM)] * 2 + [pl.BlockSpec(memory_space=VMEM)],
        out_specs=pl.BlockSpec(memory_space=VMEM),
        compiler_params=pltpu.CompilerParams(vmem_limit_bytes=8 * MIB),
        cost_estimate=pl.CostEstimate(flops=0, bytes_accessed=3 * MIB, transcendentals=0),
        name="leave",
    )(ctx, order, kv)


def attend_kernel(ctx, order, queries, kv, out):
    start = 0
    for r in range(REQS):
        length = ctx[r]
        page_of = [order[jnp.minimum(start + j, PAGES - 1)] for j in range(MAXP)]
        start = start + (length + (PAGE - 1)) // PAGE
        inside = lax.broadcasted_iota(jnp.int32, (GROUP, MAXP * PAGE), 1) < length
        for g in range(KV_HEADS):
            cols = slice(g * HEAD_DIM, (g + 1) * HEAD_DIM)
            keys = jnp.concatenate([kv[0, p, :, cols] for p in page_of], 0)
            values = jnp.concatenate([kv[1, p, :, cols] for p in page_of], 0)
            scores = lax.dot_general(
                queries[r, g * GROUP : (g + 1) * GROUP, :],
                keys,
                (((1,), (1,)), ((), ())),
                preferred_element_type=jnp.float32,
            ) * HEAD_DIM ** (-0.5)
            scores = jnp.where(inside, scores, -1e30)
            expo = jnp.exp(scores - jnp.max(scores, axis=-1, keepdims=True))
            probs = (expo / jnp.sum(expo, axis=-1, keepdims=True)).astype(jnp.bfloat16)
            out[r, g * GROUP : (g + 1) * GROUP, :] = jnp.dot(
                probs, values, preferred_element_type=jnp.float32
            ).astype(jnp.bfloat16)


def attend(ctx, order, queries, kv):
    out = pl.pallas_call(
        attend_kernel,
        out_shape=jax.ShapeDtypeStruct((REQS, HEADS, HEAD_DIM), jnp.bfloat16),
        in_specs=[pl.BlockSpec(memory_space=SMEM)] * 2 + [pl.BlockSpec(memory_space=VMEM)] * 2,
        out_specs=pl.BlockSpec(memory_space=VMEM),
        compiler_params=pltpu.CompilerParams(vmem_limit_bytes=10 * MIB),
        cost_estimate=pl.CostEstimate(
            flops=4 * REQS * HEADS * MAXP * PAGE * HEAD_DIM,
            bytes_accessed=2 * MIB,
            transcendentals=REQS * HEADS * MAXP * PAGE,
        ),
        name="attend",
    )(ctx, order, queries.reshape(REQS, HEADS, HEAD_DIM), kv)
    return out.reshape(REQS, HEADS * HEAD_DIM)


def expert_kernel(count, *refs):
    rows, refs = refs[:count], refs[count:]
    gates, ups, downs, refs = refs[:2], refs[2:4], refs[4:6], refs[6:]
    outs, (gate, upper, hidden) = refs[:count], refs[count:]
    step = pl.program_id(0)

    @pl.when(step < K_STEPS)
    def _():
        block = jnp.concatenate([r[...] for r in rows], 0)
        new_gate = jnp.dot(
            block,
            jnp.concatenate([w[...] for w in gates], 1),
            preferred_element_type=jnp.float32,
        )
        new_upper = jnp.dot(
            block,
            jnp.concatenate([w[...] for w in ups], 1),
            preferred_element_type=jnp.float32,
        )

        @pl.when(step == 0)
        def _():
            gate[...] = new_gate
            upper[...] = new_upper

        @pl.when(step > 0)
        def _():
            gate[...] += new_gate
            upper[...] += new_upper

    @pl.when(step == K_STEPS - 1)
    def _():
        v = gate[...]
        hidden[...] = (v / (1.0 + jnp.exp(-v)) * upper[...]).astype(jnp.bfloat16)

    @pl.when(step >= K_STEPS)
    def _():
        part = jnp.dot(
            hidden[...],
            jnp.concatenate([w[...] for w in downs], 0),
            preferred_element_type=jnp.float32,
        ).astype(jnp.bfloat16)
        for i, out in enumerate(outs):
            out[...] = part[i * CAP : (i + 1) * CAP]


def experts(rows, gates, ups, downs):
    count = len(rows)
    size = count * CAP
    kb, nb = D // K_STEPS, D // N_STEPS

    def early(i):
        return jnp.minimum(i, K_STEPS - 1)

    def late(i):
        return jnp.maximum(i - K_STEPS, 0)

    return pl.pallas_call(
        functools.partial(expert_kernel, count),
        out_shape=[jax.ShapeDtypeStruct((CAP, D), jnp.bfloat16)] * count,
        grid=(K_STEPS + N_STEPS,),
        in_specs=[pl.BlockSpec((CAP, kb), lambda i: (0, early(i)))] * count
        + [pl.BlockSpec((kb, FQ), lambda i: (early(i), 0))] * 4
        + [pl.BlockSpec((FQ, nb), lambda i: (0, late(i)))] * 2,
        out_specs=[pl.BlockSpec((CAP, nb), lambda i: (0, late(i)))] * count,
        scratch_shapes=[
            pltpu.VMEM((size, 2 * FQ), jnp.float32),
            pltpu.VMEM((size, 2 * FQ), jnp.float32),
            pltpu.VMEM((size, 2 * FQ), jnp.bfloat16),
        ],
        compiler_params=pltpu.CompilerParams(vmem_limit_bytes=24 * MIB),
        cost_estimate=pl.CostEstimate(
            flops=12 * size * D * FQ, bytes_accessed=18 * MIB, transcendentals=0
        ),
        name="experts",
    )(*rows, *gates, *ups, *downs)


def home_kernel(onehot, *refs):
    *pieces, out = refs
    out[...] = lax.dot_general(
        onehot[...],
        jnp.concatenate([p[...] for p in pieces], 0),
        (((0,), (0,)), ((), ())),
        preferred_element_type=jnp.float32,
    ).astype(jnp.bfloat16)


def bring_home(onehot, pieces):
    nb = D // 4
    return pl.pallas_call(
        home_kernel,
        out_shape=jax.ShapeDtypeStruct((TOK, D), jnp.bfloat16),
        grid=(4,),
        in_specs=[pl.BlockSpec((NX * CAP, TOK), lambda i: (0, 0))]
        + [pl.BlockSpec((CAP, nb), lambda i: (0, i))] * NX,
        out_specs=pl.BlockSpec((TOK, nb), lambda i: (0, i)),
        compiler_params=pltpu.CompilerParams(vmem_limit_bytes=12 * MIB),
        cost_estimate=pl.CostEstimate(
            flops=2 * NX * CAP * TOK * D, bytes_accessed=3 * MIB, transcendentals=0
        ),
        name="bring_home",
    )(onehot, *pieces)


def add(a, b):
    return (a.astype(jnp.float32) + b.astype(jnp.float32)).astype(jnp.bfloat16)


def local(queries, kv_cache, ctx_len, page_order, hidden_in, routes, w_gate, w_up, w_down):
    ctx, order, kv = ctx_len[0, 0], page_order[0, 0], kv_cache[0, 0]
    onehot, *piece = pack(routes, hidden_in)
    got = [piece[0]] + [over_x(piece[d], d) for d in (1, 2, 3)]
    arrived = lax.ppermute(leave(ctx, order, kv), "inst", [(i, i + 8) for i in range(8)])
    gates, ups, downs = ((w[0], other_core(w[0])) for w in (w_gate, w_up, w_down))
    attn_out = attend(ctx, order, queries[0, 0], kv)
    across = [over_z(g) for g in got]
    home = [None] * NX
    for group in ((0, 1, 3), (2,)):
        rows = [got[d] for d in group] + [across[d] for d in group]
        part = experts(rows, gates, ups, downs)
        for i, d in enumerate(group):
            whole = add(part[i], back_over_z(part[len(group) + i]))
            home[d] = over_x(whole, -d) if d else whole
    moe_out = bring_home(onehot, home)
    return attn_out[None, None], moe_out, arrived[None, None]


def solution(mesh):
    placed = (
        P("inst", "ep", None, None),
        P("inst", "ep", None, None, None, None),
        P("inst", "ep", None),
        P("inst", "ep", None),
        P(("inst", "ep"), None),
        P(("inst", "ep"), None),
        P("ep", None, None),
        P("ep", None, None),
        P("ep", None, None),
    )
    return jax.shard_map(
        local,
        mesh=mesh,
        in_specs=placed,
        out_specs=(
            P("inst", "ep", None, None),
            P(("inst", "ep"), None),
            P("inst", "ep", None, None, None, None),
        ),
        check_vma=False,
    )
```

time: 219 us -> 153 us (0.70)
  the two profiles are of different devices: /device:TPU:80 before, /device:TPU:1 now
where the time goes in v2:
time: 153 us; the launch traced here: 152 us
  waiting for transfers between devices  49.7 us (32%)
  starting transfers between devices  43.8 us (29%)
  Pallas kernels  29.1 us (19%)
  local copies, waits for them, and re-layouts  27.3 us (18%)
  other arithmetic  1.57 us (1%)
    ppermute x17, waiting for transfers between devices, move(): return lax.ppermute(block, ('inst', 'ep'), route)  49.7 us
    ppermute x17, starting transfers between devices, move(): return lax.ppermute(block, ('inst', 'ep'), route)  41.4 us
    unnamed x58, local copies, waits for them, and re-layouts  26.6 us
    pallas_call x2, Pallas kernels, experts(): pl.pallas_call(functools.partial(expert_kernel, count), out_shape=[jax.Sh...  18.5 us
    pallas_call x1, Pallas kernels, attend(): pl.pallas_call(attend_kernel, out_shape=jax.ShapeDtypeStruct((REQS, HEADS...  5.81 us
  transfers between devices with their start and end apart: 18, of which 7 were waited for; matrix products, arithmetic and copies ran while one was open for 1% of the time, Pallas kernels for 18%

profile of v2, /device:TPU:1, one launch (start us, length us, event | category | flops | bytes accessed | tf_op | source)
XLA Modules:
  0.0 152.2 jit_solution(17031253932576952083)
XLA Ops:
  0.6 3.3 %collective-permute-start.5 = (bf16[4096,384]{1,0:T(8,128)(2,1)}, bf16[4096,384]{1,0:T(8,128)(2,1)S(1)}, u32[]{:S(2)}, u32[]{:S(2)}) collective-permute-start(bf16[4096,384]{1,0:T(8,128)(2,1)} %bitcast.15), channel_id=1, source_target_pairs={{0,1},{1,0},{2,3},{3,2},{64,65},{65,64},{66,67},{67,66},{128,129},... | collective-permute-start | bytes 9437192 | tf_op jit(solution)/shard_map/ppermute | solution.py:42
  4.1 0.4 collective-permute-start.7
  4.5 1.2 copy-done.13
  5.7 0.7 copy-done.24
  6.3 0.9 pack.1
  7.3 2.7 %collective-permute-start.1 = (bf16[64,4096]{1,0:T(8,128)(2,1)S(1)}, bf16[64,4096]{1,0:T(8,128)(2,1)S(1)}, u32[]{:S(2)}, u32[]{:S(2)}) collective-permute-start(bf16[64,4096]{1,0:T(8,128)(2,1)S(1)} %get-tuple-element.19), channel_id=1, source_target_pairs={{0,12},{1,13},{2,14},{3,15},{64,76},{65,77},{66,78},{67,79},{128,1... | collective-permute-start | bytes 1572872 | tf_op jit(solution)/shard_map/ppermute | solution.py:42
  10.0 12.0 %collective-permute-done.refs_1_ = bf16[64,4096]{1,0:T(8,128)(2,1)S(1)} collective-permute-done((bf16[64,4096]{1,0:T(8,128)(2,1)S(1)}, bf16[64,4096]{1,0:T(8,128)(2,1)S(1)}, u32[]{:S(2)}, u32[]{:S(2)}) %collective-permute-start) | collective-permute-done | bytes 524320 | tf_op jit(solution)/shard_map/ppermute | solution.py:42
  22.0 3.8 %collective-permute-start.2 = (bf16[64,4096]{1,0:T(8,128)(2,1)S(1)}, bf16[64,4096]{1,0:T(8,128)(2,1)S(1)}, u32[]{:S(2)}, u32[]{:S(2)}) collective-permute-start(bf16[64,4096]{1,0:T(8,128)(2,1)S(1)} %get-tuple-element.17.refs_0_), channel_id=1, source_target_pairs={{0,2},{1,195},{2,64},{3,1},{64,66},{65,3},{66,128},{67,65},{128,13... | collective-permute-start | bytes 1572872 | tf_op jit(solution)/shard_map/ppermute | solution.py:42
  25.8 1.5 %collective-permute-start.11 = (bf16[64,4096]{1,0:T(8,128)(2,1)S(1)}, bf16[64,4096]{1,0:T(8,128)(2,1)}, u32[]{:S(2)}, u32[]{:S(2)}) collective-permute-start(bf16[64,4096]{1,0:T(8,128)(2,1)S(1)} %get-tuple-element.24), channel_id=1, source_target_pairs={{0,8},{1,9},{2,10},{3,11},{64,72},{65,73},{66,74},{67,75},{128,136... | collective-permute-start | bytes 1572872 | tf_op jit(solution)/shard_map/ppermute | solution.py:42
  27.4 4.6 %collective-permute-done.2.refs_3_ = bf16[64,4096]{1,0:T(8,128)(2,1)S(1)} collective-permute-done((bf16[64,4096]{1,0:T(8,128)(2,1)S(1)}, bf16[64,4096]{1,0:T(8,128)(2,1)S(1)}, u32[]{:S(2)}, u32[]{:S(2)}) %collective-permute-start.2) | collective-permute-done | bytes 524320 | tf_op jit(solution)/shard_map/ppermute | solution.py:42
  31.9 3.5 %collective-permute-start.3 = (bf16[64,4096]{1,0:T(8,128)(2,1)S(1)}, bf16[64,4096]{1,0:T(8,128)(2,1)S(1)}, u32[]{:S(2)}, u32[]{:S(2)}) collective-permute-start(bf16[64,4096]{1,0:T(8,128)(2,1)S(1)} %collective-permute-done.refs_1_), channel_id=1, source_target_pairs={{0,2},{1,195},{2,64},{3,1},{64,66},{65,3},{66,128},{67,65},{128,13... | collective-permute-start | bytes 1572872 | tf_op jit(solution)/shard_map/ppermute | solution.py:42
  35.5 3.3 %collective-permute-done.11.refs_0_ = bf16[64,4096]{1,0:T(8,128)(2,1)} collective-permute-done((bf16[64,4096]{1,0:T(8,128)(2,1)S(1)}, bf16[64,4096]{1,0:T(8,128)(2,1)}, u32[]{:S(2)}, u32[]{:S(2)}) %collective-permute-start.11) | collective-permute-done | bytes 524320 | tf_op jit(solution)/shard_map/ppermute | solution.py:42
  38.8 2.8 %collective-permute-start.4 = (bf16[64,4096]{1,0:T(8,128)(2,1)S(1)}, bf16[64,4096]{1,0:T(8,128)(2,1)S(1)}, u32[]{:S(2)}, u32[]{:S(2)}) collective-permute-start(bf16[64,4096]{1,0:T(8,128)(2,1)S(1)} %collective-permute-done.1.refs_2_), channel_id=1, source_target_pairs={{0,2},{1,195},{2,64},{3,1},{64,66},{65,3},{66,128},{67,65},{128,13... | collective-permute-start | bytes 1572872 | tf_op jit(solution)/shard_map/ppermute | solution.py:42
  41.5 1.6 %copy-done = bf16[1,1,2,16,64,512]{5,4,3,2,1,0:T(8,128)(2,1)S(1)} copy-done((bf16[1,1,2,16,64,512]{5,4,3,2,1,0:T(8,128)(2,1)S(1)}, bf16[1,1,2,16,64,512]{5,4,3,2,1,0:T(8,128)(2,1)}, u32[]{:S(2)}) %copy-start) | copy-done | bytes 2097176
  43.1 0.7 copy-done.20
  43.8 0.7 copy-done.22
  44.5 1.6 %leave.1 = bf16[2,8,64,512]{3,2,1,0:T(8,128)(2,1)} custom-call(s32[4]{0:T(128)S(1)} %bitcast.25, s32[16]{0:T(128)S(1)} %bitcast.27, bf16[2,16,64,512]{3,2,1,0:T(8,128)(2,1)S(1)} %bitcast.13), custom_call_target="tpu_custom_call" | custom-call | bytes 3145728 | tf_op jit(solution)/shard_map/leave/pallas_call | solution.py:106
  46.0 2.4 %collective-permute-start.17 = (bf16[2,8,64,512]{3,2,1,0:T(8,128)(2,1)}, bf16[2,8,64,512]{3,2,1,0:T(8,128)(2,1)}, u32[]{:S(2)}, u32[]{:S(2)}) collective-permute-start(bf16[2,8,64,512]{3,2,1,0:T(8,128)(2,1)} %leave.1), channel_id=1, source_target_pairs={{0,128},{16,144},{32,160},{48,176},{64,192},{80,208},{96,224},{112... | collective-permute-start | bytes 3145736 | tf_op jit(solution)/shard_map/ppermute | solution.py:272
  48.4 2.3 %collective-permute-start.12 = (bf16[64,4096]{1,0:T(8,128)(2,1)}, bf16[64,4096]{1,0:T(8,128)(2,1)}, u32[]{:S(2)}, u32[]{:S(2)}) collective-permute-start(bf16[64,4096]{1,0:T(8,128)(2,1)} %collective-permute-done.11.refs_0_), channel_id=1, source_target_pairs={{0,2},{1,195},{2,64},{3,1},{64,66},{65,3},{66,128},{67,65},{128,13... | collective-permute-start | bytes 1572872 | tf_op jit(solution)/shard_map/ppermute | solution.py:42
  50.8 4.1 %copy-done.3 = bf16[1,4096,384]{2,1,0:T(8,128)(2,1)S(1)} copy-done((bf16[1,4096,384]{2,1,0:T(8,128)(2,1)S(1)}, bf16[1,4096,384]{2,1,0:T(8,128)(2,1)}, u32[]{:S(2)}) %copy-start.3) | copy-done | bytes 3145752
  55.0 1.9 %copy-done.5 = bf16[1,384,4096]{2,1,0:T(8,128)(2,1)S(1)} copy-done((bf16[1,384,4096]{2,1,0:T(8,128)(2,1)S(1)}, bf16[1,384,4096]{2,1,0:T(8,128)(2,1)}, u32[]{:S(2)}) %copy-start.5) | copy-done | bytes 3145752
  56.9 12.1 %experts.2 = (bf16[64,4096]{1,0:T(8,128)(2,1)S(1)}, bf16[64,4096]{1,0:T(8,128)(2,1)S(1)}, bf16[64,4096]{1,0:T(8,128)(2,1)S(1)}, bf16[64,4096]{1,0:T(8,128)(2,1)S...) custom-call(bf16[64,4096]{1,0:T(8,128)(2,1)S(1)} %get-tuple-element.17.refs_0_, ...), custom_call_target="tpu_custom_call" | custom-call | flops 7247757312 | bytes 18874368 | tf_op jit(solution)/shard_map/experts/pallas_call | solution.py:216
  69.0 0.8 copy-done.14
  69.8 0.8 copy-done.16
  70.7 0.8 copy-done.18
  71.4 0.8 copy-done.25
  72.3 0.8 copy-done.26
  73.1 5.8 %attend.1 = bf16[4,64,128]{2,1,0:T(8,128)(2,1)S(1)} custom-call(s32[4]{0:T(128)S(1)} %bitcast.26, s32[16]{0:T(128)S(1)} %bitcast.28, bf16[4,64,128]{2,1,0:T(8,128)(2,1)S(1)} %bitcast.24, bf16[2,16,64,512]{3,2,1,0:T(8,128)(2,1)S(1)} %bitcast.14), custom_call_target="tpu_custom_call" | custom-call | flops 67108864 | bytes 2097152 | tf_op jit(solution)/shard_map/attend/pallas_call | solution.py:143
  78.9 0.7 broadcast_in_dim_reshape.3
  79.6 13.1 %collective-permute-start.9 = (bf16[64,4096]{1,0:T(8,128)(2,1)}, bf16[64,4096]{1,0:T(8,128)(2,1)S(1)}, u32[]{:S(2)}, u32[]{:S(2)}) collective-permute-start(bf16[64,4096]{1,0:T(8,128)(2,1)} %copy-done.26), channel_id=1, source_target_pairs={{0,194},{1,3},{2,0},{3,65},{64,2},{65,67},{66,64},{67,129},{128,66... | collective-permute-start | bytes 1572872 | tf_op jit(solution)/shard_map/ppermute | solution.py:42
  92.7 2.9 %collective-permute-start.8 = (bf16[64,4096]{1,0:T(8,128)(2,1)}, bf16[64,4096]{1,0:T(8,128)(2,1)S(1)}, u32[]{:S(2)}, u32[]{:S(2)}) collective-permute-start(bf16[64,4096]{1,0:T(8,128)(2,1)} %copy-done.25), channel_id=1, source_target_pairs={{0,194},{1,3},{2,0},{3,65},{64,2},{65,67},{66,64},{67,129},{128,66... | collective-permute-start | bytes 1572872 | tf_op jit(solution)/shard_map/ppermute | solution.py:42
  95.6 10.0 %collective-permute-done.12.refs_1_ = bf16[64,4096]{1,0:T(8,128)(2,1)} collective-permute-done((bf16[64,4096]{1,0:T(8,128)(2,1)}, bf16[64,4096]{1,0:T(8,128)(2,1)}, u32[]{:S(2)}, u32[]{:S(2)}) %collective-permute-start.12) | collective-permute-done | bytes 524320 | tf_op jit(solution)/shard_map/ppermute | solution.py:42
  105.6 1.9 %copy-done.4 = bf16[1,4096,384]{2,1,0:T(8,128)(2,1)S(1)} copy-done((bf16[1,4096,384]{2,1,0:T(8,128)(2,1)S(1)}, bf16[1,4096,384]{2,1,0:T(8,128)(2,1)}, u32[]{:S(2)}) %copy-start.4) | copy-done | bytes 3145752
  107.5 1.9 %copy-done.6 = bf16[1,384,4096]{2,1,0:T(8,128)(2,1)S(1)} copy-done((bf16[1,384,4096]{2,1,0:T(8,128)(2,1)S(1)}, bf16[1,384,4096]{2,1,0:T(8,128)(2,1)}, u32[]{:S(2)}) %copy-start.6) | copy-done | bytes 3145752
  109.4 1.9 %copy-done.8 = bf16[4096,384]{1,0:T(8,128)(2,1)S(1)} copy-done((bf16[4096,384]{1,0:T(8,128)(2,1)S(1)}, bf16[4096,384]{1,0:T(8,128)(2,1)}, u32[]{:S(2)}) %copy-start.8) | copy-done | bytes 3145752
  111.3 1.9 %copy-done.10 = bf16[4096,384]{1,0:T(8,128)(2,1)S(1)} copy-done((bf16[4096,384]{1,0:T(8,128)(2,1)S(1)}, bf16[4096,384]{1,0:T(8,128)(2,1)}, u32[]{:S(2)}) %copy-start.10) | copy-done | bytes 3145752
  113.2 1.9 %copy-done.12 = bf16[384,4096]{1,0:T(8,128)(2,1)S(1)} copy-done((bf16[384,4096]{1,0:T(8,128)(2,1)S(1)}, bf16[384,4096]{1,0:T(8,128)(2,1)}, u32[]{:S(2)}) %copy-start.12) | copy-done | bytes 3145752
  115.1 6.4 %experts.3 = (bf16[64,4096]{1,0:T(8,128)(2,1)S(1)}, bf16[64,4096]{1,0:T(8,128)(2,1)S(1)}) custom-call(bf16[64,4096]{1,0:T(8,128)(2,1)} %collective-permute-done.11.refs_0_, bf16[64,4096]{1,0:T(8,128)(2,1)} %collective-permute-done.12.refs_1_, bf16[4096,384]{1,0:T(8,128)(2,1)S(1)} %bitcast.17, bf16[4096,384]{1,0:T(8,128)(2,1)S(1)} %copy-done.8, ...), custom_call_target="tpu_custom_call" | custom-call | flops 2415919104 | bytes 18874368 | tf_op jit(solution)/shard_map/experts/pallas_call | solution.py:216
  121.6 1.2 add_convert_fusion
  122.8 1.1 collective-permute-start.16
  123.9 0.1 add_convert_fusion.2
  124.0 1.7 %collective-permute-start.10 = (bf16[64,4096]{1,0:T(8,128)(2,1)S(1)}, bf16[64,4096]{1,0:T(8,128)(2,1)S(1)}, u32[]{:S(2)}, u32[]{:S(2)}) collective-permute-start(bf16[64,4096]{1,0:T(8,128)(2,1)S(1)} %add_convert_fusion.2), channel_id=1, source_target_pairs={{0,12},{1,13},{2,14},{3,15},{64,76},{65,77},{66,78},{67,79},{128,1... | collective-permute-start | bytes 1572872 | tf_op jit(solution)/shard_map/ppermute | solution.py:42
  125.8 6.1 %collective-permute-done.13 = bf16[64,4096]{1,0:T(8,128)(2,1)S(1)} collective-permute-done((bf16[64,4096]{1,0:T(8,128)(2,1)S(1)}, bf16[64,4096]{1,0:T(8,128)(2,1)S(1)}, u32[]{:S(2)}, u32[]{:S(2)}) %collective-permute-start.13) | collective-permute-done | bytes 524320 | tf_op jit(solution)/shard_map/ppermute | solution.py:42
  131.8 0.1 add_convert_fusion.1
  132.0 1.8 %collective-permute-start.14 = (bf16[64,4096]{1,0:T(8,128)(2,1)S(1)}, bf16[64,4096]{1,0:T(8,128)(2,1)S(1)}, u32[]{:S(2)}, u32[]{:S(2)}) collective-permute-start(bf16[64,4096]{1,0:T(8,128)(2,1)S(1)} %add_convert_fusion.1), channel_id=1, source_target_pairs={{0,8},{1,9},{2,10},{3,11},{64,72},{65,73},{66,74},{67,75},{128,136... | collective-permute-start | bytes 1572872 | tf_op jit(solution)/shard_map/ppermute | solution.py:42
  133.9 13.7 %collective-permute-done.16.refs_3_ = bf16[64,4096]{1,0:T(8,128)(2,1)S(1)} collective-permute-done((bf16[64,4096]{1,0:T(8,128)(2,1)S(1)}, bf16[64,4096]{1,0:T(8,128)(2,1)S(1)}, u32[]{:S(2)}, u32[]{:S(2)}) %collective-permute-start.16) | collective-permute-done | bytes 524320 | tf_op jit(solution)/shard_map/ppermute | solution.py:42
  147.6 2.3 %bring_home.1 = bf16[128,4096]{1,0:T(8,128)(2,1)} custom-call(bf16[256,128]{1,0:T(8,128)(2,1)S(1)} %get-tuple-element.16.onehot, bf16[64,4096]{1,0:T(8,128)(2,1)S(1)} %add_convert_fusion.3.refs_0_, bf16[64,4096]{1,0:T(8,128)(2,1)S(1)} %collective-permute-done.10.refs_1_, bf16[64,4096]{1,0:T(8,128)(2,1)S(1)} %collective-permute-done.14.refs_2_, ...), custom_call_target="tpu_custom_call" | custom-call | flops 268435456 | bytes 3145728 | tf_op jit(solution)/shard_map/bring_home/pallas_call | solution.py:249
  149.9 2.3 %copy.16 = bf16[1,1,2,8,64,512]{5,4,3,2,1,0:T(8,128)(2,1)} copy(bf16[1,1,2,8,64,512]{5,4,3,2,1,0:T(8,128)(2,1)} %bitcast.7) | data formatting | bytes 2097152
  (57 shorter events, 0.6 us)
Async XLA Ops:
  0.6 50.2 %collective-permute-start.5 = (bf16[4096,384]{1,0:T(8,128)(2,1)}, bf16[4096,384]{1,0:T(8,128)(2,1)S(1)}, u32[]{:S(2)}, u32[]{:S(2)}) collective-permute-start(bf16[4096,384]{1,0:T(8,128)(2,1)} %bitcast.15), channel_id=1, source_target_pairs={{0,1},{1,0},{2,3},{3,2},{64,65},{65,64},{66,67},{67,66},{128,129},... | collective-permute-start | bytes 9437192 | tf_op jit(solution)/shard_map/ppermute | solution.py:42
  4.0 46.8 %collective-permute-start.6 = (bf16[4096,384]{1,0:T(8,128)(2,1)}, bf16[4096,384]{1,0:T(8,128)(2,1)S(1)}, u32[]{:S(2)}, u32[]{:S(2)}) collective-permute-start(bf16[4096,384]{1,0:T(8,128)(2,1)} %bitcast.18), channel_id=1, source_target_pairs={{0,1},{1,0},{2,3},{3,2},{64,65},{65,64},{66,67},{67,66},{128,129},... | collective-permute-start | bytes 9437192 | tf_op jit(solution)/shard_map/ppermute | solution.py:42
  4.1 46.7 %collective-permute-start.7 = (bf16[384,4096]{1,0:T(8,128)(2,1)}, bf16[384,4096]{1,0:T(8,128)(2,1)S(1)}, u32[]{:S(2)}, u32[]{:S(2)}) collective-permute-start(bf16[384,4096]{1,0:T(8,128)(2,1)} %bitcast.21), channel_id=1, source_target_pairs={{0,1},{1,0},{2,3},{3,2},{64,65},{65,64},{66,67},{67,66},{128,129},... | collective-permute-start | bytes 9437192 | tf_op jit(solution)/shard_map/ppermute | solution.py:42
  4.5 1.2 copy-start.13
  5.7 0.7 copy-start.24
  7.2 14.8 %collective-permute-start = (bf16[64,4096]{1,0:T(8,128)(2,1)S(1)}, bf16[64,4096]{1,0:T(8,128)(2,1)S(1)}, u32[]{:S(2)}, u32[]{:S(2)}) collective-permute-start(bf16[64,4096]{1,0:T(8,128)(2,1)S(1)} %get-tuple-element.18), channel_id=1, source_target_pairs={{0,4},{1,5},{2,6},{3,7},{64,68},{65,69},{66,70},{67,71},{128,132},... | collective-permute-start | bytes 1572872 | tf_op jit(solution)/shard_map/ppermute | solution.py:42
  7.3 18.5 %collective-permute-start.1 = (bf16[64,4096]{1,0:T(8,128)(2,1)S(1)}, bf16[64,4096]{1,0:T(8,128)(2,1)S(1)}, u32[]{:S(2)}, u32[]{:S(2)}) collective-permute-start(bf16[64,4096]{1,0:T(8,128)(2,1)S(1)} %get-tuple-element.19), channel_id=1, source_target_pairs={{0,12},{1,13},{2,14},{3,15},{64,76},{65,77},{66,78},{67,79},{128,1... | collective-permute-start | bytes 1572872 | tf_op jit(solution)/shard_map/ppermute | solution.py:42
  22.0 10.0 %collective-permute-start.2 = (bf16[64,4096]{1,0:T(8,128)(2,1)S(1)}, bf16[64,4096]{1,0:T(8,128)(2,1)S(1)}, u32[]{:S(2)}, u32[]{:S(2)}) collective-permute-start(bf16[64,4096]{1,0:T(8,128)(2,1)S(1)} %get-tuple-element.17.refs_0_), channel_id=1, source_target_pairs={{0,2},{1,195},{2,64},{3,1},{64,66},{65,3},{66,128},{67,65},{128,13... | collective-permute-start | bytes 1572872 | tf_op jit(solution)/shard_map/ppermute | solution.py:42
  25.8 12.9 %collective-permute-start.11 = (bf16[64,4096]{1,0:T(8,128)(2,1)S(1)}, bf16[64,4096]{1,0:T(8,128)(2,1)}, u32[]{:S(2)}, u32[]{:S(2)}) collective-permute-start(bf16[64,4096]{1,0:T(8,128)(2,1)S(1)} %get-tuple-element.24), channel_id=1, source_target_pairs={{0,8},{1,9},{2,10},{3,11},{64,72},{65,73},{66,74},{67,75},{128,136... | collective-permute-start | bytes 1572872 | tf_op jit(solution)/shard_map/ppermute | solution.py:42
  31.9 14.1 %collective-permute-start.3 = (bf16[64,4096]{1,0:T(8,128)(2,1)S(1)}, bf16[64,4096]{1,0:T(8,128)(2,1)S(1)}, u32[]{:S(2)}, u32[]{:S(2)}) collective-permute-start(bf16[64,4096]{1,0:T(8,128)(2,1)S(1)} %collective-permute-done.refs_1_), channel_id=1, source_target_pairs={{0,2},{1,195},{2,64},{3,1},{64,66},{65,3},{66,128},{67,65},{128,13... | collective-permute-start | bytes 1572872 | tf_op jit(solution)/shard_map/ppermute | solution.py:42
  38.8 9.7 %collective-permute-start.4 = (bf16[64,4096]{1,0:T(8,128)(2,1)S(1)}, bf16[64,4096]{1,0:T(8,128)(2,1)S(1)}, u32[]{:S(2)}, u32[]{:S(2)}) collective-permute-start(bf16[64,4096]{1,0:T(8,128)(2,1)S(1)} %collective-permute-done.1.refs_2_), channel_id=1, source_target_pairs={{0,2},{1,195},{2,64},{3,1},{64,66},{65,3},{66,128},{67,65},{128,13... | collective-permute-start | bytes 1572872 | tf_op jit(solution)/shard_map/ppermute | solution.py:42
  41.5 1.6 %copy-start = (bf16[1,1,2,16,64,512]{5,4,3,2,1,0:T(8,128)(2,1)S(1)}, bf16[1,1,2,16,64,512]{5,4,3,2,1,0:T(8,128)(2,1)}, u32[]{:S(2)}) copy-start(bf16[1,1,2,16,64,512]{5,4,3,2,1,0:T(8,128)(2,1)} %param.10) | copy-start | bytes 6291460
  43.1 0.7 copy-start.20
  43.8 0.7 copy-start.22
  44.4 6.4 %copy-start.2 = (bf16[1,4096,384]{2,1,0:T(8,128)(2,1)S(1)}, bf16[1,4096,384]{2,1,0:T(8,128)(2,1)}, u32[]{:S(2)}) copy-start(bf16[1,4096,384]{2,1,0:T(8,128)(2,1)} %param.15) | copy-start | bytes 9437188
  44.4 28.6 %copy-start.21 = (s32[1,1,4]{2,1,0:T(1,128)S(1)}, s32[1,1,4]{2,1,0:T(1,128)}, u32[]{:S(2)}) copy-start(s32[1,1,4]{2,1,0:T(1,128)} %param.11) | copy-start | bytes 52
  44.4 28.6 %copy-start.23 = (s32[1,1,16]{2,1,0:T(1,128)S(1)}, s32[1,1,16]{2,1,0:T(1,128)}, u32[]{:S(2)}) copy-start(s32[1,1,16]{2,1,0:T(1,128)} %param.12) | copy-start | bytes 196
  46.0 27.1 %copy-start.1 = (bf16[1,1,2,16,64,512]{5,4,3,2,1,0:T(8,128)(2,1)S(1)}, bf16[1,1,2,16,64,512]{5,4,3,2,1,0:T(8,128)(2,1)}, u32[]{:S(2)}) copy-start(bf16[1,1,2,16,64,512]{5,4,3,2,1,0:T(8,128)(2,1)} %param.10) | copy-start | bytes 6291460
  46.0 33.5 %collective-permute-start.17 = (bf16[2,8,64,512]{3,2,1,0:T(8,128)(2,1)}, bf16[2,8,64,512]{3,2,1,0:T(8,128)(2,1)}, u32[]{:S(2)}, u32[]{:S(2)}) collective-permute-start(bf16[2,8,64,512]{3,2,1,0:T(8,128)(2,1)} %leave.1), channel_id=1, source_target_pairs={{0,128},{16,144},{32,160},{48,176},{64,192},{80,208},{96,224},{112... | collective-permute-start | bytes 3145736 | tf_op jit(solution)/shard_map/ppermute | solution.py:272
  48.4 57.2 %collective-permute-start.12 = (bf16[64,4096]{1,0:T(8,128)(2,1)}, bf16[64,4096]{1,0:T(8,128)(2,1)}, u32[]{:S(2)}, u32[]{:S(2)}) collective-permute-start(bf16[64,4096]{1,0:T(8,128)(2,1)} %collective-permute-done.11.refs_0_), channel_id=1, source_target_pairs={{0,2},{1,195},{2,64},{3,1},{64,66},{65,3},{66,128},{67,65},{128,13... | collective-permute-start | bytes 1572872 | tf_op jit(solution)/shard_map/ppermute | solution.py:42
  50.8 18.2 %copy-start.7 = (bf16[4096,384]{1,0:T(8,128)(2,1)}, bf16[4096,384]{1,0:T(8,128)(2,1)S(1)}, u32[]{:S(2)}) copy-start(bf16[4096,384]{1,0:T(8,128)(2,1)S(1)} %collective-permute-done.5.refs_7_.refs_3_) | copy-start | bytes 9437188
  50.8 18.2 %copy-start.9 = (bf16[4096,384]{1,0:T(8,128)(2,1)}, bf16[4096,384]{1,0:T(8,128)(2,1)S(1)}, u32[]{:S(2)}) copy-start(bf16[4096,384]{1,0:T(8,128)(2,1)S(1)} %collective-permute-done.6.refs_9_.refs_5_) | copy-start | bytes 9437188
  50.8 4.1 %copy-start.3 = (bf16[1,4096,384]{2,1,0:T(8,128)(2,1)S(1)}, bf16[1,4096,384]{2,1,0:T(8,128)(2,1)}, u32[]{:S(2)}) copy-start(bf16[1,4096,384]{2,1,0:T(8,128)(2,1)} %param.16) | copy-start | bytes 9437188
  55.0 1.9 %copy-start.5 = (bf16[1,384,4096]{2,1,0:T(8,128)(2,1)S(1)}, bf16[1,384,4096]{2,1,0:T(8,128)(2,1)}, u32[]{:S(2)}) copy-start(bf16[1,384,4096]{2,1,0:T(8,128)(2,1)} %param.17) | copy-start | bytes 9437188
  56.9 12.2 %copy-start.11 = (bf16[384,4096]{1,0:T(8,128)(2,1)}, bf16[384,4096]{1,0:T(8,128)(2,1)S(1)}, u32[]{:S(2)}) copy-start(bf16[384,4096]{1,0:T(8,128)(2,1)S(1)} %collective-permute-done.7.refs_11_.refs_7_) | copy-start | bytes 9437188
  56.9 16.2 %copy-start.27 = (bf16[1,1,4,8192]{3,2,1,0:T(4,128)(2,1)S(1)}, bf16[1,1,4,8192]{3,2,1,0:T(4,128)(2,1)}, u32[]{:S(2)}) copy-start(bf16[1,1,4,8192]{3,2,1,0:T(4,128)(2,1)} %param.9) | copy-start | bytes 196612
  69.0 0.8 copy-start.14
  69.8 0.8 copy-start.16
  70.7 0.8 copy-start.18
  71.4 0.8 copy-start.25
  72.3 0.8 copy-start.26
  73.1 48.5 %collective-permute-start.15 = (bf16[64,4096]{1,0:T(8,128)(2,1)}, bf16[64,4096]{1,0:T(8,128)(2,1)}, u32[]{:S(2)}, u32[]{:S(2)}) collective-permute-start(bf16[64,4096]{1,0:T(8,128)(2,1)} %get-tuple-element.28), channel_id=1, source_target_pairs={{0,194},{1,3},{2,0},{3,65},{64,2},{65,67},{66,64},{67,129},{128,66... | collective-permute-start | bytes 1572872 | tf_op jit(solution)/shard_map/ppermute | solution.py:42
  79.6 44.3 %collective-permute-start.9 = (bf16[64,4096]{1,0:T(8,128)(2,1)}, bf16[64,4096]{1,0:T(8,128)(2,1)S(1)}, u32[]{:S(2)}, u32[]{:S(2)}) collective-permute-start(bf16[64,4096]{1,0:T(8,128)(2,1)} %copy-done.26), channel_id=1, source_target_pairs={{0,194},{1,3},{2,0},{3,65},{64,2},{65,67},{66,64},{67,129},{128,66... | collective-permute-start | bytes 1572872 | tf_op jit(solution)/shard_map/ppermute | solution.py:42
  92.7 41.1 %collective-permute-start.8 = (bf16[64,4096]{1,0:T(8,128)(2,1)}, bf16[64,4096]{1,0:T(8,128)(2,1)S(1)}, u32[]{:S(2)}, u32[]{:S(2)}) collective-permute-start(bf16[64,4096]{1,0:T(8,128)(2,1)} %copy-done.25), channel_id=1, source_target_pairs={{0,194},{1,3},{2,0},{3,65},{64,2},{65,67},{66,64},{67,129},{128,66... | collective-permute-start | bytes 1572872 | tf_op jit(solution)/shard_map/ppermute | solution.py:42
  105.6 1.9 %copy-start.4 = (bf16[1,4096,384]{2,1,0:T(8,128)(2,1)S(1)}, bf16[1,4096,384]{2,1,0:T(8,128)(2,1)}, u32[]{:S(2)}) copy-start(bf16[1,4096,384]{2,1,0:T(8,128)(2,1)} %param.16) | copy-start | bytes 9437188
  107.5 1.9 %copy-start.6 = (bf16[1,384,4096]{2,1,0:T(8,128)(2,1)S(1)}, bf16[1,384,4096]{2,1,0:T(8,128)(2,1)}, u32[]{:S(2)}) copy-start(bf16[1,384,4096]{2,1,0:T(8,128)(2,1)} %param.17) | copy-start | bytes 9437188
  109.4 1.9 %copy-start.8 = (bf16[4096,384]{1,0:T(8,128)(2,1)S(1)}, bf16[4096,384]{1,0:T(8,128)(2,1)}, u32[]{:S(2)}) copy-start(bf16[4096,384]{1,0:T(8,128)(2,1)} %copy-done.7) | copy-start | bytes 9437188
  111.3 1.9 %copy-start.10 = (bf16[4096,384]{1,0:T(8,128)(2,1)S(1)}, bf16[4096,384]{1,0:T(8,128)(2,1)}, u32[]{:S(2)}) copy-start(bf16[4096,384]{1,0:T(8,128)(2,1)} %copy-done.9) | copy-start | bytes 9437188
  113.2 1.9 %copy-start.12 = (bf16[384,4096]{1,0:T(8,128)(2,1)S(1)}, bf16[384,4096]{1,0:T(8,128)(2,1)}, u32[]{:S(2)}) copy-start(bf16[384,4096]{1,0:T(8,128)(2,1)} %copy-done.11) | copy-start | bytes 9437188
  115.1 6.5 %copy-start.19 = (bf16[64,4096]{1,0:T(8,128)(2,1)S(1)}, bf16[64,4096]{1,0:T(8,128)(2,1)}, u32[]{:S(2)}) copy-start(bf16[64,4096]{1,0:T(8,128)(2,1)} %copy-done.18) | copy-start | bytes 1572868
  115.1 8.8 %copy-start.17 = (bf16[64,4096]{1,0:T(8,128)(2,1)S(1)}, bf16[64,4096]{1,0:T(8,128)(2,1)}, u32[]{:S(2)}) copy-start(bf16[64,4096]{1,0:T(8,128)(2,1)} %copy-done.16) | copy-start | bytes 1572868
  121.5 12.3 %copy-start.15 = (bf16[64,4096]{1,0:T(8,128)(2,1)S(1)}, bf16[64,4096]{1,0:T(8,128)(2,1)}, u32[]{:S(2)}) copy-start(bf16[64,4096]{1,0:T(8,128)(2,1)} %copy-done.14) | copy-start | bytes 1572868
  121.5 10.3 %collective-permute-start.13 = (bf16[64,4096]{1,0:T(8,128)(2,1)S(1)}, bf16[64,4096]{1,0:T(8,128)(2,1)S(1)}, u32[]{:S(2)}, u32[]{:S(2)}) collective-permute-start(bf16[64,4096]{1,0:T(8,128)(2,1)S(1)} %get-tuple-element.26), channel_id=1, source_target_pairs={{0,194},{1,3},{2,0},{3,65},{64,2},{65,67},{66,64},{67,129},{128,66... | collective-permute-start | bytes 1572872 | tf_op jit(solution)/shard_map/ppermute | solution.py:42
  122.8 24.8 %collective-permute-start.16 = (bf16[64,4096]{1,0:T(8,128)(2,1)S(1)}, bf16[64,4096]{1,0:T(8,128)(2,1)S(1)}, u32[]{:S(2)}, u32[]{:S(2)}) collective-permute-start(bf16[64,4096]{1,0:T(8,128)(2,1)S(1)} %add_convert_fusion), channel_id=1, source_target_pairs={{0,4},{1,5},{2,6},{3,7},{64,68},{65,69},{66,70},{67,71},{128,132},... | collective-permute-start | bytes 1572872 | tf_op jit(solution)/shard_map/ppermute | solution.py:42
  124.0 23.6 %collective-permute-start.10 = (bf16[64,4096]{1,0:T(8,128)(2,1)S(1)}, bf16[64,4096]{1,0:T(8,128)(2,1)S(1)}, u32[]{:S(2)}, u32[]{:S(2)}) collective-permute-start(bf16[64,4096]{1,0:T(8,128)(2,1)S(1)} %add_convert_fusion.2), channel_id=1, source_target_pairs={{0,12},{1,13},{2,14},{3,15},{64,76},{65,77},{66,78},{67,79},{128,1... | collective-permute-start | bytes 1572872 | tf_op jit(solution)/shard_map/ppermute | solution.py:42
  132.0 15.6 %collective-permute-start.14 = (bf16[64,4096]{1,0:T(8,128)(2,1)S(1)}, bf16[64,4096]{1,0:T(8,128)(2,1)S(1)}, u32[]{:S(2)}, u32[]{:S(2)}) collective-permute-start(bf16[64,4096]{1,0:T(8,128)(2,1)S(1)} %add_convert_fusion.1), channel_id=1, source_target_pairs={{0,8},{1,9},{2,10},{3,11},{64,72},{65,73},{66,74},{67,75},{128,136... | collective-permute-start | bytes 1572872 | tf_op jit(solution)/shard_map/ppermute | solution.py:42

commit v3 on v2

v3 whole, which is shorter than its diff:
```python
import functools

import jax
import jax.numpy as jnp
from jax import lax
from jax.experimental import pallas as pl
from jax.experimental.pallas import tpu as pltpu
from jax.sharding import PartitionSpec as P

HEADS = 64
KV_HEADS = 4
HEAD_DIM = 128
GROUP = HEADS // KV_HEADS
PAGE = 64
MAXP = 8
PAGES = 16
REQS = 4
CAP = 64
TOK = 128
D = 4096
FQ = 384
NX, NY, NZ, NC = 4, 4, 8, 2
KB, NB = 2048, 1024
EARLY = 4
MIB = 1 << 20
VMEM = pltpu.VMEM
SMEM = pltpu.SMEM
LANE = 128
NO_COST = pl.CostEstimate(flops=0, bytes_accessed=0, transcendentals=0)
ANYWHERE = [pl.BlockSpec(memory_space=pl.ANY)]


def device_id(x, y, z, c):
    x, y, z = x % NX, y % NY, z % NZ
    return ((z // 2) * NY + y) * 16 + x * 4 + (z % 2) * 2 + c


def move(block, to):
    route = [
        (device_id(x, y, z, c), device_id(*to(x, y, z, c)))
        for x in range(NX)
        for y in range(NY)
        for z in range(NZ)
        for c in range(NC)
    ]
    return lax.ppermute(block, ("inst", "ep"), route)


def over_x(block, dx):
    return move(block, lambda x, y, z, c: (x + dx, y, z, c))


def over_z(block):
    return move(block, lambda x, y, z, c: (x, y, z + 1 - 2 * c, c))


def back_over_z(block):
    return move(block, lambda x, y, z, c: (x, y, z - 1 + 2 * c, c))


def other_core(block):
    return move(block, lambda x, y, z, c: (x, y, z, 1 - c))


def bundle_copies(weights, bundle):
    gate, up, down = weights
    copies, row = [], 0
    for w in (gate, up, down):
        size = w.shape[0]
        for j in range(w.shape[1] // LANE):
            copies.append((w.at[:, j * LANE : (j + 1) * LANE], bundle.at[row : row + size, :]))
            row += size
    return copies


def pack_kernel(routes, hidden, *refs):
    weights, (onehot, *pieces, bundle), (tokens, named, sems) = refs[:3], refs[3:9], refs[9:]
    first = [(routes, named), (hidden, tokens)]
    copies = [
        pltpu.make_async_copy(src, dst, sems.at[i])
        for i, (src, dst) in enumerate(first + bundle_copies(weights, bundle))
    ]
    for copy in copies:
        copy.start()
    copies[0].wait()
    x = lax.axis_index("ep") // 4
    rel = jnp.bitwise_and(named[...] - x, NX - 1)
    match = (rel == lax.broadcasted_iota(jnp.int32, (8, TOK), 0)).astype(jnp.float32)
    earlier = lax.broadcasted_iota(jnp.int32, (TOK, TOK), 0) < lax.broadcasted_iota(
        jnp.int32, (TOK, TOK), 1
    )
    rank = jnp.dot(
        match.astype(jnp.bfloat16),
        earlier.astype(jnp.float32).astype(jnp.bfloat16),
        preferred_element_type=jnp.float32,
    )
    slot = jnp.sum(rank * match, axis=0, keepdims=True).astype(jnp.int32)
    target = rel * CAP + slot
    chosen = (lax.broadcasted_iota(jnp.int32, (NX * CAP, TOK), 0) == target).astype(jnp.float32)
    onehot[...] = chosen.astype(jnp.bfloat16)
    copies[1].wait()
    for d in range(NX):
        pieces[d][...] = jnp.dot(
            onehot[d * CAP : (d + 1) * CAP, :], tokens[...], preferred_element_type=jnp.float32
        ).astype(jnp.bfloat16)
    for copy in copies[2:]:
        copy.wait()


def pack(routes, hidden, gate, up, down):
    return pl.pallas_call(
        pack_kernel,
        out_shape=[jax.ShapeDtypeStruct((NX * CAP, TOK), jnp.bfloat16)]
        + [jax.ShapeDtypeStruct((CAP, D), jnp.bfloat16)] * NX
        + [jax.ShapeDtypeStruct((9 * D, LANE), jnp.bfloat16)],
        in_specs=[pl.BlockSpec(memory_space=pltpu.HBM)] * 5,
        out_specs=[pl.BlockSpec(memory_space=VMEM)] * (2 + NX),
        scratch_shapes=[
            pltpu.VMEM((TOK, D), jnp.bfloat16),
            pltpu.VMEM((1, TOK), jnp.int32),
            pltpu.SemaphoreType.DMA((2 + 6 + D // LANE,)),
        ],
        compiler_params=pltpu.CompilerParams(vmem_limit_bytes=8 * MIB),
        cost_estimate=NO_COST,
        name="pack",
    )(
        *(
            pltpu.with_memory_space_constraint(v, pltpu.HBM)
            for v in (routes.reshape(1, TOK), hidden, gate, up, down)
        )
    )


def leave_kernel(parts, ctx, order, kv, *refs):
    out = refs[-1]
    pages = (ctx[0] + (PAGE - 1)) // PAGE
    for i, (side, j) in enumerate(parts):
        page = kv[side, order[j]]
        out[i] = jnp.where(j < pages, page, jnp.zeros_like(page))


def leave(parts, ctx, order, kv, *deps):
    return pl.pallas_call(
        functools.partial(leave_kernel, parts),
        out_shape=jax.ShapeDtypeStruct((len(parts), PAGE, KV_HEADS * HEAD_DIM), jnp.bfloat16),
        in_specs=[pl.BlockSpec(memory_space=SMEM)] * 2
        + [pl.BlockSpec(memory_space=VMEM)]
        + ANYWHERE * len(deps),
        out_specs=pl.BlockSpec(memory_space=VMEM),
        compiler_params=pltpu.CompilerParams(vmem_limit_bytes=8 * MIB),
        cost_estimate=NO_COST,
        name="leave",
    )(ctx, order, kv, *deps)


def land_kernel(*refs):
    *blocks, out = refs
    row = 0
    for block in blocks:
        out[row : row + block.shape[0]] = block[...]
        row += block.shape[0]


def land(*blocks):
    rows = 2 * MAXP
    out = pl.pallas_call(
        land_kernel,
        out_shape=jax.ShapeDtypeStruct((rows, PAGE, KV_HEADS * HEAD_DIM), jnp.bfloat16),
        in_specs=[pl.BlockSpec(memory_space=VMEM)] * len(blocks),
        out_specs=pl.BlockSpec(memory_space=VMEM),
        compiler_params=pltpu.CompilerParams(vmem_limit_bytes=8 * MIB),
        cost_estimate=NO_COST,
        name="land",
    )(*blocks)
    return out.reshape(2, MAXP, PAGE, KV_HEADS * HEAD_DIM)


def onward(block):
    return lax.ppermute(block, "inst", [(i, i + 8) for i in range(8)])


def attend_kernel(ctx, order, queries, kv, *refs):
    out = refs[-1]
    start = 0
    for r in range(REQS):
        length = ctx[r]
        page_of = [order[jnp.minimum(start + j, PAGES - 1)] for j in range(MAXP)]
        start = start + (length + (PAGE - 1)) // PAGE
        inside = lax.broadcasted_iota(jnp.int32, (GROUP, MAXP * PAGE), 1) < length
        for g in range(KV_HEADS):
            cols = slice(g * HEAD_DIM, (g + 1) * HEAD_DIM)
            keys = jnp.concatenate([kv[0, p, :, cols] for p in page_of], 0)
            values = jnp.concatenate([kv[1, p, :, cols] for p in page_of], 0)
            scores = lax.dot_general(
                queries[r, g * GROUP : (g + 1) * GROUP, :],
                keys,
                (((1,), (1,)), ((), ())),
                preferred_element_type=jnp.float32,
            ) * HEAD_DIM ** (-0.5)
            scores = jnp.where(inside, scores, -1e30)
            expo = jnp.exp(scores - jnp.max(scores, axis=-1, keepdims=True))
            probs = (expo / jnp.sum(expo, axis=-1, keepdims=True)).astype(jnp.bfloat16)
            mixed = jnp.dot(probs, values, preferred_element_type=jnp.float32).astype(jnp.bfloat16)
            for h in range(GROUP):
                head = (g * GROUP + h) * HEAD_DIM
                out[r : r + 1, head : head + HEAD_DIM] = mixed[h : h + 1, :]


def attend(ctx, order, queries, kv, *deps):
    return pl.pallas_call(
        attend_kernel,
        out_shape=jax.ShapeDtypeStruct((REQS, HEADS * HEAD_DIM), jnp.bfloat16),
        in_specs=[pl.BlockSpec(memory_space=SMEM)] * 2
        + [pl.BlockSpec(memory_space=VMEM)] * 2
        + ANYWHERE * len(deps),
        out_specs=pl.BlockSpec(memory_space=VMEM),
        compiler_params=pltpu.CompilerParams(vmem_limit_bytes=8 * MIB),
        cost_estimate=pl.CostEstimate(
            flops=0, bytes_accessed=12 * MIB, transcendentals=0
        ),
        name="attend",
    )(ctx, order, queries.reshape(REQS, HEADS, HEAD_DIM), kv, *deps)


def expert_kernel(*refs):
    rows, bundles, (*outs, gate, upper, hidden) = refs[:2], refs[2:4], refs[-5:]

    def widen(k, first):
        ks = pl.ds(pl.multiple_of(k * KB, KB), KB)
        block = jnp.concatenate([r[:, ks] for r in rows], 0)
        for base, total in ((0, gate), (3 * D, upper)):
            new = jnp.dot(
                block,
                jnp.concatenate(
                    [
                        w[pl.ds(pl.multiple_of(base + j * D + k * KB, KB), KB), :]
                        for w in bundles
                        for j in range(3)
                    ],
                    1,
                ),
                preferred_element_type=jnp.float32,
            )
            if first:
                total[...] = new
            else:
                total[...] += new

    widen(0, True)

    @pl.loop(1, D // KB)
    def _(k):
        widen(k, False)

    v = gate[...]
    hidden[...] = (v / (1.0 + jnp.exp(-v)) * upper[...]).astype(jnp.bfloat16)
    across = NB // LANE

    @pl.loop(0, D // NB)
    def _(n):
        ns = pl.ds(pl.multiple_of(n * NB, NB), NB)
        down = jnp.concatenate(
            [
                jnp.concatenate(
                    [
                        w[pl.ds(pl.multiple_of(6 * D + (n * across + j) * FQ, LANE), FQ), :]
                        for j in range(across)
                    ],
                    1,
                )
                for w in bundles
            ],
            0,
        )
        part = jnp.dot(hidden[...], down, preferred_element_type=jnp.float32).astype(jnp.bfloat16)
        for i, out in enumerate(outs):
            out[:, ns] = part[i * CAP : (i + 1) * CAP]


def experts(rows, bundles, *deps):
    size = 2 * CAP
    return pl.pallas_call(
        expert_kernel,
        out_shape=[jax.ShapeDtypeStruct((CAP, D), jnp.bfloat16)] * 2,
        in_specs=[pl.BlockSpec(memory_space=VMEM)] * 4 + ANYWHERE * len(deps),
        out_specs=[pl.BlockSpec(memory_space=VMEM)] * 2,
        scratch_shapes=[
            pltpu.VMEM((size, 2 * FQ), jnp.float32),
            pltpu.VMEM((size, 2 * FQ), jnp.float32),
            pltpu.VMEM((size, 2 * FQ), jnp.bfloat16),
        ],
        compiler_params=pltpu.CompilerParams(vmem_limit_bytes=8 * MIB),
        cost_estimate=pl.CostEstimate(
            flops=0, bytes_accessed=12 * MIB, transcendentals=0
        ),
        name="experts",
    )(*rows, *bundles, *deps)


def hold_kernel(block, *refs):
    refs[-1][...] = block[...]


def hold(block, *deps):
    return pl.pallas_call(
        hold_kernel,
        out_shape=jax.ShapeDtypeStruct(block.shape, block.dtype),
        in_specs=[pl.BlockSpec(memory_space=VMEM)] + ANYWHERE * len(deps),
        out_specs=pl.BlockSpec(memory_space=VMEM),
        compiler_params=pltpu.CompilerParams(vmem_limit_bytes=8 * MIB),
        cost_estimate=NO_COST,
        name="hold",
    )(block, *deps)


def home_kernel(onehot, *refs):
    *pieces, out = refs
    out[...] = lax.dot_general(
        onehot[...],
        jnp.concatenate([p[...] for p in pieces], 0),
        (((0,), (0,)), ((), ())),
        preferred_element_type=jnp.float32,
    ).astype(jnp.bfloat16)


def bring_home(onehot, pieces):
    nb = D // 4
    return pl.pallas_call(
        home_kernel,
        out_shape=jax.ShapeDtypeStruct((TOK, D), jnp.bfloat16),
        grid=(4,),
        in_specs=[pl.BlockSpec((NX * CAP, TOK), lambda i: (0, 0))]
        + [pl.BlockSpec((CAP, nb), lambda i: (0, i))] * NX,
        out_specs=pl.BlockSpec((TOK, nb), lambda i: (0, i)),
        compiler_params=pltpu.CompilerParams(vmem_limit_bytes=8 * MIB),
        cost_estimate=NO_COST,
        name="bring_home",
    )(onehot, *pieces)


def add_kernel(a, b, out):
    out[...] = (a[...].astype(jnp.float32) + b[...].astype(jnp.float32)).astype(jnp.bfloat16)


def add(a, b):
    return pl.pallas_call(
        add_kernel,
        out_shape=jax.ShapeDtypeStruct(a.shape, a.dtype),
        in_specs=[pl.BlockSpec(memory_space=VMEM)] * 2,
        out_specs=pl.BlockSpec(memory_space=VMEM),
        compiler_params=pltpu.CompilerParams(vmem_limit_bytes=8 * MIB),
        cost_estimate=NO_COST,
        name="add",
    )(a, b)


def local(queries, kv_cache, ctx_len, page_order, hidden_in, routes, w_gate, w_up, w_down):
    ctx, order, kv = ctx_len[0, 0], page_order[0, 0], kv_cache[0, 0]
    leaving = [(side, j) for side in range(2) for j in range(MAXP)]
    onehot, *piece, bundle = pack(routes, hidden_in, w_gate[0], w_up[0], w_down[0])
    bundles = tuple(
        pltpu.with_memory_space_constraint(b, VMEM) for b in (bundle, other_core(bundle))
    )
    first = onward(leave(leaving[:EARLY], ctx, order, kv, onehot))
    attn_out = attend(ctx, order, queries[0, 0], kv, onehot)
    got = [piece[0]] + [over_x(piece[d], d) for d in (1, 2, 3)]
    got[1] = hold(got[1], attn_out, first)
    got[2] = hold(got[2], got[3])
    across = [over_z(g) for g in got]
    home = [None] * NX
    whole = {}
    kept = attn_out
    for d in (1, 3, 2, 0):
        deps = (kept,) if d else (kept, whole[1], whole[3])
        kept, lent = experts((got[d], across[d]), bundles, *deps)
        returned = back_over_z(lent)
        whole[d] = add(kept, returned)
        home[d] = over_x(whole[d], -d) if d else whole[d]
    rest = onward(leave(leaving[EARLY:], ctx, order, kv, returned))
    moe_out = bring_home(onehot, home)
    return attn_out[None, None], moe_out, land(first, rest)[None, None]


def solution(mesh):
    placed = (
        P("inst", "ep", None, None),
        P("inst", "ep", None, None, None, None),
        P("inst", "ep", None),
        P("inst", "ep", None),
        P(("inst", "ep"), None),
        P(("inst", "ep"), None),
        P("ep", None, None),
        P("ep", None, None),
        P("ep", None, None),
    )
    return jax.shard_map(
        local,
        mesh=mesh,
        in_specs=placed,
        out_specs=(
            P("inst", "ep", None, None),
            P(("inst", "ep"), None),
            P("inst", "ep", None, None, None, None),
        ),
        check_vma=False,
    )
```

time: 153 us -> 123 us (0.80)
  the two profiles are of different devices: /device:TPU:1 before, /device:TPU:216 now
where the time goes in v3:
time: 123 us; the launch traced here: 122 us
  waiting for transfers between devices  68.5 us (56%)
  Pallas kernels  29.5 us (24%)
  starting transfers between devices  22 us (18%)
  local copies, waits for them, and re-layouts  1.71 us (1%)
    ppermute x15, waiting for transfers between devices, move(): return lax.ppermute(block, ('inst', 'ep'), route)  50.6 us
    ppermute x15, starting transfers between devices, move(): return lax.ppermute(block, ('inst', 'ep'), route)  19.4 us
    ppermute x2, waiting for transfers between devices, onward(): return lax.ppermute(block, 'inst', [(i, i + 8) for i in range(8)])  17.9 us
    pallas_call x4, Pallas kernels, experts(): pl.pallas_call(expert_kernel, out_shape=[jax.ShapeDtypeStruct((CAP, D), j...  13.4 us
    pallas_call x1, Pallas kernels, attend(): pl.pallas_call(attend_kernel, out_shape=jax.ShapeDtypeStruct((REQS, HEADS...  6.47 us
    pallas_call x1, Pallas kernels, pack(): pl.pallas_call(pack_kernel, out_shape=[jax.ShapeDtypeStruct((NX * CAP, TO...  4.55 us
    ppermute x2, starting transfers between devices, onward(): return lax.ppermute(block, 'inst', [(i, i + 8) for i in range(8)])  2.58 us
  transfers between devices with their start and end apart: 17, of which 12 were waited for; matrix products, arithmetic and copies ran while one was open for 0% of the time, Pallas kernels for 17%

profile of v3, /device:TPU:216, one launch (start us, length us, event | category | flops | bytes accessed | tf_op | source)
XLA Modules:
  0.0 122.5 jit_solution(12468330410541229899)
XLA Ops:
  0.7 4.5 %pack.1 = (bf16[256,128]{1,0:T(8,128)(2,1)S(1)}, bf16[64,4096]{1,0:T(8,128)(2,1)S(1)}, bf16[64,4096]{1,0:T(8,128)(2,1)S(1)}, bf16[64,4096]{1,0:T(8,128)(2,1)S(1)...) custom-call(s32[1,128]{1,0:T(1,128)} %bitcast.30, bf16[128,4096]{1,0:T(8,128)(2,1)} %hidden.1, ...), custom_call_target="tpu_custom_call" | custom-call | tf_op jit(solution)/shard_map/pack/pallas_call | solution.py:111
  5.2 0.1 collective-permute-start.1
  5.3 1.6 %collective-permute-start.6 = (bf16[64,4096]{1,0:T(8,128)(2,1)S(1)}, bf16[64,4096]{1,0:T(8,128)(2,1)S(1)}, u32[]{:S(2)}, u32[]{:S(2)}) collective-permute-start(bf16[64,4096]{1,0:T(8,128)(2,1)S(1)} %get-tuple-element.22), channel_id=1, source_target_pairs={{0,4},{1,5},{2,6},{3,7},{64,68},{65,69},{66,70},{67,71},{128,132},... | collective-permute-start | bytes 1572872 | tf_op jit(solution)/shard_map/ppermute | solution.py:46
  6.9 1.7 %collective-permute-start.3 = (bf16[64,4096]{1,0:T(8,128)(2,1)S(1)}, bf16[64,4096]{1,0:T(8,128)(2,1)S(1)}, u32[]{:S(2)}, u32[]{:S(2)}) collective-permute-start(bf16[64,4096]{1,0:T(8,128)(2,1)S(1)} %get-tuple-element.21), channel_id=1, source_target_pairs={{0,12},{1,13},{2,14},{3,15},{64,76},{65,77},{66,78},{67,79},{128,1... | collective-permute-start | bytes 1572872 | tf_op jit(solution)/shard_map/ppermute | solution.py:46
  8.7 0.6 leave.2
  9.2 1.3 %collective-permute-start.7 = (bf16[4,64,512]{2,1,0:T(8,128)(2,1)S(1)}, bf16[4,64,512]{2,1,0:T(8,128)(2,1)S(1)}, u32[]{:S(2)}, u32[]{:S(2)}) collective-permute-start(bf16[4,64,512]{2,1,0:T(8,128)(2,1)S(1)} %leave.2), channel_id=1, source_target_pairs={{0,128},{16,144},{32,160},{48,176},{64,192},{80,208},{96,224},{112... | collective-permute-start | bytes 786440 | tf_op jit(solution)/shard_map/ppermute | solution.py:179
  10.5 1.9 %collective-permute-start.2 = (bf16[64,4096]{1,0:T(8,128)(2,1)S(1)}, bf16[64,4096]{1,0:T(8,128)(2,1)S(1)}, u32[]{:S(2)}, u32[]{:S(2)}) collective-permute-start(bf16[64,4096]{1,0:T(8,128)(2,1)S(1)} %get-tuple-element.20), channel_id=1, source_target_pairs={{0,8},{1,9},{2,10},{3,11},{64,72},{65,73},{66,74},{67,75},{128,136... | collective-permute-start | bytes 1572872 | tf_op jit(solution)/shard_map/ppermute | solution.py:46
  12.5 6.5 %attend.1.refs_0_.refs_4_ = bf16[4,8192]{1,0:T(4,128)(2,1)} custom-call(s32[4]{0:T(128)S(1)} %bitcast.20, s32[16]{0:T(128)S(1)} %bitcast.23, bf16[4,64,128]{2,1,0:T(8,128)(2,1)S(1)} %bitcast.18, bf16[2,16,64,512]{3,2,1,0:T(8,128)(2,1)S(1)} %bitcast.15, bf16[256,128]{1,0:T(8,128)(2,1)S(1)} %get-tuple-element.17.refs_0_.onehot), custom_call_target="tpu_custom_call" | custom-call | bytes 12582912 | tf_op jit(solution)/shard_map/attend/pallas_call | solution.py:210
  18.9 9.8 %collective-permute-done.7.refs_1_.refs_0_ = bf16[4,64,512]{2,1,0:T(8,128)(2,1)S(1)} collective-permute-done((bf16[4,64,512]{2,1,0:T(8,128)(2,1)S(1)}, bf16[4,64,512]{2,1,0:T(8,128)(2,1)S(1)}, u32[]{:S(2)}, u32[]{:S(2)}) %collective-permute-start.7) | collective-permute-done | bytes 262176 | tf_op jit(solution)/shard_map/ppermute | solution.py:179
  28.8 0.0 collective-permute-done.6.block
  28.8 0.8 copy-done.1
  29.6 0.1 collective-permute-start.8
  29.7 1.7 %collective-permute-done.3.refs_0_ = bf16[64,4096]{1,0:T(8,128)(2,1)S(1)} collective-permute-done((bf16[64,4096]{1,0:T(8,128)(2,1)S(1)}, bf16[64,4096]{1,0:T(8,128)(2,1)S(1)}, u32[]{:S(2)}, u32[]{:S(2)}) %collective-permute-start.3) | collective-permute-done | bytes 524320 | tf_op jit(solution)/shard_map/ppermute | solution.py:46
  31.4 1.0 collective-permute-start.5
  32.4 0.7 collective-permute-done.2.block
  33.1 1.1 collective-permute-start.4
  34.2 4.7 %collective-permute-done.8.refs_1_ = bf16[64,4096]{1,0:T(8,128)(2,1)S(1)} collective-permute-done((bf16[64,4096]{1,0:T(8,128)(2,1)S(1)}, bf16[64,4096]{1,0:T(8,128)(2,1)S(1)}, u32[]{:S(2)}, u32[]{:S(2)}) %collective-permute-start.8) | collective-permute-done | bytes 524320 | tf_op jit(solution)/shard_map/ppermute | solution.py:46
  38.9 0.0 collective-permute-done.1.refs_3_
  38.9 0.8 copy-done.2
  39.7 3.3 %experts.4 = (bf16[64,4096]{1,0:T(8,128)(2,1)S(1)}, bf16[64,4096]{1,0:T(8,128)(2,1)S(1)}) custom-call(bf16[64,4096]{1,0:T(8,128)(2,1)S(1)} %hold.3.refs_0_, bf16[64,4096]{1,0:T(8,128)(2,1)S(1)} %collective-permute-done.8.refs_1_, bf16[36864,128]{1,0:T(8,128)(2,1)S(1)} %get-tuple-element.19.refs_2_, bf16[36864,128]{1,0:T(8,128)(2,1)S(1)} %collective-permute-done.1.refs_3_, ...), custom_call_target="tpu_custom_call" | custom-call | bytes 12582912 | tf_op jit(solution)/shard_map/experts/pallas_call | solution.py:282
  43.1 1.4 %collective-permute-done.5.refs_1_ = bf16[64,4096]{1,0:T(8,128)(2,1)S(1)} collective-permute-done((bf16[64,4096]{1,0:T(8,128)(2,1)S(1)}, bf16[64,4096]{1,0:T(8,128)(2,1)S(1)}, u32[]{:S(2)}, u32[]{:S(2)}) %collective-permute-start.5) | collective-permute-done | bytes 524320 | tf_op jit(solution)/shard_map/ppermute | solution.py:46
  44.5 3.3 %experts.5 = (bf16[64,4096]{1,0:T(8,128)(2,1)S(1)}, bf16[64,4096]{1,0:T(8,128)(2,1)S(1)}) custom-call(bf16[64,4096]{1,0:T(8,128)(2,1)S(1)} %collective-permute-done.3.refs_0_, bf16[64,4096]{1,0:T(8,128)(2,1)S(1)} %collective-permute-done.5.refs_1_, bf16[36864,128]{1,0:T(8,128)(2,1)S(1)} %get-tuple-element.19.refs_2_, ...), custom_call_target="tpu_custom_call" | custom-call | bytes 12582912 | tf_op jit(solution)/shard_map/experts/pallas_call | solution.py:282
  47.9 1.4 %collective-permute-start.10 = (bf16[64,4096]{1,0:T(8,128)(2,1)S(1)}, bf16[64,4096]{1,0:T(8,128)(2,1)S(1)}, u32[]{:S(2)}, u32[]{:S(2)}) collective-permute-start(bf16[64,4096]{1,0:T(8,128)(2,1)S(1)} %get-tuple-element.27), channel_id=1, source_target_pairs={{0,194},{1,3},{2,0},{3,65},{64,2},{65,67},{66,64},{67,129},{128,66... | collective-permute-start | bytes 1572872 | tf_op jit(solution)/shard_map/ppermute | solution.py:46
  49.2 0.1 collective-permute-start.9
  49.3 1.9 %collective-permute-start = (bf16[64,4096]{1,0:T(8,128)(2,1)S(1)}, bf16[64,4096]{1,0:T(8,128)(2,1)S(1)}, u32[]{:S(2)}, u32[]{:S(2)}) collective-permute-start(bf16[64,4096]{1,0:T(8,128)(2,1)S(1)} %get-tuple-element.18.refs_0_), channel_id=1, source_target_pairs={{0,2},{1,195},{2,64},{3,1},{64,66},{65,3},{66,128},{67,65},{128,13... | collective-permute-start | bytes 1572872 | tf_op jit(solution)/shard_map/ppermute | solution.py:46
  51.3 3.3 %experts.6 = (bf16[64,4096]{1,0:T(8,128)(2,1)S(1)}, bf16[64,4096]{1,0:T(8,128)(2,1)S(1)}) custom-call(bf16[64,4096]{1,0:T(8,128)(2,1)S(1)} %hold.2.refs_0_, bf16[64,4096]{1,0:T(8,128)(2,1)S(1)} %collective-permute-done.4.refs_1_, bf16[36864,128]{1,0:T(8,128)(2,1)S(1)} %get-tuple-element.19.refs_2_, bf16[36864,128]{1,0:T(8,128)(2,1)S(1)} %collective-permute-done.1.refs_3_, ...), custom_call_target="tpu_custom_call" | custom-call | bytes 12582912 | tf_op jit(solution)/shard_map/experts/pallas_call | solution.py:282
  54.6 5.8 %collective-permute-done.10.b = bf16[64,4096]{1,0:T(8,128)(2,1)S(1)} collective-permute-done((bf16[64,4096]{1,0:T(8,128)(2,1)S(1)}, bf16[64,4096]{1,0:T(8,128)(2,1)S(1)}, u32[]{:S(2)}, u32[]{:S(2)}) %collective-permute-start.10) | collective-permute-done | bytes 524320 | tf_op jit(solution)/shard_map/ppermute | solution.py:46
  60.4 0.1 add.5.refs_6_
  60.5 5.5 %collective-permute-done.9.b = bf16[64,4096]{1,0:T(8,128)(2,1)S(1)} collective-permute-done((bf16[64,4096]{1,0:T(8,128)(2,1)S(1)}, bf16[64,4096]{1,0:T(8,128)(2,1)S(1)}, u32[]{:S(2)}, u32[]{:S(2)}) %collective-permute-start.9) | collective-permute-done | bytes 524320 | tf_op jit(solution)/shard_map/ppermute | solution.py:46
  66.0 0.1 add.4.refs_5_
  66.1 0.0 collective-permute-done.refs_1_
  66.2 3.4 %experts.7 = (bf16[64,4096]{1,0:T(8,128)(2,1)S(1)}, bf16[64,4096]{1,0:T(8,128)(2,1)S(1)}) custom-call(bf16[64,4096]{1,0:T(8,128)(2,1)S(1)} %get-tuple-element.18.refs_0_, bf16[64,4096]{1,0:T(8,128)(2,1)S(1)} %collective-permute-done.refs_1_, bf16[36864,128]{1,0:T(8,128)(2,1)S(1)} %get-tuple-element.19.refs_2_, ...), custom_call_target="tpu_custom_call" | custom-call | bytes 12582912 | tf_op jit(solution)/shard_map/experts/pallas_call | solution.py:282
  69.5 1.7 %collective-permute-start.11 = (bf16[64,4096]{1,0:T(8,128)(2,1)S(1)}, bf16[64,4096]{1,0:T(8,128)(2,1)S(1)}, u32[]{:S(2)}, u32[]{:S(2)}) collective-permute-start(bf16[64,4096]{1,0:T(8,128)(2,1)S(1)} %get-tuple-element.29), channel_id=1, source_target_pairs={{0,194},{1,3},{2,0},{3,65},{64,2},{65,67},{66,64},{67,129},{128,66... | collective-permute-start | bytes 1572872 | tf_op jit(solution)/shard_map/ppermute | solution.py:46
  71.2 1.6 %collective-permute-start.13 = (bf16[64,4096]{1,0:T(8,128)(2,1)S(1)}, bf16[64,4096]{1,0:T(8,128)(2,1)S(1)}, u32[]{:S(2)}, u32[]{:S(2)}) collective-permute-start(bf16[64,4096]{1,0:T(8,128)(2,1)S(1)} %get-tuple-element.30), channel_id=1, source_target_pairs={{0,194},{1,3},{2,0},{3,65},{64,2},{65,67},{66,64},{67,129},{128,66... | collective-permute-start | bytes 1572872 | tf_op jit(solution)/shard_map/ppermute | solution.py:46
  72.9 5.9 %collective-permute-done.11.b.refs_0_ = bf16[64,4096]{1,0:T(8,128)(2,1)S(1)} collective-permute-done((bf16[64,4096]{1,0:T(8,128)(2,1)S(1)}, bf16[64,4096]{1,0:T(8,128)(2,1)S(1)}, u32[]{:S(2)}, u32[]{:S(2)}) %collective-permute-start.11) | collective-permute-done | bytes 524320 | tf_op jit(solution)/shard_map/ppermute | solution.py:46
  78.8 0.7 leave.3
  79.4 1.3 %collective-permute-start.16 = (bf16[12,64,512]{2,1,0:T(8,128)(2,1)S(1)}, bf16[12,64,512]{2,1,0:T(8,128)(2,1)S(1)}, u32[]{:S(2)}, u32[]{:S(2)}) collective-permute-start(bf16[12,64,512]{2,1,0:T(8,128)(2,1)S(1)} %leave.3), channel_id=1, source_target_pairs={{0,128},{16,144},{32,160},{48,176},{64,192},{80,208},{96,224},{112... | collective-permute-start | bytes 2359304 | tf_op jit(solution)/shard_map/ppermute | solution.py:179
  80.7 3.7 %collective-permute-done.13.b = bf16[64,4096]{1,0:T(8,128)(2,1)S(1)} collective-permute-done((bf16[64,4096]{1,0:T(8,128)(2,1)S(1)}, bf16[64,4096]{1,0:T(8,128)(2,1)S(1)}, u32[]{:S(2)}, u32[]{:S(2)}) %collective-permute-start.13) | collective-permute-done | bytes 524320 | tf_op jit(solution)/shard_map/ppermute | solution.py:46
  84.4 0.1 add.7
  84.5 1.9 %collective-permute-start.14 = (bf16[64,4096]{1,0:T(8,128)(2,1)S(1)}, bf16[64,4096]{1,0:T(8,128)(2,1)S(1)}, u32[]{:S(2)}, u32[]{:S(2)}) collective-permute-start(bf16[64,4096]{1,0:T(8,128)(2,1)S(1)} %add.7), channel_id=1, source_target_pairs={{0,8},{1,9},{2,10},{3,11},{64,72},{65,73},{66,74},{67,75},{128,136... | collective-permute-start | bytes 1572872 | tf_op jit(solution)/shard_map/ppermute | solution.py:46
  86.4 0.6 collective-permute-start.15
  87.0 2.6 %collective-permute-start.12 = (bf16[64,4096]{1,0:T(8,128)(2,1)S(1)}, bf16[64,4096]{1,0:T(8,128)(2,1)S(1)}, u32[]{:S(2)}, u32[]{:S(2)}) collective-permute-start(bf16[64,4096]{1,0:T(8,128)(2,1)S(1)} %add.4.refs_5_), channel_id=1, source_target_pairs={{0,12},{1,13},{2,14},{3,15},{64,76},{65,77},{66,78},{67,79},{128,1... | collective-permute-start | bytes 1572872 | tf_op jit(solution)/shard_map/ppermute | solution.py:46
  89.7 0.1 add.6.refs_0_
  89.8 11.2 %collective-permute-done.14.refs_2_ = bf16[64,4096]{1,0:T(8,128)(2,1)S(1)} collective-permute-done((bf16[64,4096]{1,0:T(8,128)(2,1)S(1)}, bf16[64,4096]{1,0:T(8,128)(2,1)S(1)}, u32[]{:S(2)}, u32[]{:S(2)}) %collective-permute-start.14) | collective-permute-done | bytes 524320 | tf_op jit(solution)/shard_map/ppermute | solution.py:46
  101.0 10.1 %collective-permute-done.15.refs_3_ = bf16[64,4096]{1,0:T(8,128)(2,1)S(1)} collective-permute-done((bf16[64,4096]{1,0:T(8,128)(2,1)S(1)}, bf16[64,4096]{1,0:T(8,128)(2,1)S(1)}, u32[]{:S(2)}, u32[]{:S(2)}) %collective-permute-start.15) | collective-permute-done | bytes 524320 | tf_op jit(solution)/shard_map/ppermute | solution.py:46
  111.1 2.3 %bring_home.1 = bf16[128,4096]{1,0:T(8,128)(2,1)} custom-call(bf16[256,128]{1,0:T(8,128)(2,1)S(1)} %get-tuple-element.17.refs_0_.onehot, bf16[64,4096]{1,0:T(8,128)(2,1)S(1)} %add.6.refs_0_, bf16[64,4096]{1,0:T(8,128)(2,1)S(1)} %collective-permute-done.12.refs_1_, bf16[64,4096]{1,0:T(8,128)(2,1)S(1)} %collective-permute-done.14.refs_2_, ...), custom_call_target="tpu_custom_call" | custom-call | tf_op jit(solution)/shard_map/bring_home/pallas_call | solution.py:328
  113.4 8.0 %collective-permute-done.16.refs_1_ = bf16[12,64,512]{2,1,0:T(8,128)(2,1)S(1)} collective-permute-done((bf16[12,64,512]{2,1,0:T(8,128)(2,1)S(1)}, bf16[12,64,512]{2,1,0:T(8,128)(2,1)S(1)}, u32[]{:S(2)}, u32[]{:S(2)}) %collective-permute-start.16) | collective-permute-done | bytes 786464 | tf_op jit(solution)/shard_map/ppermute | solution.py:179
  121.5 1.0 land.1
  (15 shorter events, 0.1 us)
Async XLA Ops:
  0.6 8.0 %copy-start = (bf16[1,1,2,16,64,512]{5,4,3,2,1,0:T(8,128)(2,1)S(1)}, bf16[1,1,2,16,64,512]{5,4,3,2,1,0:T(8,128)(2,1)}, u32[]{:S(2)}) copy-start(bf16[1,1,2,16,64,512]{5,4,3,2,1,0:T(8,128)(2,1)} %param.10) | copy-start | bytes 6291460
  0.6 8.0 %copy-start.3 = (s32[1,1,4]{2,1,0:T(1,128)S(1)}, s32[1,1,4]{2,1,0:T(1,128)}, u32[]{:S(2)}) copy-start(s32[1,1,4]{2,1,0:T(1,128)} %param.11) | copy-start | bytes 52
  0.7 8.0 %copy-start.4 = (s32[1,1,16]{2,1,0:T(1,128)S(1)}, s32[1,1,16]{2,1,0:T(1,128)}, u32[]{:S(2)}) copy-start(s32[1,1,16]{2,1,0:T(1,128)} %param.12) | copy-start | bytes 196
  0.7 11.8 %copy-start.5 = (bf16[1,1,4,8192]{3,2,1,0:T(4,128)(2,1)S(1)}, bf16[1,1,4,8192]{3,2,1,0:T(4,128)(2,1)}, u32[]{:S(2)}) copy-start(bf16[1,1,4,8192]{3,2,1,0:T(4,128)(2,1)} %param.9) | copy-start | bytes 196612
  5.2 33.7 %collective-permute-start.1 = (bf16[36864,128]{1,0:T(8,128)(2,1)S(1)}, bf16[36864,128]{1,0:T(8,128)(2,1)S(1)}, u32[]{:S(2)}, u32[]{:S(2)}) collective-permute-start(bf16[36864,128]{1,0:T(8,128)(2,1)S(1)} %get-tuple-element.19.refs_2_), channel_id=1, source_target_pairs={{0,1},{1,0},{2,3},{3,2},{64,65},{65,64},{66,67},{67,66},{128,129},... | collective-permute-start | bytes 28311560 | tf_op jit(solution)/shard_map/ppermute | solution.py:46
  5.3 23.4 %collective-permute-start.6 = (bf16[64,4096]{1,0:T(8,128)(2,1)S(1)}, bf16[64,4096]{1,0:T(8,128)(2,1)S(1)}, u32[]{:S(2)}, u32[]{:S(2)}) collective-permute-start(bf16[64,4096]{1,0:T(8,128)(2,1)S(1)} %get-tuple-element.22), channel_id=1, source_target_pairs={{0,4},{1,5},{2,6},{3,7},{64,68},{65,69},{66,70},{67,71},{128,132},... | collective-permute-start | bytes 1572872 | tf_op jit(solution)/shard_map/ppermute | solution.py:46
  6.9 24.5 %collective-permute-start.3 = (bf16[64,4096]{1,0:T(8,128)(2,1)S(1)}, bf16[64,4096]{1,0:T(8,128)(2,1)S(1)}, u32[]{:S(2)}, u32[]{:S(2)}) collective-permute-start(bf16[64,4096]{1,0:T(8,128)(2,1)S(1)} %get-tuple-element.21), channel_id=1, source_target_pairs={{0,12},{1,13},{2,14},{3,15},{64,76},{65,77},{66,78},{67,79},{128,1... | collective-permute-start | bytes 1572872 | tf_op jit(solution)/shard_map/ppermute | solution.py:46
  9.2 19.5 %collective-permute-start.7 = (bf16[4,64,512]{2,1,0:T(8,128)(2,1)S(1)}, bf16[4,64,512]{2,1,0:T(8,128)(2,1)S(1)}, u32[]{:S(2)}, u32[]{:S(2)}) collective-permute-start(bf16[4,64,512]{2,1,0:T(8,128)(2,1)S(1)} %leave.2), channel_id=1, source_target_pairs={{0,128},{16,144},{32,160},{48,176},{64,192},{80,208},{96,224},{112... | collective-permute-start | bytes 786440 | tf_op jit(solution)/shard_map/ppermute | solution.py:179
  10.5 22.6 %collective-permute-start.2 = (bf16[64,4096]{1,0:T(8,128)(2,1)S(1)}, bf16[64,4096]{1,0:T(8,128)(2,1)S(1)}, u32[]{:S(2)}, u32[]{:S(2)}) collective-permute-start(bf16[64,4096]{1,0:T(8,128)(2,1)S(1)} %get-tuple-element.20), channel_id=1, source_target_pairs={{0,8},{1,9},{2,10},{3,11},{64,72},{65,73},{66,74},{67,75},{128,136... | collective-permute-start | bytes 1572872 | tf_op jit(solution)/shard_map/ppermute | solution.py:46
  28.8 0.8 copy-start.1
  29.6 9.3 %collective-permute-start.8 = (bf16[64,4096]{1,0:T(8,128)(2,1)S(1)}, bf16[64,4096]{1,0:T(8,128)(2,1)S(1)}, u32[]{:S(2)}, u32[]{:S(2)}) collective-permute-start(bf16[64,4096]{1,0:T(8,128)(2,1)S(1)} %hold.3.refs_0_), channel_id=1, source_target_pairs={{0,2},{1,195},{2,64},{3,1},{64,66},{65,3},{66,128},{67,65},{128,13... | collective-permute-start | bytes 1572872 | tf_op jit(solution)/shard_map/ppermute | solution.py:46
  31.4 13.1 %collective-permute-start.5 = (bf16[64,4096]{1,0:T(8,128)(2,1)S(1)}, bf16[64,4096]{1,0:T(8,128)(2,1)S(1)}, u32[]{:S(2)}, u32[]{:S(2)}) collective-permute-start(bf16[64,4096]{1,0:T(8,128)(2,1)S(1)} %collective-permute-done.3.refs_0_), channel_id=1, source_target_pairs={{0,2},{1,195},{2,64},{3,1},{64,66},{65,3},{66,128},{67,65},{128,13... | collective-permute-start | bytes 1572872 | tf_op jit(solution)/shard_map/ppermute | solution.py:46
  33.1 18.1 %collective-permute-start.4 = (bf16[64,4096]{1,0:T(8,128)(2,1)S(1)}, bf16[64,4096]{1,0:T(8,128)(2,1)S(1)}, u32[]{:S(2)}, u32[]{:S(2)}) collective-permute-start(bf16[64,4096]{1,0:T(8,128)(2,1)S(1)} %hold.2.refs_0_), channel_id=1, source_target_pairs={{0,2},{1,195},{2,64},{3,1},{64,66},{65,3},{66,128},{67,65},{128,13... | collective-permute-start | bytes 1572872 | tf_op jit(solution)/shard_map/ppermute | solution.py:46
  38.9 0.8 copy-start.2
  47.9 12.5 %collective-permute-start.10 = (bf16[64,4096]{1,0:T(8,128)(2,1)S(1)}, bf16[64,4096]{1,0:T(8,128)(2,1)S(1)}, u32[]{:S(2)}, u32[]{:S(2)}) collective-permute-start(bf16[64,4096]{1,0:T(8,128)(2,1)S(1)} %get-tuple-element.27), channel_id=1, source_target_pairs={{0,194},{1,3},{2,0},{3,65},{64,2},{65,67},{66,64},{67,129},{128,66... | collective-permute-start | bytes 1572872 | tf_op jit(solution)/shard_map/ppermute | solution.py:46
  49.2 16.8 %collective-permute-start.9 = (bf16[64,4096]{1,0:T(8,128)(2,1)S(1)}, bf16[64,4096]{1,0:T(8,128)(2,1)S(1)}, u32[]{:S(2)}, u32[]{:S(2)}) collective-permute-start(bf16[64,4096]{1,0:T(8,128)(2,1)S(1)} %get-tuple-element.26), channel_id=1, source_target_pairs={{0,194},{1,3},{2,0},{3,65},{64,2},{65,67},{66,64},{67,129},{128,66... | collective-permute-start | bytes 1572872 | tf_op jit(solution)/shard_map/ppermute | solution.py:46
  49.3 16.8 %collective-permute-start = (bf16[64,4096]{1,0:T(8,128)(2,1)S(1)}, bf16[64,4096]{1,0:T(8,128)(2,1)S(1)}, u32[]{:S(2)}, u32[]{:S(2)}) collective-permute-start(bf16[64,4096]{1,0:T(8,128)(2,1)S(1)} %get-tuple-element.18.refs_0_), channel_id=1, source_target_pairs={{0,2},{1,195},{2,64},{3,1},{64,66},{65,3},{66,128},{67,65},{128,13... | collective-permute-start | bytes 1572872 | tf_op jit(solution)/shard_map/ppermute | solution.py:46
  69.5 9.3 %collective-permute-start.11 = (bf16[64,4096]{1,0:T(8,128)(2,1)S(1)}, bf16[64,4096]{1,0:T(8,128)(2,1)S(1)}, u32[]{:S(2)}, u32[]{:S(2)}) collective-permute-start(bf16[64,4096]{1,0:T(8,128)(2,1)S(1)} %get-tuple-element.29), channel_id=1, source_target_pairs={{0,194},{1,3},{2,0},{3,65},{64,2},{65,67},{66,64},{67,129},{128,66... | collective-permute-start | bytes 1572872 | tf_op jit(solution)/shard_map/ppermute | solution.py:46
  71.2 13.2 %collective-permute-start.13 = (bf16[64,4096]{1,0:T(8,128)(2,1)S(1)}, bf16[64,4096]{1,0:T(8,128)(2,1)S(1)}, u32[]{:S(2)}, u32[]{:S(2)}) collective-permute-start(bf16[64,4096]{1,0:T(8,128)(2,1)S(1)} %get-tuple-element.30), channel_id=1, source_target_pairs={{0,194},{1,3},{2,0},{3,65},{64,2},{65,67},{66,64},{67,129},{128,66... | collective-permute-start | bytes 1572872 | tf_op jit(solution)/shard_map/ppermute | solution.py:46
  79.4 42.0 %collective-permute-start.16 = (bf16[12,64,512]{2,1,0:T(8,128)(2,1)S(1)}, bf16[12,64,512]{2,1,0:T(8,128)(2,1)S(1)}, u32[]{:S(2)}, u32[]{:S(2)}) collective-permute-start(bf16[12,64,512]{2,1,0:T(8,128)(2,1)S(1)} %leave.3), channel_id=1, source_target_pairs={{0,128},{16,144},{32,160},{48,176},{64,192},{80,208},{96,224},{112... | collective-permute-start | bytes 2359304 | tf_op jit(solution)/shard_map/ppermute | solution.py:179
  84.5 16.4 %collective-permute-start.14 = (bf16[64,4096]{1,0:T(8,128)(2,1)S(1)}, bf16[64,4096]{1,0:T(8,128)(2,1)S(1)}, u32[]{:S(2)}, u32[]{:S(2)}) collective-permute-start(bf16[64,4096]{1,0:T(8,128)(2,1)S(1)} %add.7), channel_id=1, source_target_pairs={{0,8},{1,9},{2,10},{3,11},{64,72},{65,73},{66,74},{67,75},{128,136... | collective-permute-start | bytes 1572872 | tf_op jit(solution)/shard_map/ppermute | solution.py:46
  86.4 24.7 %collective-permute-start.15 = (bf16[64,4096]{1,0:T(8,128)(2,1)S(1)}, bf16[64,4096]{1,0:T(8,128)(2,1)S(1)}, u32[]{:S(2)}, u32[]{:S(2)}) collective-permute-start(bf16[64,4096]{1,0:T(8,128)(2,1)S(1)} %add.5.refs_6_), channel_id=1, source_target_pairs={{0,4},{1,5},{2,6},{3,7},{64,68},{65,69},{66,70},{67,71},{128,132},... | collective-permute-start | bytes 1572872 | tf_op jit(solution)/shard_map/ppermute | solution.py:46
  87.0 24.1 %collective-permute-start.12 = (bf16[64,4096]{1,0:T(8,128)(2,1)S(1)}, bf16[64,4096]{1,0:T(8,128)(2,1)S(1)}, u32[]{:S(2)}, u32[]{:S(2)}) collective-permute-start(bf16[64,4096]{1,0:T(8,128)(2,1)S(1)} %add.4.refs_5_), channel_id=1, source_target_pairs={{0,12},{1,13},{2,14},{3,15},{64,76},{65,77},{66,78},{67,79},{128,1... | collective-permute-start | bytes 1572872 | tf_op jit(solution)/shard_map/ppermute | solution.py:46

commit v4 on v3

--- a/solution.py
+++ b/solution.py
@@ -21,11 +21,12 @@
 FQ = 384
 NX, NY, NZ, NC = 4, 4, 8, 2
 KB, NB = 2048, 1024
-EARLY = 4
+EARLY = 12
 MIB = 1 << 20
 VMEM = pltpu.VMEM
 SMEM = pltpu.SMEM
 LANE = 128
+EXTRA = 16
 NO_COST = pl.CostEstimate(flops=0, bytes_accessed=0, transcendentals=0)
 ANYWHERE = [pl.BlockSpec(memory_space=pl.ANY)]
 
@@ -73,8 +74,34 @@
     return copies
 
 
+def place(routes, onehot):
+    x = lax.axis_index("ep") // 4
+    rel = jnp.bitwise_and(routes - x, NX - 1)
+    match = (rel == lax.broadcasted_iota(jnp.int32, (8, TOK), 0)).astype(jnp.float32)
+    earlier = lax.broadcasted_iota(jnp.int32, (TOK, TOK), 0) < lax.broadcasted_iota(
+        jnp.int32, (TOK, TOK), 1
+    )
+    rank = jnp.dot(
+        match.astype(jnp.bfloat16),
+        earlier.astype(jnp.float32).astype(jnp.bfloat16),
+        preferred_element_type=jnp.float32,
+    )
+    slot = jnp.sum(rank * match, axis=0, keepdims=True).astype(jnp.int32)
+    target = rel * CAP + slot
+    chosen = (lax.broadcasted_iota(jnp.int32, (NX * CAP, TOK), 0) == target).astype(jnp.float32)
+    onehot[...] = chosen.astype(jnp.bfloat16)
+
+
+def pick(onehot, tokens, pieces):
+    for d in range(NX):
+        pieces[d][...] = jnp.dot(
+            onehot[d * CAP : (d + 1) * CAP, :], tokens[...], preferred_element_type=jnp.float32
+        ).astype(jnp.bfloat16)
+
+
 def pack_kernel(routes, hidden, *refs):
-    weights, (onehot, *pieces, bundle), (tokens, named, sems) = refs[:3], refs[3:9], refs[9:]
+    weights, (onehot, *pieces, bundle, parcel), (named, sems) = refs[:3], refs[3:10], refs[10:]
+    tokens = parcel.at[:TOK, :]
     first = [(routes, named), (hidden, tokens)]
     copies = [
         pltpu.make_async_copy(src, dst, sems.at[i])
@@ -83,28 +110,35 @@
     for copy in copies:
         copy.start()
     copies[0].wait()
-    x = lax.axis_index("ep") // 4
-    rel = jnp.bitwise_and(named[...] - x, NX - 1)
-    match = (rel == lax.broadcasted_iota(jnp.int32, (8, TOK), 0)).astype(jnp.float32)
-    earlier = lax.broadcasted_iota(jnp.int32, (TOK, TOK), 0) < lax.broadcasted_iota(
-        jnp.int32, (TOK, TOK), 1
-    )
-    rank = jnp.dot(
-        match.astype(jnp.bfloat16),
-        earlier.astype(jnp.float32).astype(jnp.bfloat16),
-        preferred_element_type=jnp.float32,
-    )
-    slot = jnp.sum(rank * match, axis=0, keepdims=True).astype(jnp.int32)
-    target = rel * CAP + slot
-    chosen = (lax.broadcasted_iota(jnp.int32, (NX * CAP, TOK), 0) == target).astype(jnp.float32)
-    onehot[...] = chosen.astype(jnp.bfloat16)
+    parcel[TOK:, :LANE] = jnp.broadcast_to(
+        named[...].astype(jnp.float32), (EXTRA, TOK)
+    ).astype(jnp.bfloat16)
+    parcel[TOK:, LANE:] = jnp.zeros((EXTRA, D - LANE), jnp.bfloat16)
+    place(named[...], onehot)
     copies[1].wait()
-    for d in range(NX):
-        pieces[d][...] = jnp.dot(
-            onehot[d * CAP : (d + 1) * CAP, :], tokens[...], preferred_element_type=jnp.float32
-        ).astype(jnp.bfloat16)
+    pick(onehot, tokens, pieces)
     for copy in copies[2:]:
         copy.wait()
+
+
+def pack_other_kernel(parcel, *refs):
+    pieces, onehot = refs[-5:-1], refs[-1]
+    named = parcel[TOK:, :LANE].astype(jnp.float32)[:1].astype(jnp.int32)
+    place(named, onehot)
+    pick(onehot, parcel.at[:TOK, :], pieces)
+
+
+def pack_other(parcel, *deps):
+    return pl.pallas_call(
+        pack_other_kernel,
+        out_shape=[jax.ShapeDtypeStruct((CAP, D), jnp.bfloat16)] * NX,
+        in_specs=[pl.BlockSpec(memory_space=VMEM)] + ANYWHERE * len(deps),
+        out_specs=[pl.BlockSpec(memory_space=VMEM)] * NX,
+        scratch_shapes=[pltpu.VMEM((NX * CAP, TOK), jnp.bfloat16)],
+        compiler_params=pltpu.CompilerParams(vmem_limit_bytes=8 * MIB),
+        cost_estimate=NO_COST,
+        name="pack_other",
+    )(parcel, *deps)
 
 
 def pack(routes, hidden, gate, up, down):
@@ -112,11 +146,11 @@
         pack_kernel,
         out_shape=[jax.ShapeDtypeStruct((NX * CAP, TOK), jnp.bfloat16)]
         + [jax.ShapeDtypeStruct((CAP, D), jnp.bfloat16)] * NX
-        + [jax.ShapeDtypeStruct((9 * D, LANE), jnp.bfloat16)],
-        in_specs=[pl.BlockSpec(memory_space=pltpu.HBM)] * 5,
-        out_specs=[pl.BlockSpec(memory_space=VMEM)] * (2 + NX),
+        + [jax.ShapeDtypeStruct((9 * D, LANE), jnp.bfloat16)]
+        + [jax.ShapeDtypeStruct((TOK + EXTRA, D), jnp.bfloat16)],
+        in_specs=ANYWHERE * 5,
+        out_specs=[pl.BlockSpec(memory_space=VMEM)] * (3 + NX),
         scratch_shapes=[
-            pltpu.VMEM((TOK, D), jnp.bfloat16),
             pltpu.VMEM((1, TOK), jnp.int32),
             pltpu.SemaphoreType.DMA((2 + 6 + D // LANE,)),
         ],
@@ -154,24 +188,24 @@
 
 
 def land_kernel(*refs):
-    *blocks, out = refs
+    _, *blocks, out = refs
     row = 0
     for block in blocks:
         out[row : row + block.shape[0]] = block[...]
         row += block.shape[0]
 
 
-def land(*blocks):
+def land(dep, *blocks):
     rows = 2 * MAXP
     out = pl.pallas_call(
         land_kernel,
         out_shape=jax.ShapeDtypeStruct((rows, PAGE, KV_HEADS * HEAD_DIM), jnp.bfloat16),
-        in_specs=[pl.BlockSpec(memory_space=VMEM)] * len(blocks),
+        in_specs=ANYWHERE + [pl.BlockSpec(memory_space=VMEM)] * len(blocks),
         out_specs=pl.BlockSpec(memory_space=VMEM),
         compiler_params=pltpu.CompilerParams(vmem_limit_bytes=8 * MIB),
         cost_estimate=NO_COST,
         name="land",
-    )(*blocks)
+    )(dep, *blocks)
     return out.reshape(2, MAXP, PAGE, KV_HEADS * HEAD_DIM)
 
 
@@ -180,7 +214,8 @@
 
 
 def attend_kernel(ctx, order, queries, kv, *refs):
-    out = refs[-1]
+    out, token = refs[-2:]
+    token[...] = jnp.zeros_like(token)
     start = 0
     for r in range(REQS):
         length = ctx[r]
@@ -209,14 +244,17 @@
 def attend(ctx, order, queries, kv, *deps):
     return pl.pallas_call(
         attend_kernel,
-        out_shape=jax.ShapeDtypeStruct((REQS, HEADS * HEAD_DIM), jnp.bfloat16),
+        out_shape=[
+            jax.ShapeDtypeStruct((REQS, HEADS * HEAD_DIM), jnp.bfloat16),
+            jax.ShapeDtypeStruct((8, LANE), jnp.float32),
+        ],
         in_specs=[pl.BlockSpec(memory_space=SMEM)] * 2
         + [pl.BlockSpec(memory_space=VMEM)] * 2
         + ANYWHERE * len(deps),
-        out_specs=pl.BlockSpec(memory_space=VMEM),
+        out_specs=[pl.BlockSpec(memory_space=VMEM)] * 2,
         compiler_params=pltpu.CompilerParams(vmem_limit_bytes=8 * MIB),
         cost_estimate=pl.CostEstimate(
-            flops=0, bytes_accessed=12 * MIB, transcendentals=0
+            flops=8 * 10**9, bytes_accessed=12 * MIB, transcendentals=0
         ),
         name="attend",
     )(ctx, order, queries.reshape(REQS, HEADS, HEAD_DIM), kv, *deps)
@@ -314,7 +352,8 @@
 
 
 def home_kernel(onehot, *refs):
-    *pieces, out = refs
+    *pieces, out, token = refs
+    token[...] = jnp.zeros_like(token)
     out[...] = lax.dot_general(
         onehot[...],
         jnp.concatenate([p[...] for p in pieces], 0),
@@ -327,58 +366,67 @@
     nb = D // 4
     return pl.pallas_call(
         home_kernel,
-        out_shape=jax.ShapeDtypeStruct((TOK, D), jnp.bfloat16),
+        out_shape=[
+            jax.ShapeDtypeStruct((TOK, D), jnp.bfloat16),
+            jax.ShapeDtypeStruct((8, LANE), jnp.float32),
+        ],
         grid=(4,),
         in_specs=[pl.BlockSpec((NX * CAP, TOK), lambda i: (0, 0))]
         + [pl.BlockSpec((CAP, nb), lambda i: (0, i))] * NX,
-        out_specs=pl.BlockSpec((TOK, nb), lambda i: (0, i)),
+        out_specs=[
+            pl.BlockSpec((TOK, nb), lambda i: (0, i)),
+            pl.BlockSpec((8, LANE), lambda i: (0, 0)),
+        ],
         compiler_params=pltpu.CompilerParams(vmem_limit_bytes=8 * MIB),
         cost_estimate=NO_COST,
         name="bring_home",
     )(onehot, *pieces)
 
 
-def add_kernel(a, b, out):
-    out[...] = (a[...].astype(jnp.float32) + b[...].astype(jnp.float32)).astype(jnp.bfloat16)
-
-
-def add(a, b):
+def add_kernel(a, b, *refs):
+    refs[-1][...] = (a[...].astype(jnp.float32) + b[...].astype(jnp.float32)).astype(jnp.bfloat16)
+
+
+def add(a, b, *deps):
     return pl.pallas_call(
         add_kernel,
         out_shape=jax.ShapeDtypeStruct(a.shape, a.dtype),
-        in_specs=[pl.BlockSpec(memory_space=VMEM)] * 2,
+        in_specs=[pl.BlockSpec(memory_space=VMEM)] * 2 + ANYWHERE * len(deps),
         out_specs=pl.BlockSpec(memory_space=VMEM),
         compiler_params=pltpu.CompilerParams(vmem_limit_bytes=8 * MIB),
         cost_estimate=NO_COST,
         name="add",
-    )(a, b)
+    )(a, b, *deps)
 
 
 def local(queries, kv_cache, ctx_len, page_order, hidden_in, routes, w_gate, w_up, w_down):
     ctx, order, kv = ctx_len[0, 0], page_order[0, 0], kv_cache[0, 0]
     leaving = [(side, j) for side in range(2) for j in range(MAXP)]
-    onehot, *piece, bundle = pack(routes, hidden_in, w_gate[0], w_up[0], w_down[0])
+    onehot, *piece, bundle, parcel = pack(routes, hidden_in, w_gate[0], w_up[0], w_down[0])
     bundles = tuple(
         pltpu.with_memory_space_constraint(b, VMEM) for b in (bundle, other_core(bundle))
     )
-    first = onward(leave(leaving[:EARLY], ctx, order, kv, onehot))
-    attn_out = attend(ctx, order, queries[0, 0], kv, onehot)
+    attn_out, attended = attend(ctx, order, queries[0, 0], kv, onehot)
+    their_parcel = over_z(parcel)
+    piece[2] = hold(piece[2], their_parcel, attended)
     got = [piece[0]] + [over_x(piece[d], d) for d in (1, 2, 3)]
-    got[1] = hold(got[1], attn_out, first)
-    got[2] = hold(got[2], got[3])
-    across = [over_z(g) for g in got]
-    home = [None] * NX
-    whole = {}
-    kept = attn_out
-    for d in (1, 3, 2, 0):
-        deps = (kept,) if d else (kept, whole[1], whole[3])
-        kept, lent = experts((got[d], across[d]), bundles, *deps)
-        returned = back_over_z(lent)
-        whole[d] = add(kept, returned)
+    theirs = pack_other(their_parcel, attended, got[1], got[3])
+    first = onward(leave(leaving[:EARLY], ctx, order, kv, theirs[0]))
+    across = [theirs[0]] + [over_x(theirs[d], d) for d in (1, 2, 3)]
+    home, whole, kept = {}, {}, {}
+    deps = {1: (2,), 3: (1,), 0: (3,)}
+    for d in (2, 1, 3, 0):
+        need = [kept[i] for i in deps.get(d, ())]
+        if d == 1:
+            need += [first, across[3]]
+        if d == 0:
+            need += [whole[2]]
+        kept[d], lent = experts((got[d], across[d]), bundles, *need)
+        whole[d] = add(kept[d], back_over_z(lent))
         home[d] = over_x(whole[d], -d) if d else whole[d]
-    rest = onward(leave(leaving[EARLY:], ctx, order, kv, returned))
-    moe_out = bring_home(onehot, home)
-    return attn_out[None, None], moe_out, land(first, rest)[None, None]
+    rest = onward(leave(leaving[EARLY:], ctx, order, kv, first))
+    moe_out, finished = bring_home(onehot, [home[d] for d in range(NX)])
+    return attn_out[None, None], moe_out, land(finished, first, rest)[None, None]
 
 
 def solution(mesh):

time: 123 us -> 108 us (0.88)
  waiting for transfers between devices: 68.5 us -> 55.6 us
  starting transfers between devices: 22 us -> 19.4 us
  local copies, waits for them, and re-layouts: 1.71 us -> 0.03 us
    ppermute x15, waiting for transfers between devices: 50.6 us -> 43.9 us  [move(): return lax.ppermute(block, ('inst', 'ep'), route)]
    ppermute x2, waiting for transfers between devices: 17.9 us -> 11.7 us  [onward(): return lax.ppermute(block, 'inst', [(i, i + 8) for i in range(8)])]
    ppermute x15, starting transfers between devices: 19.4 us -> 16.8 us  [move(): return lax.ppermute(block, ('inst', 'ep'), route)]
    unnamed x13 -> x9, local copies, waits for them, and re-layouts: 1.71 us -> 0.03 us
    pallas_call x2 -> x3, Pallas kernels: 8.78 us -> 9.64 us  [the longest x1 6.47 us: attend(): pl.pallas_call(attend_kernel, out_shape=[jax.ShapeDtypeStruct((REQS, HEAD...]
  transfers between devices with their start and end apart: 17 -> 17, of which waited for: 12 -> 11; matrix products, arithmetic and copies ran while one was open for 0% -> 0% of each run, Pallas kernels for 17% -> 23%
where the time goes in v4:
time: 108 us; the launch traced here: 106 us
  waiting for transfers between devices  55.6 us (51%)
  Pallas kernels  30.4 us (28%)
  starting transfers between devices  19.4 us (18%)
    ppermute x15, waiting for transfers between devices, move(): return lax.ppermute(block, ('inst', 'ep'), route)  43.9 us
    ppermute x15, starting transfers between devices, move(): return lax.ppermute(block, ('inst', 'ep'), route)  16.8 us
    pallas_call x4, Pallas kernels, experts(): pl.pallas_call(expert_kernel, out_shape=[jax.ShapeDtypeStruct((CAP, D), j...  13.4 us
    ppermute x2, waiting for transfers between devices, onward(): return lax.ppermute(block, 'inst', [(i, i + 8) for i in range(8)])  11.7 us
    pallas_call x1, Pallas kernels, attend(): pl.pallas_call(attend_kernel, out_shape=[jax.ShapeDtypeStruct((REQS, HEAD...  6.47 us
    pallas_call x1, Pallas kernels, pack(): pl.pallas_call(pack_kernel, out_shape=[jax.ShapeDtypeStruct((NX * CAP, TO...  4.55 us
    ppermute x2, starting transfers between devices, onward(): return lax.ppermute(block, 'inst', [(i, i + 8) for i in range(8)])  2.58 us
    pallas_call x1, Pallas kernels, bring_home(): pl.pallas_call(home_kernel, out_shape=[jax.ShapeDtypeStruct((TOK, D), jnp...  2.32 us
  transfers between devices with their start and end apart: 17, of which 11 were waited for; matrix products, arithmetic and copies ran while one was open for 0% of the time, Pallas kernels for 23%

profile of v4, /device:TPU:216, one launch (start us, length us, event | category | flops | bytes accessed | tf_op | source)
XLA Modules:
  0.0 106.3 jit_solution(12196582148021382720)
XLA Ops:
  0.7 4.6 %pack.1 = (bf16[256,128]{1,0:T(8,128)(2,1)S(1)}, bf16[64,4096]{1,0:T(8,128)(2,1)S(1)}, bf16[64,4096]{1,0:T(8,128)(2,1)S(1)}, bf16[64,4096]{1,0:T(8,128)(2,1)S(1)...) custom-call(s32[1,128]{1,0:T(1,128)} %bitcast.29, ...), custom_call_target="tpu_custom_call" | custom-call | tf_op jit(solution)/shard_map/pack/pallas_call | solution.py:145
  5.2 0.1 collective-permute-start.3
  5.3 1.1 %collective-permute-start = (bf16[144,4096]{1,0:T(8,128)(2,1)S(1)}, bf16[144,4096]{1,0:T(8,128)(2,1)S(1)}, u32[]{:S(2)}, u32[]{:S(2)}) collective-permute-start(bf16[144,4096]{1,0:T(8,128)(2,1)S(1)} %get-tuple-element.29), channel_id=1, source_target_pairs={{0,2},{1,195},{2,64},{3,1},{64,66},{65,3},{66,128},{67,65},{128,13... | collective-permute-start | bytes 3538952 | tf_op jit(solution)/shard_map/ppermute | solution.py:47
  6.4 1.5 %collective-permute-start.1 = (bf16[64,4096]{1,0:T(8,128)(2,1)S(1)}, bf16[64,4096]{1,0:T(8,128)(2,1)S(1)}, u32[]{:S(2)}, u32[]{:S(2)}) collective-permute-start(bf16[64,4096]{1,0:T(8,128)(2,1)S(1)} %get-tuple-element.31), channel_id=1, source_target_pairs={{0,4},{1,5},{2,6},{3,7},{64,68},{65,69},{66,70},{67,71},{128,132},... | collective-permute-start | bytes 1572872 | tf_op jit(solution)/shard_map/ppermute | solution.py:47
  7.9 1.7 %collective-permute-start.2 = (bf16[64,4096]{1,0:T(8,128)(2,1)S(1)}, bf16[64,4096]{1,0:T(8,128)(2,1)S(1)}, u32[]{:S(2)}, u32[]{:S(2)}) collective-permute-start(bf16[64,4096]{1,0:T(8,128)(2,1)S(1)} %get-tuple-element.32), channel_id=1, source_target_pairs={{0,12},{1,13},{2,14},{3,15},{64,76},{65,77},{66,78},{67,79},{128,1... | collective-permute-start | bytes 1572872 | tf_op jit(solution)/shard_map/ppermute | solution.py:47
  9.7 6.5 %attend.1 = (bf16[4,8192]{1,0:T(4,128)(2,1)}, f32[8,128]{1,0:T(8,128)S(1)}) custom-call(s32[4]{0:T(128)S(1)} %bitcast.18, s32[16]{0:T(128)S(1)} %bitcast.21, bf16[4,64,128]{2,1,0:T(8,128)(2,1)S(1)} %bitcast.17, bf16[2,16,64,512]{3,2,1,0:T(8,128)(2,1)S(1)} %bitcast.14, bf16[256,128]{1,0:T(8,128)(2,1)S(1)} %get-tuple-element.26.refs_0_.onehot), custom_call_target="tpu_custom_call" | custom-call | flops 8000000000 | bytes 12582912 | tf_op jit(solution)/shard_map/attend/pallas_call | solution.py:245
  16.2 5.4 %collective-permute-done.parcel.refs_0_ = bf16[144,4096]{1,0:T(8,128)(2,1)S(1)} collective-permute-done((bf16[144,4096]{1,0:T(8,128)(2,1)S(1)}, bf16[144,4096]{1,0:T(8,128)(2,1)S(1)}, u32[]{:S(2)}, u32[]{:S(2)}) %collective-permute-start) | collective-permute-done | bytes 1179680 | tf_op jit(solution)/shard_map/ppermute | solution.py:47
  21.7 3.1 %collective-permute-start.6 = (bf16[64,4096]{1,0:T(8,128)(2,1)S(1)}, bf16[64,4096]{1,0:T(8,128)(2,1)S(1)}, u32[]{:S(2)}, u32[]{:S(2)}) collective-permute-start(bf16[64,4096]{1,0:T(8,128)(2,1)S(1)} %hold.1), channel_id=1, source_target_pairs={{0,8},{1,9},{2,10},{3,11},{64,72},{65,73},{66,74},{67,75},{128,136... | collective-permute-start | bytes 1572872 | tf_op jit(solution)/shard_map/ppermute | solution.py:47
  24.8 0.0 collective-permute-done.1.refs_1_.refs_0_
  24.8 0.0 collective-permute-done.2.refs_2_.refs_0_
  24.8 0.9 pack_other.1
  25.6 0.7 leave.2
  26.3 1.3 %collective-permute-start.8 = (bf16[12,64,512]{2,1,0:T(8,128)(2,1)S(1)}, bf16[12,64,512]{2,1,0:T(8,128)(2,1)S(1)}, u32[]{:S(2)}, u32[]{:S(2)}) collective-permute-start(bf16[12,64,512]{2,1,0:T(8,128)(2,1)S(1)} %leave.2), channel_id=1, source_target_pairs={{0,128},{16,144},{32,160},{48,176},{64,192},{80,208},{96,224},{112... | collective-permute-start | bytes 2359304 | tf_op jit(solution)/shard_map/ppermute | solution.py:213
  27.6 0.6 collective-permute-start.7
  28.2 2.8 %collective-permute-start.4 = (bf16[64,4096]{1,0:T(8,128)(2,1)S(1)}, bf16[64,4096]{1,0:T(8,128)(2,1)S(1)}, u32[]{:S(2)}, u32[]{:S(2)}) collective-permute-start(bf16[64,4096]{1,0:T(8,128)(2,1)S(1)} %get-tuple-element.35), channel_id=1, source_target_pairs={{0,12},{1,13},{2,14},{3,15},{64,76},{65,77},{66,78},{67,79},{128,1... | collective-permute-start | bytes 1572872 | tf_op jit(solution)/shard_map/ppermute | solution.py:47
  30.9 7.1 %collective-permute-done.6.refs_0_ = bf16[64,4096]{1,0:T(8,128)(2,1)S(1)} collective-permute-done((bf16[64,4096]{1,0:T(8,128)(2,1)S(1)}, bf16[64,4096]{1,0:T(8,128)(2,1)S(1)}, u32[]{:S(2)}, u32[]{:S(2)}) %collective-permute-start.6) | collective-permute-done | bytes 524320 | tf_op jit(solution)/shard_map/ppermute | solution.py:47
  38.1 1.6 %collective-permute-start.5 = (bf16[64,4096]{1,0:T(8,128)(2,1)S(1)}, bf16[64,4096]{1,0:T(8,128)(2,1)S(1)}, u32[]{:S(2)}, u32[]{:S(2)}) collective-permute-start(bf16[64,4096]{1,0:T(8,128)(2,1)S(1)} %get-tuple-element.36), channel_id=1, source_target_pairs={{0,4},{1,5},{2,6},{3,7},{64,68},{65,69},{66,70},{67,71},{128,132},... | collective-permute-start | bytes 1572872 | tf_op jit(solution)/shard_map/ppermute | solution.py:47
  39.7 9.7 %collective-permute-done.7.refs_1_ = bf16[64,4096]{1,0:T(8,128)(2,1)S(1)} collective-permute-done((bf16[64,4096]{1,0:T(8,128)(2,1)S(1)}, bf16[64,4096]{1,0:T(8,128)(2,1)S(1)}, u32[]{:S(2)}, u32[]{:S(2)}) %collective-permute-start.7) | collective-permute-done | bytes 524320 | tf_op jit(solution)/shard_map/ppermute | solution.py:47
  49.4 0.0 collective-permute-done.3.refs_3_
  49.4 3.4 %experts.4 = (bf16[64,4096]{1,0:T(8,128)(2,1)S(1)}, bf16[64,4096]{1,0:T(8,128)(2,1)S(1)}) custom-call(bf16[64,4096]{1,0:T(8,128)(2,1)S(1)} %collective-permute-done.6.refs_0_, bf16[64,4096]{1,0:T(8,128)(2,1)S(1)} %collective-permute-done.7.refs_1_, bf16[36864,128]{1,0:T(8,128)(2,1)S(1)} %get-tuple-element.34.refs_2_, ...), custom_call_target="tpu_custom_call" | custom-call | bytes 12582912 | tf_op jit(solution)/shard_map/experts/pallas_call | solution.py:320
  52.8 1.2 %collective-permute-start.9 = (bf16[64,4096]{1,0:T(8,128)(2,1)S(1)}, bf16[64,4096]{1,0:T(8,128)(2,1)S(1)}, u32[]{:S(2)}, u32[]{:S(2)}) collective-permute-start(bf16[64,4096]{1,0:T(8,128)(2,1)S(1)} %get-tuple-element.42), channel_id=1, source_target_pairs={{0,194},{1,3},{2,0},{3,65},{64,2},{65,67},{66,64},{67,129},{128,66... | collective-permute-start | bytes 1572872 | tf_op jit(solution)/shard_map/ppermute | solution.py:47
  54.0 5.2 %collective-permute-done.4.refs_6_.refs_1_ = bf16[64,4096]{1,0:T(8,128)(2,1)S(1)} collective-permute-done((bf16[64,4096]{1,0:T(8,128)(2,1)S(1)}, bf16[64,4096]{1,0:T(8,128)(2,1)S(1)}, u32[]{:S(2)}, u32[]{:S(2)}) %collective-permute-start.4) | collective-permute-done | bytes 524320 | tf_op jit(solution)/shard_map/ppermute | solution.py:47
  59.2 0.0 collective-permute-done.5.refs_1_
  59.2 9.5 %collective-permute-done.8.refs_5_.refs_0_.refs_1_ = bf16[12,64,512]{2,1,0:T(8,128)(2,1)S(1)} collective-permute-done((bf16[12,64,512]{2,1,0:T(8,128)(2,1)S(1)}, bf16[12,64,512]{2,1,0:T(8,128)(2,1)S(1)}, u32[]{:S(2)}, u32[]{:S(2)}) %collective-permute-start.8) | collective-permute-done | bytes 786464 | tf_op jit(solution)/shard_map/ppermute | solution.py:213
  68.8 3.3 %experts.5 = (bf16[64,4096]{1,0:T(8,128)(2,1)S(1)}, bf16[64,4096]{1,0:T(8,128)(2,1)S(1)}) custom-call(bf16[64,4096]{1,0:T(8,128)(2,1)S(1)} %collective-permute-done.1.refs_1_.refs_0_, bf16[64,4096]{1,0:T(8,128)(2,1)S(1)} %collective-permute-done.5.refs_1_, bf16[36864,128]{1,0:T(8,128)(2,1)S(1)} %get-tuple-element.34.refs_2_, ...), custom_call_target="tpu_custom_call" | custom-call | bytes 12582912 | tf_op jit(solution)/shard_map/experts/pallas_call | solution.py:320
  72.1 0.2 collective-permute-start.11
  72.3 3.4 %experts.6 = (bf16[64,4096]{1,0:T(8,128)(2,1)S(1)}, bf16[64,4096]{1,0:T(8,128)(2,1)S(1)}) custom-call(bf16[64,4096]{1,0:T(8,128)(2,1)S(1)} %collective-permute-done.2.refs_2_.refs_0_, bf16[64,4096]{1,0:T(8,128)(2,1)S(1)} %collective-permute-done.4.refs_6_.refs_1_, bf16[36864,128]{1,0:T(8,128)(2,1)S(1)} %get-tuple-element.34.refs_2_, ...), custom_call_target="tpu_custom_call" | custom-call | bytes 12582912 | tf_op jit(solution)/shard_map/experts/pallas_call | solution.py:320
  75.7 0.1 collective-permute-start.14
  75.8 0.1 add.4.refs_5_
  75.9 0.6 collective-permute-start.13
  76.5 3.4 %experts.7 = (bf16[64,4096]{1,0:T(8,128)(2,1)S(1)}, bf16[64,4096]{1,0:T(8,128)(2,1)S(1)}) custom-call(bf16[64,4096]{1,0:T(8,128)(2,1)S(1)} %get-tuple-element.28.refs_0_, bf16[64,4096]{1,0:T(8,128)(2,1)S(1)} %get-tuple-element.33.refs_0_.refs_1_, bf16[36864,128]{1,0:T(8,128)(2,1)S(1)} %get-tuple-element.34.refs_2_, ...), custom_call_target="tpu_custom_call" | custom-call | bytes 12582912 | tf_op jit(solution)/shard_map/experts/pallas_call | solution.py:320
  79.9 0.1 collective-permute-start.10
  80.0 1.4 %collective-permute-done.11.b = bf16[64,4096]{1,0:T(8,128)(2,1)S(1)} collective-permute-done((bf16[64,4096]{1,0:T(8,128)(2,1)S(1)}, bf16[64,4096]{1,0:T(8,128)(2,1)S(1)}, u32[]{:S(2)}, u32[]{:S(2)}) %collective-permute-start.11) | collective-permute-done | bytes 524320 | tf_op jit(solution)/shard_map/ppermute | solution.py:47
  81.4 0.1 add.6
  81.5 1.4 %collective-permute-start.12 = (bf16[64,4096]{1,0:T(8,128)(2,1)S(1)}, bf16[64,4096]{1,0:T(8,128)(2,1)S(1)}, u32[]{:S(2)}, u32[]{:S(2)}) collective-permute-start(bf16[64,4096]{1,0:T(8,128)(2,1)S(1)} %add.6), channel_id=1, source_target_pairs={{0,12},{1,13},{2,14},{3,15},{64,76},{65,77},{66,78},{67,79},{128,1... | collective-permute-start | bytes 1572872 | tf_op jit(solution)/shard_map/ppermute | solution.py:47
  82.9 4.1 %collective-permute-done.14.b = bf16[64,4096]{1,0:T(8,128)(2,1)S(1)} collective-permute-done((bf16[64,4096]{1,0:T(8,128)(2,1)S(1)}, bf16[64,4096]{1,0:T(8,128)(2,1)S(1)}, u32[]{:S(2)}, u32[]{:S(2)}) %collective-permute-start.14) | collective-permute-done | bytes 524320 | tf_op jit(solution)/shard_map/ppermute | solution.py:47
  87.0 0.1 add.7
  87.1 0.7 collective-permute-start.15
  87.8 0.6 leave.3
  88.4 1.3 %collective-permute-start.16 = (bf16[4,64,512]{2,1,0:T(8,128)(2,1)S(1)}, bf16[4,64,512]{2,1,0:T(8,128)(2,1)S(1)}, u32[]{:S(2)}, u32[]{:S(2)}) collective-permute-start(bf16[4,64,512]{2,1,0:T(8,128)(2,1)S(1)} %leave.3), channel_id=1, source_target_pairs={{0,128},{16,144},{32,160},{48,176},{64,192},{80,208},{96,224},{112... | collective-permute-start | bytes 786440 | tf_op jit(solution)/shard_map/ppermute | solution.py:213
  89.7 2.9 %collective-permute-done.10.b = bf16[64,4096]{1,0:T(8,128)(2,1)S(1)} collective-permute-done((bf16[64,4096]{1,0:T(8,128)(2,1)S(1)}, bf16[64,4096]{1,0:T(8,128)(2,1)S(1)}, u32[]{:S(2)}, u32[]{:S(2)}) %collective-permute-start.10) | collective-permute-done | bytes 524320 | tf_op jit(solution)/shard_map/ppermute | solution.py:47
  92.6 0.1 add.5.refs_0_
  92.7 6.2 %collective-permute-done.12.refs_1_ = bf16[64,4096]{1,0:T(8,128)(2,1)S(1)} collective-permute-done((bf16[64,4096]{1,0:T(8,128)(2,1)S(1)}, bf16[64,4096]{1,0:T(8,128)(2,1)S(1)}, u32[]{:S(2)}, u32[]{:S(2)}) %collective-permute-start.12) | collective-permute-done | bytes 524320 | tf_op jit(solution)/shard_map/ppermute | solution.py:47
  99.0 0.0 collective-permute-done.13.refs_2_
  99.0 1.8 %collective-permute-done.15.refs_3_ = bf16[64,4096]{1,0:T(8,128)(2,1)S(1)} collective-permute-done((bf16[64,4096]{1,0:T(8,128)(2,1)S(1)}, bf16[64,4096]{1,0:T(8,128)(2,1)S(1)}, u32[]{:S(2)}, u32[]{:S(2)}) %collective-permute-start.15) | collective-permute-done | bytes 524320 | tf_op jit(solution)/shard_map/ppermute | solution.py:47
  100.7 2.3 %bring_home.1 = (bf16[128,4096]{1,0:T(8,128)(2,1)}, f32[8,128]{1,0:T(8,128)S(1)}) custom-call(bf16[256,128]{1,0:T(8,128)(2,1)S(1)} %get-tuple-element.26.refs_0_.onehot, bf16[64,4096]{1,0:T(8,128)(2,1)S(1)} %add.5.refs_0_, bf16[64,4096]{1,0:T(8,128)(2,1)S(1)} %collective-permute-done.12.refs_1_, bf16[64,4096]{1,0:T(8,128)(2,1)S(1)} %collective-permute-done.13.refs_2_, ...), custom_call_target="tpu_custom_call" | custom-call | tf_op jit(solution)/shard_map/bring_home/pallas_call | solution.py:367
  103.1 2.2 %collective-permute-done.16.refs_2_ = bf16[4,64,512]{2,1,0:T(8,128)(2,1)S(1)} collective-permute-done((bf16[4,64,512]{2,1,0:T(8,128)(2,1)S(1)}, bf16[4,64,512]{2,1,0:T(8,128)(2,1)S(1)}, u32[]{:S(2)}, u32[]{:S(2)}) %collective-permute-start.16) | collective-permute-done | bytes 262176 | tf_op jit(solution)/shard_map/ppermute | solution.py:213
  105.2 1.0 land.1
  (11 shorter events, 0.1 us)
Async XLA Ops:
  0.6 9.0 %copy-start.3 = (bf16[1,1,4,8192]{3,2,1,0:T(4,128)(2,1)S(1)}, bf16[1,1,4,8192]{3,2,1,0:T(4,128)(2,1)}, u32[]{:S(2)}) copy-start(bf16[1,1,4,8192]{3,2,1,0:T(4,128)(2,1)} %param.9) | copy-start | bytes 196612
  0.6 9.0 %copy-start = (bf16[1,1,2,16,64,512]{5,4,3,2,1,0:T(8,128)(2,1)S(1)}, bf16[1,1,2,16,64,512]{5,4,3,2,1,0:T(8,128)(2,1)}, u32[]{:S(2)}) copy-start(bf16[1,1,2,16,64,512]{5,4,3,2,1,0:T(8,128)(2,1)} %param.10) | copy-start | bytes 6291460
  0.7 9.0 %copy-start.1 = (s32[1,1,4]{2,1,0:T(1,128)S(1)}, s32[1,1,4]{2,1,0:T(1,128)}, u32[]{:S(2)}) copy-start(s32[1,1,4]{2,1,0:T(1,128)} %param.11) | copy-start | bytes 52
  0.7 9.0 %copy-start.2 = (s32[1,1,16]{2,1,0:T(1,128)S(1)}, s32[1,1,16]{2,1,0:T(1,128)}, u32[]{:S(2)}) copy-start(s32[1,1,16]{2,1,0:T(1,128)} %param.12) | copy-start | bytes 196
  5.2 44.1 %collective-permute-start.3 = (bf16[36864,128]{1,0:T(8,128)(2,1)S(1)}, bf16[36864,128]{1,0:T(8,128)(2,1)S(1)}, u32[]{:S(2)}, u32[]{:S(2)}) collective-permute-start(bf16[36864,128]{1,0:T(8,128)(2,1)S(1)} %get-tuple-element.34.refs_2_), channel_id=1, source_target_pairs={{0,1},{1,0},{2,3},{3,2},{64,65},{65,64},{66,67},{67,66},{128,129},... | collective-permute-start | bytes 28311560 | tf_op jit(solution)/shard_map/ppermute | solution.py:47
  5.3 16.3 %collective-permute-start = (bf16[144,4096]{1,0:T(8,128)(2,1)S(1)}, bf16[144,4096]{1,0:T(8,128)(2,1)S(1)}, u32[]{:S(2)}, u32[]{:S(2)}) collective-permute-start(bf16[144,4096]{1,0:T(8,128)(2,1)S(1)} %get-tuple-element.29), channel_id=1, source_target_pairs={{0,2},{1,195},{2,64},{3,1},{64,66},{65,3},{66,128},{67,65},{128,13... | collective-permute-start | bytes 3538952 | tf_op jit(solution)/shard_map/ppermute | solution.py:47
  6.4 18.3 %collective-permute-start.1 = (bf16[64,4096]{1,0:T(8,128)(2,1)S(1)}, bf16[64,4096]{1,0:T(8,128)(2,1)S(1)}, u32[]{:S(2)}, u32[]{:S(2)}) collective-permute-start(bf16[64,4096]{1,0:T(8,128)(2,1)S(1)} %get-tuple-element.31), channel_id=1, source_target_pairs={{0,4},{1,5},{2,6},{3,7},{64,68},{65,69},{66,70},{67,71},{128,132},... | collective-permute-start | bytes 1572872 | tf_op jit(solution)/shard_map/ppermute | solution.py:47
  7.9 16.8 %collective-permute-start.2 = (bf16[64,4096]{1,0:T(8,128)(2,1)S(1)}, bf16[64,4096]{1,0:T(8,128)(2,1)S(1)}, u32[]{:S(2)}, u32[]{:S(2)}) collective-permute-start(bf16[64,4096]{1,0:T(8,128)(2,1)S(1)} %get-tuple-element.32), channel_id=1, source_target_pairs={{0,12},{1,13},{2,14},{3,15},{64,76},{65,77},{66,78},{67,79},{128,1... | collective-permute-start | bytes 1572872 | tf_op jit(solution)/shard_map/ppermute | solution.py:47
  21.7 16.4 %collective-permute-start.6 = (bf16[64,4096]{1,0:T(8,128)(2,1)S(1)}, bf16[64,4096]{1,0:T(8,128)(2,1)S(1)}, u32[]{:S(2)}, u32[]{:S(2)}) collective-permute-start(bf16[64,4096]{1,0:T(8,128)(2,1)S(1)} %hold.1), channel_id=1, source_target_pairs={{0,8},{1,9},{2,10},{3,11},{64,72},{65,73},{66,74},{67,75},{128,136... | collective-permute-start | bytes 1572872 | tf_op jit(solution)/shard_map/ppermute | solution.py:47
  26.3 42.5 %collective-permute-start.8 = (bf16[12,64,512]{2,1,0:T(8,128)(2,1)S(1)}, bf16[12,64,512]{2,1,0:T(8,128)(2,1)S(1)}, u32[]{:S(2)}, u32[]{:S(2)}) collective-permute-start(bf16[12,64,512]{2,1,0:T(8,128)(2,1)S(1)} %leave.2), channel_id=1, source_target_pairs={{0,128},{16,144},{32,160},{48,176},{64,192},{80,208},{96,224},{112... | collective-permute-start | bytes 2359304 | tf_op jit(solution)/shard_map/ppermute | solution.py:213
  27.6 21.8 %collective-permute-start.7 = (bf16[64,4096]{1,0:T(8,128)(2,1)S(1)}, bf16[64,4096]{1,0:T(8,128)(2,1)S(1)}, u32[]{:S(2)}, u32[]{:S(2)}) collective-permute-start(bf16[64,4096]{1,0:T(8,128)(2,1)S(1)} %get-tuple-element.38), channel_id=1, source_target_pairs={{0,8},{1,9},{2,10},{3,11},{64,72},{65,73},{66,74},{67,75},{128,136... | collective-permute-start | bytes 1572872 | tf_op jit(solution)/shard_map/ppermute | solution.py:47
  28.2 31.0 %collective-permute-start.4 = (bf16[64,4096]{1,0:T(8,128)(2,1)S(1)}, bf16[64,4096]{1,0:T(8,128)(2,1)S(1)}, u32[]{:S(2)}, u32[]{:S(2)}) collective-permute-start(bf16[64,4096]{1,0:T(8,128)(2,1)S(1)} %get-tuple-element.35), channel_id=1, source_target_pairs={{0,12},{1,13},{2,14},{3,15},{64,76},{65,77},{66,78},{67,79},{128,1... | collective-permute-start | bytes 1572872 | tf_op jit(solution)/shard_map/ppermute | solution.py:47
  38.1 21.1 %collective-permute-start.5 = (bf16[64,4096]{1,0:T(8,128)(2,1)S(1)}, bf16[64,4096]{1,0:T(8,128)(2,1)S(1)}, u32[]{:S(2)}, u32[]{:S(2)}) collective-permute-start(bf16[64,4096]{1,0:T(8,128)(2,1)S(1)} %get-tuple-element.36), channel_id=1, source_target_pairs={{0,4},{1,5},{2,6},{3,7},{64,68},{65,69},{66,70},{67,71},{128,132},... | collective-permute-start | bytes 1572872 | tf_op jit(solution)/shard_map/ppermute | solution.py:47
  52.8 23.0 %collective-permute-start.9 = (bf16[64,4096]{1,0:T(8,128)(2,1)S(1)}, bf16[64,4096]{1,0:T(8,128)(2,1)S(1)}, u32[]{:S(2)}, u32[]{:S(2)}) collective-permute-start(bf16[64,4096]{1,0:T(8,128)(2,1)S(1)} %get-tuple-element.42), channel_id=1, source_target_pairs={{0,194},{1,3},{2,0},{3,65},{64,2},{65,67},{66,64},{67,129},{128,66... | collective-permute-start | bytes 1572872 | tf_op jit(solution)/shard_map/ppermute | solution.py:47
  72.1 9.3 %collective-permute-start.11 = (bf16[64,4096]{1,0:T(8,128)(2,1)S(1)}, bf16[64,4096]{1,0:T(8,128)(2,1)S(1)}, u32[]{:S(2)}, u32[]{:S(2)}) collective-permute-start(bf16[64,4096]{1,0:T(8,128)(2,1)S(1)} %get-tuple-element.45), channel_id=1, source_target_pairs={{0,194},{1,3},{2,0},{3,65},{64,2},{65,67},{66,64},{67,129},{128,66... | collective-permute-start | bytes 1572872 | tf_op jit(solution)/shard_map/ppermute | solution.py:47
  75.7 11.3 %collective-permute-start.14 = (bf16[64,4096]{1,0:T(8,128)(2,1)S(1)}, bf16[64,4096]{1,0:T(8,128)(2,1)S(1)}, u32[]{:S(2)}, u32[]{:S(2)}) collective-permute-start(bf16[64,4096]{1,0:T(8,128)(2,1)S(1)} %get-tuple-element.46), channel_id=1, source_target_pairs={{0,194},{1,3},{2,0},{3,65},{64,2},{65,67},{66,64},{67,129},{128,66... | collective-permute-start | bytes 1572872 | tf_op jit(solution)/shard_map/ppermute | solution.py:47
  75.9 23.1 %collective-permute-start.13 = (bf16[64,4096]{1,0:T(8,128)(2,1)S(1)}, bf16[64,4096]{1,0:T(8,128)(2,1)S(1)}, u32[]{:S(2)}, u32[]{:S(2)}) collective-permute-start(bf16[64,4096]{1,0:T(8,128)(2,1)S(1)} %add.4.refs_5_), channel_id=1, source_target_pairs={{0,8},{1,9},{2,10},{3,11},{64,72},{65,73},{66,74},{67,75},{128,136... | collective-permute-start | bytes 1572872 | tf_op jit(solution)/shard_map/ppermute | solution.py:47
  79.9 12.8 %collective-permute-start.10 = (bf16[64,4096]{1,0:T(8,128)(2,1)S(1)}, bf16[64,4096]{1,0:T(8,128)(2,1)S(1)}, u32[]{:S(2)}, u32[]{:S(2)}) collective-permute-start(bf16[64,4096]{1,0:T(8,128)(2,1)S(1)} %get-tuple-element.44), channel_id=1, source_target_pairs={{0,194},{1,3},{2,0},{3,65},{64,2},{65,67},{66,64},{67,129},{128,66... | collective-permute-start | bytes 1572872 | tf_op jit(solution)/shard_map/ppermute | solution.py:47
  81.5 17.5 %collective-permute-start.12 = (bf16[64,4096]{1,0:T(8,128)(2,1)S(1)}, bf16[64,4096]{1,0:T(8,128)(2,1)S(1)}, u32[]{:S(2)}, u32[]{:S(2)}) collective-permute-start(bf16[64,4096]{1,0:T(8,128)(2,1)S(1)} %add.6), channel_id=1, source_target_pairs={{0,12},{1,13},{2,14},{3,15},{64,76},{65,77},{66,78},{67,79},{128,1... | collective-permute-start | bytes 1572872 | tf_op jit(solution)/shard_map/ppermute | solution.py:47
  87.1 13.6 %collective-permute-start.15 = (bf16[64,4096]{1,0:T(8,128)(2,1)S(1)}, bf16[64,4096]{1,0:T(8,128)(2,1)S(1)}, u32[]{:S(2)}, u32[]{:S(2)}) collective-permute-start(bf16[64,4096]{1,0:T(8,128)(2,1)S(1)} %add.7), channel_id=1, source_target_pairs={{0,4},{1,5},{2,6},{3,7},{64,68},{65,69},{66,70},{67,71},{128,132},... | collective-permute-start | bytes 1572872 | tf_op jit(solution)/shard_map/ppermute | solution.py:47
  88.4 16.8 %collective-permute-start.16 = (bf16[4,64,512]{2,1,0:T(8,128)(2,1)S(1)}, bf16[4,64,512]{2,1,0:T(8,128)(2,1)S(1)}, u32[]{:S(2)}, u32[]{:S(2)}) collective-permute-start(bf16[4,64,512]{2,1,0:T(8,128)(2,1)S(1)} %leave.3), channel_id=1, source_target_pairs={{0,128},{16,144},{32,160},{48,176},{64,192},{80,208},{96,224},{112... | collective-permute-start | bytes 786440 | tf_op jit(solution)/shard_map/ppermute | solution.py:213

commit v5 on v4

--- a/solution.py
+++ b/solution.py
@@ -408,8 +408,9 @@
     )
     attn_out, attended = attend(ctx, order, queries[0, 0], kv, onehot)
     their_parcel = over_z(parcel)
-    piece[2] = hold(piece[2], their_parcel, attended)
-    got = [piece[0]] + [over_x(piece[d], d) for d in (1, 2, 3)]
+    got = [piece[0], over_x(piece[1], 1), None, over_x(piece[3], 3)]
+    piece[2] = hold(piece[2], got[1], got[3], attended)
+    got[2] = over_x(piece[2], 2)
     theirs = pack_other(their_parcel, attended, got[1], got[3])
     first = onward(leave(leaving[:EARLY], ctx, order, kv, theirs[0]))
     across = [theirs[0]] + [over_x(theirs[d], d) for d in (1, 2, 3)]

time: 108 us -> 106 us (0.981)
  waiting for transfers between devices: 55.6 us -> 50.6 us
  starting transfers between devices: 19.4 us -> 23.4 us
    ppermute x15, starting transfers between devices: 16.8 us -> 20.8 us  [move(): return lax.ppermute(block, ('inst', 'ep'), route)]
    ppermute x15, waiting for transfers between devices: 43.9 us -> 41 us  [move(): return lax.ppermute(block, ('inst', 'ep'), route)]
    ppermute x2, waiting for transfers between devices: 11.7 us -> 9.54 us  [onward(): return lax.ppermute(block, 'inst', [(i, i + 8) for i in range(8)])]
  transfers between devices with their start and end apart: 17 -> 17, of which waited for: 11 -> 10; matrix products, arithmetic and copies ran while one was open for 0% -> 0% of each run, Pallas kernels for 23% -> 24%
where the time goes in v5:
time: 106 us; the launch traced here: 105 us
  waiting for transfers between devices  50.6 us (48%)
  Pallas kernels  30.4 us (29%)
  starting transfers between devices  23.4 us (22%)
    ppermute x15, waiting for transfers between devices, move(): return lax.ppermute(block, ('inst', 'ep'), route)  41 us
    ppermute x15, starting transfers between devices, move(): return lax.ppermute(block, ('inst', 'ep'), route)  20.8 us
    pallas_call x4, Pallas kernels, experts(): pl.pallas_call(expert_kernel, out_shape=[jax.ShapeDtypeStruct((CAP, D), j...  13.4 us
    ppermute x2, waiting for transfers between devices, onward(): return lax.ppermute(block, 'inst', [(i, i + 8) for i in range(8)])  9.54 us
    pallas_call x1, Pallas kernels, attend(): pl.pallas_call(attend_kernel, out_shape=[jax.ShapeDtypeStruct((REQS, HEAD...  6.47 us
    pallas_call x1, Pallas kernels, pack(): pl.pallas_call(pack_kernel, out_shape=[jax.ShapeDtypeStruct((NX * CAP, TO...  4.55 us
    ppermute x2, starting transfers between devices, onward(): return lax.ppermute(block, 'inst', [(i, i + 8) for i in range(8)])  2.58 us
    pallas_call x1, Pallas kernels, bring_home(): pl.pallas_call(home_kernel, out_shape=[jax.ShapeDtypeStruct((TOK, D), jnp...  2.32 us
  transfers between devices with their start and end apart: 17, of which 10 were waited for; matrix products, arithmetic and copies ran while one was open for 0% of the time, Pallas kernels for 24%

profile of v5, /device:TPU:216, one launch (start us, length us, event | category | flops | bytes accessed | tf_op | source)
XLA Modules:
  0.0 105.3 jit_solution(13618317762377032586)
XLA Ops:
  0.7 4.6 %pack.1 = (bf16[256,128]{1,0:T(8,128)(2,1)S(1)}, bf16[64,4096]{1,0:T(8,128)(2,1)S(1)}, bf16[64,4096]{1,0:T(8,128)(2,1)S(1)}, bf16[64,4096]{1,0:T(8,128)(2,1)S(1)...) custom-call(s32[1,128]{1,0:T(1,128)} %bitcast.29, ...), custom_call_target="tpu_custom_call" | custom-call | tf_op jit(solution)/shard_map/pack/pallas_call | solution.py:145
  5.2 0.1 collective-permute-start.3
  5.3 1.1 %collective-permute-start = (bf16[144,4096]{1,0:T(8,128)(2,1)S(1)}, bf16[144,4096]{1,0:T(8,128)(2,1)S(1)}, u32[]{:S(2)}, u32[]{:S(2)}) collective-permute-start(bf16[144,4096]{1,0:T(8,128)(2,1)S(1)} %get-tuple-element.29), channel_id=1, source_target_pairs={{0,2},{1,195},{2,64},{3,1},{64,66},{65,3},{66,128},{67,65},{128,13... | collective-permute-start | bytes 3538952 | tf_op jit(solution)/shard_map/ppermute | solution.py:47
  6.4 1.5 %collective-permute-start.1 = (bf16[64,4096]{1,0:T(8,128)(2,1)S(1)}, bf16[64,4096]{1,0:T(8,128)(2,1)S(1)}, u32[]{:S(2)}, u32[]{:S(2)}) collective-permute-start(bf16[64,4096]{1,0:T(8,128)(2,1)S(1)} %get-tuple-element.31), channel_id=1, source_target_pairs={{0,4},{1,5},{2,6},{3,7},{64,68},{65,69},{66,70},{67,71},{128,132},... | collective-permute-start | bytes 1572872 | tf_op jit(solution)/shard_map/ppermute | solution.py:47
  7.9 1.7 %collective-permute-start.2 = (bf16[64,4096]{1,0:T(8,128)(2,1)S(1)}, bf16[64,4096]{1,0:T(8,128)(2,1)S(1)}, u32[]{:S(2)}, u32[]{:S(2)}) collective-permute-start(bf16[64,4096]{1,0:T(8,128)(2,1)S(1)} %get-tuple-element.32), channel_id=1, source_target_pairs={{0,12},{1,13},{2,14},{3,15},{64,76},{65,77},{66,78},{67,79},{128,1... | collective-permute-start | bytes 1572872 | tf_op jit(solution)/shard_map/ppermute | solution.py:47
  9.7 6.5 %attend.1 = (bf16[4,8192]{1,0:T(4,128)(2,1)}, f32[8,128]{1,0:T(8,128)S(1)}) custom-call(s32[4]{0:T(128)S(1)} %bitcast.18, s32[16]{0:T(128)S(1)} %bitcast.21, bf16[4,64,128]{2,1,0:T(8,128)(2,1)S(1)} %bitcast.17, bf16[2,16,64,512]{3,2,1,0:T(8,128)(2,1)S(1)} %bitcast.14, bf16[256,128]{1,0:T(8,128)(2,1)S(1)} %get-tuple-element.26.refs_0_.onehot), custom_call_target="tpu_custom_call" | custom-call | flops 8000000000 | bytes 12582912 | tf_op jit(solution)/shard_map/attend/pallas_call | solution.py:245
  16.2 5.4 %collective-permute-done.1.refs_1_.refs_0_ = bf16[64,4096]{1,0:T(8,128)(2,1)S(1)} collective-permute-done((bf16[64,4096]{1,0:T(8,128)(2,1)S(1)}, bf16[64,4096]{1,0:T(8,128)(2,1)S(1)}, u32[]{:S(2)}, u32[]{:S(2)}) %collective-permute-start.1) | collective-permute-done | bytes 524320 | tf_op jit(solution)/shard_map/ppermute | solution.py:47
  21.6 0.0 collective-permute-done.2.refs_2_.refs_1_.refs_0_
  21.6 2.8 %collective-permute-start.6 = (bf16[64,4096]{1,0:T(8,128)(2,1)S(1)}, bf16[64,4096]{1,0:T(8,128)(2,1)S(1)}, u32[]{:S(2)}, u32[]{:S(2)}) collective-permute-start(bf16[64,4096]{1,0:T(8,128)(2,1)S(1)} %hold.1), channel_id=1, source_target_pairs={{0,8},{1,9},{2,10},{3,11},{64,72},{65,73},{66,74},{67,75},{128,136... | collective-permute-start | bytes 1572872 | tf_op jit(solution)/shard_map/ppermute | solution.py:47
  24.5 0.0 collective-permute-done.parcel
  24.5 0.9 pack_other.1
  25.3 0.7 leave.2
  26.0 1.3 %collective-permute-start.8 = (bf16[12,64,512]{2,1,0:T(8,128)(2,1)S(1)}, bf16[12,64,512]{2,1,0:T(8,128)(2,1)S(1)}, u32[]{:S(2)}, u32[]{:S(2)}) collective-permute-start(bf16[12,64,512]{2,1,0:T(8,128)(2,1)S(1)} %leave.2), channel_id=1, source_target_pairs={{0,128},{16,144},{32,160},{48,176},{64,192},{80,208},{96,224},{112... | collective-permute-start | bytes 2359304 | tf_op jit(solution)/shard_map/ppermute | solution.py:213
  27.3 0.9 collective-permute-start.7
  28.2 3.0 %collective-permute-start.4 = (bf16[64,4096]{1,0:T(8,128)(2,1)S(1)}, bf16[64,4096]{1,0:T(8,128)(2,1)S(1)}, u32[]{:S(2)}, u32[]{:S(2)}) collective-permute-start(bf16[64,4096]{1,0:T(8,128)(2,1)S(1)} %get-tuple-element.35), channel_id=1, source_target_pairs={{0,12},{1,13},{2,14},{3,15},{64,76},{65,77},{66,78},{67,79},{128,1... | collective-permute-start | bytes 1572872 | tf_op jit(solution)/shard_map/ppermute | solution.py:47
  31.1 7.0 %collective-permute-done.6.refs_0_ = bf16[64,4096]{1,0:T(8,128)(2,1)S(1)} collective-permute-done((bf16[64,4096]{1,0:T(8,128)(2,1)S(1)}, bf16[64,4096]{1,0:T(8,128)(2,1)S(1)}, u32[]{:S(2)}, u32[]{:S(2)}) %collective-permute-start.6) | collective-permute-done | bytes 524320 | tf_op jit(solution)/shard_map/ppermute | solution.py:47
  38.1 1.6 %collective-permute-start.5 = (bf16[64,4096]{1,0:T(8,128)(2,1)S(1)}, bf16[64,4096]{1,0:T(8,128)(2,1)S(1)}, u32[]{:S(2)}, u32[]{:S(2)}) collective-permute-start(bf16[64,4096]{1,0:T(8,128)(2,1)S(1)} %get-tuple-element.36), channel_id=1, source_target_pairs={{0,4},{1,5},{2,6},{3,7},{64,68},{65,69},{66,70},{67,71},{128,132},... | collective-permute-start | bytes 1572872 | tf_op jit(solution)/shard_map/ppermute | solution.py:47
  39.7 9.7 %collective-permute-done.7.refs_1_ = bf16[64,4096]{1,0:T(8,128)(2,1)S(1)} collective-permute-done((bf16[64,4096]{1,0:T(8,128)(2,1)S(1)}, bf16[64,4096]{1,0:T(8,128)(2,1)S(1)}, u32[]{:S(2)}, u32[]{:S(2)}) %collective-permute-start.7) | collective-permute-done | bytes 524320 | tf_op jit(solution)/shard_map/ppermute | solution.py:47
  49.4 0.0 collective-permute-done.3.refs_3_
  49.4 3.3 %experts.4 = (bf16[64,4096]{1,0:T(8,128)(2,1)S(1)}, bf16[64,4096]{1,0:T(8,128)(2,1)S(1)}) custom-call(bf16[64,4096]{1,0:T(8,128)(2,1)S(1)} %collective-permute-done.6.refs_0_, bf16[64,4096]{1,0:T(8,128)(2,1)S(1)} %collective-permute-done.7.refs_1_, bf16[36864,128]{1,0:T(8,128)(2,1)S(1)} %get-tuple-element.34.refs_2_, ...), custom_call_target="tpu_custom_call" | custom-call | bytes 12582912 | tf_op jit(solution)/shard_map/experts/pallas_call | solution.py:320
  52.7 1.2 %collective-permute-start.9 = (bf16[64,4096]{1,0:T(8,128)(2,1)S(1)}, bf16[64,4096]{1,0:T(8,128)(2,1)S(1)}, u32[]{:S(2)}, u32[]{:S(2)}) collective-permute-start(bf16[64,4096]{1,0:T(8,128)(2,1)S(1)} %get-tuple-element.42), channel_id=1, source_target_pairs={{0,194},{1,3},{2,0},{3,65},{64,2},{65,67},{66,64},{67,129},{128,66... | collective-permute-start | bytes 1572872 | tf_op jit(solution)/shard_map/ppermute | solution.py:47
  54.0 4.9 %collective-permute-done.4.refs_6_.refs_1_ = bf16[64,4096]{1,0:T(8,128)(2,1)S(1)} collective-permute-done((bf16[64,4096]{1,0:T(8,128)(2,1)S(1)}, bf16[64,4096]{1,0:T(8,128)(2,1)S(1)}, u32[]{:S(2)}, u32[]{:S(2)}) %collective-permute-start.4) | collective-permute-done | bytes 524320 | tf_op jit(solution)/shard_map/ppermute | solution.py:47
  58.8 0.0 collective-permute-done.5.refs_1_
  58.8 7.6 %collective-permute-done.8.refs_5_.refs_0_.refs_1_ = bf16[12,64,512]{2,1,0:T(8,128)(2,1)S(1)} collective-permute-done((bf16[12,64,512]{2,1,0:T(8,128)(2,1)S(1)}, bf16[12,64,512]{2,1,0:T(8,128)(2,1)S(1)}, u32[]{:S(2)}, u32[]{:S(2)}) %collective-permute-start.8) | collective-permute-done | bytes 786464 | tf_op jit(solution)/shard_map/ppermute | solution.py:213
  66.4 3.3 %experts.5 = (bf16[64,4096]{1,0:T(8,128)(2,1)S(1)}, bf16[64,4096]{1,0:T(8,128)(2,1)S(1)}) custom-call(bf16[64,4096]{1,0:T(8,128)(2,1)S(1)} %collective-permute-done.1.refs_1_.refs_0_, bf16[64,4096]{1,0:T(8,128)(2,1)S(1)} %collective-permute-done.5.refs_1_, bf16[36864,128]{1,0:T(8,128)(2,1)S(1)} %get-tuple-element.34.refs_2_, ...), custom_call_target="tpu_custom_call" | custom-call | bytes 12582912 | tf_op jit(solution)/shard_map/experts/pallas_call | solution.py:320
  69.8 1.7 %collective-permute-start.11 = (bf16[64,4096]{1,0:T(8,128)(2,1)S(1)}, bf16[64,4096]{1,0:T(8,128)(2,1)S(1)}, u32[]{:S(2)}, u32[]{:S(2)}) collective-permute-start(bf16[64,4096]{1,0:T(8,128)(2,1)S(1)} %get-tuple-element.45), channel_id=1, source_target_pairs={{0,194},{1,3},{2,0},{3,65},{64,2},{65,67},{66,64},{67,129},{128,66... | collective-permute-start | bytes 1572872 | tf_op jit(solution)/shard_map/ppermute | solution.py:47
  71.4 3.4 %experts.6 = (bf16[64,4096]{1,0:T(8,128)(2,1)S(1)}, bf16[64,4096]{1,0:T(8,128)(2,1)S(1)}) custom-call(bf16[64,4096]{1,0:T(8,128)(2,1)S(1)} %collective-permute-done.2.refs_2_.refs_1_.refs_0_, bf16[64,4096]{1,0:T(8,128)(2,1)S(1)} %collective-permute-done.4.refs_6_.refs_1_, bf16[36864,128]{1,0:T(8,128)(2,1)S(1)} %get-tuple-element.34.refs_2_, ...), custom_call_target="tpu_custom_call" | custom-call | bytes 12582912 | tf_op jit(solution)/shard_map/experts/pallas_call | solution.py:320
  74.8 0.1 collective-permute-start.14
  74.9 0.0 collective-permute-done.9.b
  74.9 0.1 add.4.refs_5_
  75.0 1.2 %collective-permute-start.13 = (bf16[64,4096]{1,0:T(8,128)(2,1)S(1)}, bf16[64,4096]{1,0:T(8,128)(2,1)S(1)}, u32[]{:S(2)}, u32[]{:S(2)}) collective-permute-start(bf16[64,4096]{1,0:T(8,128)(2,1)S(1)} %add.4.refs_5_), channel_id=1, source_target_pairs={{0,8},{1,9},{2,10},{3,11},{64,72},{65,73},{66,74},{67,75},{128,136... | collective-permute-start | bytes 1572872 | tf_op jit(solution)/shard_map/ppermute | solution.py:47
  76.2 3.3 %experts.7 = (bf16[64,4096]{1,0:T(8,128)(2,1)S(1)}, bf16[64,4096]{1,0:T(8,128)(2,1)S(1)}) custom-call(bf16[64,4096]{1,0:T(8,128)(2,1)S(1)} %get-tuple-element.28.refs_0_, bf16[64,4096]{1,0:T(8,128)(2,1)S(1)} %get-tuple-element.33.refs_0_.refs_1_, bf16[36864,128]{1,0:T(8,128)(2,1)S(1)} %get-tuple-element.34.refs_2_, ...), custom_call_target="tpu_custom_call" | custom-call | bytes 12582912 | tf_op jit(solution)/shard_map/experts/pallas_call | solution.py:320
  79.6 0.1 collective-permute-start.10
  79.7 0.1 add.6
  79.8 2.7 %collective-permute-start.12 = (bf16[64,4096]{1,0:T(8,128)(2,1)S(1)}, bf16[64,4096]{1,0:T(8,128)(2,1)S(1)}, u32[]{:S(2)}, u32[]{:S(2)}) collective-permute-start(bf16[64,4096]{1,0:T(8,128)(2,1)S(1)} %add.6), channel_id=1, source_target_pairs={{0,12},{1,13},{2,14},{3,15},{64,76},{65,77},{66,78},{67,79},{128,1... | collective-permute-start | bytes 1572872 | tf_op jit(solution)/shard_map/ppermute | solution.py:47
  82.5 2.1 %collective-permute-done.14.b = bf16[64,4096]{1,0:T(8,128)(2,1)S(1)} collective-permute-done((bf16[64,4096]{1,0:T(8,128)(2,1)S(1)}, bf16[64,4096]{1,0:T(8,128)(2,1)S(1)}, u32[]{:S(2)}, u32[]{:S(2)}) %collective-permute-start.14) | collective-permute-done | bytes 524320 | tf_op jit(solution)/shard_map/ppermute | solution.py:47
  84.6 0.1 add.7
  84.8 1.2 %collective-permute-start.15 = (bf16[64,4096]{1,0:T(8,128)(2,1)S(1)}, bf16[64,4096]{1,0:T(8,128)(2,1)S(1)}, u32[]{:S(2)}, u32[]{:S(2)}) collective-permute-start(bf16[64,4096]{1,0:T(8,128)(2,1)S(1)} %add.7), channel_id=1, source_target_pairs={{0,4},{1,5},{2,6},{3,7},{64,68},{65,69},{66,70},{67,71},{128,132},... | collective-permute-start | bytes 1572872 | tf_op jit(solution)/shard_map/ppermute | solution.py:47
  85.9 0.6 leave.3
  86.5 1.3 %collective-permute-start.16 = (bf16[4,64,512]{2,1,0:T(8,128)(2,1)S(1)}, bf16[4,64,512]{2,1,0:T(8,128)(2,1)S(1)}, u32[]{:S(2)}, u32[]{:S(2)}) collective-permute-start(bf16[4,64,512]{2,1,0:T(8,128)(2,1)S(1)} %leave.3), channel_id=1, source_target_pairs={{0,128},{16,144},{32,160},{48,176},{64,192},{80,208},{96,224},{112... | collective-permute-start | bytes 786440 | tf_op jit(solution)/shard_map/ppermute | solution.py:213
  87.8 2.4 %collective-permute-done.10.b = bf16[64,4096]{1,0:T(8,128)(2,1)S(1)} collective-permute-done((bf16[64,4096]{1,0:T(8,128)(2,1)S(1)}, bf16[64,4096]{1,0:T(8,128)(2,1)S(1)}, u32[]{:S(2)}, u32[]{:S(2)}) %collective-permute-start.10) | collective-permute-done | bytes 524320 | tf_op jit(solution)/shard_map/ppermute | solution.py:47
  90.3 0.1 add.5.refs_0_
  90.4 8.7 %collective-permute-done.12.refs_1_ = bf16[64,4096]{1,0:T(8,128)(2,1)S(1)} collective-permute-done((bf16[64,4096]{1,0:T(8,128)(2,1)S(1)}, bf16[64,4096]{1,0:T(8,128)(2,1)S(1)}, u32[]{:S(2)}, u32[]{:S(2)}) %collective-permute-start.12) | collective-permute-done | bytes 524320 | tf_op jit(solution)/shard_map/ppermute | solution.py:47
  99.1 0.0 collective-permute-done.13.refs_2_
  99.1 0.8 collective-permute-done.15.refs_3_
  99.9 2.3 %bring_home.1 = (bf16[128,4096]{1,0:T(8,128)(2,1)}, f32[8,128]{1,0:T(8,128)S(1)}) custom-call(bf16[256,128]{1,0:T(8,128)(2,1)S(1)} %get-tuple-element.26.refs_0_.onehot, bf16[64,4096]{1,0:T(8,128)(2,1)S(1)} %add.5.refs_0_, bf16[64,4096]{1,0:T(8,128)(2,1)S(1)} %collective-permute-done.12.refs_1_, bf16[64,4096]{1,0:T(8,128)(2,1)S(1)} %collective-permute-done.13.refs_2_, ...), custom_call_target="tpu_custom_call" | custom-call | tf_op jit(solution)/shard_map/bring_home/pallas_call | solution.py:367
  102.3 2.0 %collective-permute-done.16.refs_2_ = bf16[4,64,512]{2,1,0:T(8,128)(2,1)S(1)} collective-permute-done((bf16[4,64,512]{2,1,0:T(8,128)(2,1)S(1)}, bf16[4,64,512]{2,1,0:T(8,128)(2,1)S(1)}, u32[]{:S(2)}, u32[]{:S(2)}) %collective-permute-start.16) | collective-permute-done | bytes 262176 | tf_op jit(solution)/shard_map/ppermute | solution.py:213
  104.2 1.0 land.1
  (11 shorter events, 0.1 us)
Async XLA Ops:
  0.6 9.0 %copy-start.3 = (bf16[1,1,4,8192]{3,2,1,0:T(4,128)(2,1)S(1)}, bf16[1,1,4,8192]{3,2,1,0:T(4,128)(2,1)}, u32[]{:S(2)}) copy-start(bf16[1,1,4,8192]{3,2,1,0:T(4,128)(2,1)} %param.9) | copy-start | bytes 196612
  0.6 9.0 %copy-start = (bf16[1,1,2,16,64,512]{5,4,3,2,1,0:T(8,128)(2,1)S(1)}, bf16[1,1,2,16,64,512]{5,4,3,2,1,0:T(8,128)(2,1)}, u32[]{:S(2)}) copy-start(bf16[1,1,2,16,64,512]{5,4,3,2,1,0:T(8,128)(2,1)} %param.10) | copy-start | bytes 6291460
  0.7 9.0 %copy-start.1 = (s32[1,1,4]{2,1,0:T(1,128)S(1)}, s32[1,1,4]{2,1,0:T(1,128)}, u32[]{:S(2)}) copy-start(s32[1,1,4]{2,1,0:T(1,128)} %param.11) | copy-start | bytes 52
  0.7 9.0 %copy-start.2 = (s32[1,1,16]{2,1,0:T(1,128)S(1)}, s32[1,1,16]{2,1,0:T(1,128)}, u32[]{:S(2)}) copy-start(s32[1,1,16]{2,1,0:T(1,128)} %param.12) | copy-start | bytes 196
  5.2 44.1 %collective-permute-start.3 = (bf16[36864,128]{1,0:T(8,128)(2,1)S(1)}, bf16[36864,128]{1,0:T(8,128)(2,1)S(1)}, u32[]{:S(2)}, u32[]{:S(2)}) collective-permute-start(bf16[36864,128]{1,0:T(8,128)(2,1)S(1)} %get-tuple-element.34.refs_2_), channel_id=1, source_target_pairs={{0,1},{1,0},{2,3},{3,2},{64,65},{65,64},{66,67},{67,66},{128,129},... | collective-permute-start | bytes 28311560 | tf_op jit(solution)/shard_map/ppermute | solution.py:47
  5.3 19.1 %collective-permute-start = (bf16[144,4096]{1,0:T(8,128)(2,1)S(1)}, bf16[144,4096]{1,0:T(8,128)(2,1)S(1)}, u32[]{:S(2)}, u32[]{:S(2)}) collective-permute-start(bf16[144,4096]{1,0:T(8,128)(2,1)S(1)} %get-tuple-element.29), channel_id=1, source_target_pairs={{0,2},{1,195},{2,64},{3,1},{64,66},{65,3},{66,128},{67,65},{128,13... | collective-permute-start | bytes 3538952 | tf_op jit(solution)/shard_map/ppermute | solution.py:47
  6.4 15.2 %collective-permute-start.1 = (bf16[64,4096]{1,0:T(8,128)(2,1)S(1)}, bf16[64,4096]{1,0:T(8,128)(2,1)S(1)}, u32[]{:S(2)}, u32[]{:S(2)}) collective-permute-start(bf16[64,4096]{1,0:T(8,128)(2,1)S(1)} %get-tuple-element.31), channel_id=1, source_target_pairs={{0,4},{1,5},{2,6},{3,7},{64,68},{65,69},{66,70},{67,71},{128,132},... | collective-permute-start | bytes 1572872 | tf_op jit(solution)/shard_map/ppermute | solution.py:47
  7.9 13.7 %collective-permute-start.2 = (bf16[64,4096]{1,0:T(8,128)(2,1)S(1)}, bf16[64,4096]{1,0:T(8,128)(2,1)S(1)}, u32[]{:S(2)}, u32[]{:S(2)}) collective-permute-start(bf16[64,4096]{1,0:T(8,128)(2,1)S(1)} %get-tuple-element.32), channel_id=1, source_target_pairs={{0,12},{1,13},{2,14},{3,15},{64,76},{65,77},{66,78},{67,79},{128,1... | collective-permute-start | bytes 1572872 | tf_op jit(solution)/shard_map/ppermute | solution.py:47
  21.6 16.5 %collective-permute-start.6 = (bf16[64,4096]{1,0:T(8,128)(2,1)S(1)}, bf16[64,4096]{1,0:T(8,128)(2,1)S(1)}, u32[]{:S(2)}, u32[]{:S(2)}) collective-permute-start(bf16[64,4096]{1,0:T(8,128)(2,1)S(1)} %hold.1), channel_id=1, source_target_pairs={{0,8},{1,9},{2,10},{3,11},{64,72},{65,73},{66,74},{67,75},{128,136... | collective-permute-start | bytes 1572872 | tf_op jit(solution)/shard_map/ppermute | solution.py:47
  26.0 40.4 %collective-permute-start.8 = (bf16[12,64,512]{2,1,0:T(8,128)(2,1)S(1)}, bf16[12,64,512]{2,1,0:T(8,128)(2,1)S(1)}, u32[]{:S(2)}, u32[]{:S(2)}) collective-permute-start(bf16[12,64,512]{2,1,0:T(8,128)(2,1)S(1)} %leave.2), channel_id=1, source_target_pairs={{0,128},{16,144},{32,160},{48,176},{64,192},{80,208},{96,224},{112... | collective-permute-start | bytes 2359304 | tf_op jit(solution)/shard_map/ppermute | solution.py:213
  27.3 22.1 %collective-permute-start.7 = (bf16[64,4096]{1,0:T(8,128)(2,1)S(1)}, bf16[64,4096]{1,0:T(8,128)(2,1)S(1)}, u32[]{:S(2)}, u32[]{:S(2)}) collective-permute-start(bf16[64,4096]{1,0:T(8,128)(2,1)S(1)} %get-tuple-element.38), channel_id=1, source_target_pairs={{0,8},{1,9},{2,10},{3,11},{64,72},{65,73},{66,74},{67,75},{128,136... | collective-permute-start | bytes 1572872 | tf_op jit(solution)/shard_map/ppermute | solution.py:47
  28.2 30.7 %collective-permute-start.4 = (bf16[64,4096]{1,0:T(8,128)(2,1)S(1)}, bf16[64,4096]{1,0:T(8,128)(2,1)S(1)}, u32[]{:S(2)}, u32[]{:S(2)}) collective-permute-start(bf16[64,4096]{1,0:T(8,128)(2,1)S(1)} %get-tuple-element.35), channel_id=1, source_target_pairs={{0,12},{1,13},{2,14},{3,15},{64,76},{65,77},{66,78},{67,79},{128,1... | collective-permute-start | bytes 1572872 | tf_op jit(solution)/shard_map/ppermute | solution.py:47
  38.1 20.7 %collective-permute-start.5 = (bf16[64,4096]{1,0:T(8,128)(2,1)S(1)}, bf16[64,4096]{1,0:T(8,128)(2,1)S(1)}, u32[]{:S(2)}, u32[]{:S(2)}) collective-permute-start(bf16[64,4096]{1,0:T(8,128)(2,1)S(1)} %get-tuple-element.36), channel_id=1, source_target_pairs={{0,4},{1,5},{2,6},{3,7},{64,68},{65,69},{66,70},{67,71},{128,132},... | collective-permute-start | bytes 1572872 | tf_op jit(solution)/shard_map/ppermute | solution.py:47
  52.7 22.2 %collective-permute-start.9 = (bf16[64,4096]{1,0:T(8,128)(2,1)S(1)}, bf16[64,4096]{1,0:T(8,128)(2,1)S(1)}, u32[]{:S(2)}, u32[]{:S(2)}) collective-permute-start(bf16[64,4096]{1,0:T(8,128)(2,1)S(1)} %get-tuple-element.42), channel_id=1, source_target_pairs={{0,194},{1,3},{2,0},{3,65},{64,2},{65,67},{66,64},{67,129},{128,66... | collective-permute-start | bytes 1572872 | tf_op jit(solution)/shard_map/ppermute | solution.py:47
  69.8 9.9 %collective-permute-start.11 = (bf16[64,4096]{1,0:T(8,128)(2,1)S(1)}, bf16[64,4096]{1,0:T(8,128)(2,1)S(1)}, u32[]{:S(2)}, u32[]{:S(2)}) collective-permute-start(bf16[64,4096]{1,0:T(8,128)(2,1)S(1)} %get-tuple-element.45), channel_id=1, source_target_pairs={{0,194},{1,3},{2,0},{3,65},{64,2},{65,67},{66,64},{67,129},{128,66... | collective-permute-start | bytes 1572872 | tf_op jit(solution)/shard_map/ppermute | solution.py:47
  74.8 9.8 %collective-permute-start.14 = (bf16[64,4096]{1,0:T(8,128)(2,1)S(1)}, bf16[64,4096]{1,0:T(8,128)(2,1)S(1)}, u32[]{:S(2)}, u32[]{:S(2)}) collective-permute-start(bf16[64,4096]{1,0:T(8,128)(2,1)S(1)} %get-tuple-element.46), channel_id=1, source_target_pairs={{0,194},{1,3},{2,0},{3,65},{64,2},{65,67},{66,64},{67,129},{128,66... | collective-permute-start | bytes 1572872 | tf_op jit(solution)/shard_map/ppermute | solution.py:47
  75.0 24.1 %collective-permute-start.13 = (bf16[64,4096]{1,0:T(8,128)(2,1)S(1)}, bf16[64,4096]{1,0:T(8,128)(2,1)S(1)}, u32[]{:S(2)}, u32[]{:S(2)}) collective-permute-start(bf16[64,4096]{1,0:T(8,128)(2,1)S(1)} %add.4.refs_5_), channel_id=1, source_target_pairs={{0,8},{1,9},{2,10},{3,11},{64,72},{65,73},{66,74},{67,75},{128,136... | collective-permute-start | bytes 1572872 | tf_op jit(solution)/shard_map/ppermute | solution.py:47
  79.6 10.7 %collective-permute-start.10 = (bf16[64,4096]{1,0:T(8,128)(2,1)S(1)}, bf16[64,4096]{1,0:T(8,128)(2,1)S(1)}, u32[]{:S(2)}, u32[]{:S(2)}) collective-permute-start(bf16[64,4096]{1,0:T(8,128)(2,1)S(1)} %get-tuple-element.44), channel_id=1, source_target_pairs={{0,194},{1,3},{2,0},{3,65},{64,2},{65,67},{66,64},{67,129},{128,66... | collective-permute-start | bytes 1572872 | tf_op jit(solution)/shard_map/ppermute | solution.py:47
  79.8 19.3 %collective-permute-start.12 = (bf16[64,4096]{1,0:T(8,128)(2,1)S(1)}, bf16[64,4096]{1,0:T(8,128)(2,1)S(1)}, u32[]{:S(2)}, u32[]{:S(2)}) collective-permute-start(bf16[64,4096]{1,0:T(8,128)(2,1)S(1)} %add.6), channel_id=1, source_target_pairs={{0,12},{1,13},{2,14},{3,15},{64,76},{65,77},{66,78},{67,79},{128,1... | collective-permute-start | bytes 1572872 | tf_op jit(solution)/shard_map/ppermute | solution.py:47
  84.8 15.2 %collective-permute-start.15 = (bf16[64,4096]{1,0:T(8,128)(2,1)S(1)}, bf16[64,4096]{1,0:T(8,128)(2,1)S(1)}, u32[]{:S(2)}, u32[]{:S(2)}) collective-permute-start(bf16[64,4096]{1,0:T(8,128)(2,1)S(1)} %add.7), channel_id=1, source_target_pairs={{0,4},{1,5},{2,6},{3,7},{64,68},{65,69},{66,70},{67,71},{128,132},... | collective-permute-start | bytes 1572872 | tf_op jit(solution)/shard_map/ppermute | solution.py:47
  86.5 17.7 %collective-permute-start.16 = (bf16[4,64,512]{2,1,0:T(8,128)(2,1)S(1)}, bf16[4,64,512]{2,1,0:T(8,128)(2,1)S(1)}, u32[]{:S(2)}, u32[]{:S(2)}) collective-permute-start(bf16[4,64,512]{2,1,0:T(8,128)(2,1)S(1)} %leave.3), channel_id=1, source_target_pairs={{0,128},{16,144},{32,160},{48,176},{64,192},{80,208},{96,224},{112... | collective-permute-start | bytes 786440 | tf_op jit(solution)/shard_map/ppermute | solution.py:213

commit v6 on v5

--- a/solution.py
+++ b/solution.py
@@ -21,7 +21,7 @@
 FQ = 384
 NX, NY, NZ, NC = 4, 4, 8, 2
 KB, NB = 2048, 1024
-EARLY = 12
+EARLY = 11
 MIB = 1 << 20
 VMEM = pltpu.VMEM
 SMEM = pltpu.SMEM

time: 106 us -> 106 us (level)
  no operation moved by 1% of the time
where the time goes in v6:
time: 106 us; the launch traced here: 105 us
  waiting for transfers between devices  50.6 us (48%)
  Pallas kernels  30.4 us (29%)
  starting transfers between devices  23.4 us (22%)
    ppermute x15, waiting for transfers between devices, move(): return lax.ppermute(block, ('inst', 'ep'), route)  41.1 us
    ppermute x15, starting transfers between devices, move(): return lax.ppermute(block, ('inst', 'ep'), route)  20.8 us
    pallas_call x4, Pallas kernels, experts(): pl.pallas_call(expert_kernel, out_shape=[jax.ShapeDtypeStruct((CAP, D), j...  13.4 us
    ppermute x2, waiting for transfers between devices, onward(): return lax.ppermute(block, 'inst', [(i, i + 8) for i in range(8)])  9.54 us
    pallas_call x1, Pallas kernels, attend(): pl.pallas_call(attend_kernel, out_shape=[jax.ShapeDtypeStruct((REQS, HEAD...  6.47 us
    pallas_call x1, Pallas kernels, pack(): pl.pallas_call(pack_kernel, out_shape=[jax.ShapeDtypeStruct((NX * CAP, TO...  4.55 us
    ppermute x2, starting transfers between devices, onward(): return lax.ppermute(block, 'inst', [(i, i + 8) for i in range(8)])  2.58 us
    pallas_call x1, Pallas kernels, bring_home(): pl.pallas_call(home_kernel, out_shape=[jax.ShapeDtypeStruct((TOK, D), jnp...  2.32 us
  transfers between devices with their start and end apart: 17, of which 10 were waited for; matrix products, arithmetic and copies ran while one was open for 0% of the time, Pallas kernels for 24%

profile of v6, /device:TPU:216, one launch (start us, length us, event | category | flops | bytes accessed | tf_op | source)
XLA Modules:
  0.0 105.3 jit_solution(7730078301777701302)
XLA Ops:
  0.7 4.6 %pack.1 = (bf16[256,128]{1,0:T(8,128)(2,1)S(1)}, bf16[64,4096]{1,0:T(8,128)(2,1)S(1)}, bf16[64,4096]{1,0:T(8,128)(2,1)S(1)}, bf16[64,4096]{1,0:T(8,128)(2,1)S(1)...) custom-call(s32[1,128]{1,0:T(1,128)} %bitcast.29, ...), custom_call_target="tpu_custom_call" | custom-call | tf_op jit(solution)/shard_map/pack/pallas_call | solution.py:145
  5.2 0.1 collective-permute-start.3
  5.3 1.1 %collective-permute-start = (bf16[144,4096]{1,0:T(8,128)(2,1)S(1)}, bf16[144,4096]{1,0:T(8,128)(2,1)S(1)}, u32[]{:S(2)}, u32[]{:S(2)}) collective-permute-start(bf16[144,4096]{1,0:T(8,128)(2,1)S(1)} %get-tuple-element.29), channel_id=1, source_target_pairs={{0,2},{1,195},{2,64},{3,1},{64,66},{65,3},{66,128},{67,65},{128,13... | collective-permute-start | bytes 3538952 | tf_op jit(solution)/shard_map/ppermute | solution.py:47
  6.4 1.5 %collective-permute-start.1 = (bf16[64,4096]{1,0:T(8,128)(2,1)S(1)}, bf16[64,4096]{1,0:T(8,128)(2,1)S(1)}, u32[]{:S(2)}, u32[]{:S(2)}) collective-permute-start(bf16[64,4096]{1,0:T(8,128)(2,1)S(1)} %get-tuple-element.31), channel_id=1, source_target_pairs={{0,4},{1,5},{2,6},{3,7},{64,68},{65,69},{66,70},{67,71},{128,132},... | collective-permute-start | bytes 1572872 | tf_op jit(solution)/shard_map/ppermute | solution.py:47
  7.9 1.7 %collective-permute-start.2 = (bf16[64,4096]{1,0:T(8,128)(2,1)S(1)}, bf16[64,4096]{1,0:T(8,128)(2,1)S(1)}, u32[]{:S(2)}, u32[]{:S(2)}) collective-permute-start(bf16[64,4096]{1,0:T(8,128)(2,1)S(1)} %get-tuple-element.32), channel_id=1, source_target_pairs={{0,12},{1,13},{2,14},{3,15},{64,76},{65,77},{66,78},{67,79},{128,1... | collective-permute-start | bytes 1572872 | tf_op jit(solution)/shard_map/ppermute | solution.py:47
  9.7 6.5 %attend.1 = (bf16[4,8192]{1,0:T(4,128)(2,1)}, f32[8,128]{1,0:T(8,128)S(1)}) custom-call(s32[4]{0:T(128)S(1)} %bitcast.18, s32[16]{0:T(128)S(1)} %bitcast.21, bf16[4,64,128]{2,1,0:T(8,128)(2,1)S(1)} %bitcast.17, bf16[2,16,64,512]{3,2,1,0:T(8,128)(2,1)S(1)} %bitcast.14, bf16[256,128]{1,0:T(8,128)(2,1)S(1)} %get-tuple-element.26.refs_0_.onehot), custom_call_target="tpu_custom_call" | custom-call | flops 8000000000 | bytes 12582912 | tf_op jit(solution)/shard_map/attend/pallas_call | solution.py:245
  16.2 5.4 %collective-permute-done.1.refs_1_.refs_0_ = bf16[64,4096]{1,0:T(8,128)(2,1)S(1)} collective-permute-done((bf16[64,4096]{1,0:T(8,128)(2,1)S(1)}, bf16[64,4096]{1,0:T(8,128)(2,1)S(1)}, u32[]{:S(2)}, u32[]{:S(2)}) %collective-permute-start.1) | collective-permute-done | bytes 524320 | tf_op jit(solution)/shard_map/ppermute | solution.py:47
  21.6 0.0 collective-permute-done.2.refs_2_.refs_1_.refs_0_
  21.6 2.8 %collective-permute-start.6 = (bf16[64,4096]{1,0:T(8,128)(2,1)S(1)}, bf16[64,4096]{1,0:T(8,128)(2,1)S(1)}, u32[]{:S(2)}, u32[]{:S(2)}) collective-permute-start(bf16[64,4096]{1,0:T(8,128)(2,1)S(1)} %hold.1), channel_id=1, source_target_pairs={{0,8},{1,9},{2,10},{3,11},{64,72},{65,73},{66,74},{67,75},{128,136... | collective-permute-start | bytes 1572872 | tf_op jit(solution)/shard_map/ppermute | solution.py:47
  24.5 0.0 collective-permute-done.parcel
  24.5 0.9 pack_other.1
  25.3 0.7 leave.2
  26.0 1.3 %collective-permute-start.8 = (bf16[11,64,512]{2,1,0:T(8,128)(2,1)S(1)}, bf16[11,64,512]{2,1,0:T(8,128)(2,1)S(1)}, u32[]{:S(2)}, u32[]{:S(2)}) collective-permute-start(bf16[11,64,512]{2,1,0:T(8,128)(2,1)S(1)} %leave.2), channel_id=1, source_target_pairs={{0,128},{16,144},{32,160},{48,176},{64,192},{80,208},{96,224},{112... | collective-permute-start | bytes 2162696 | tf_op jit(solution)/shard_map/ppermute | solution.py:213
  27.3 0.9 collective-permute-start.7
  28.2 3.0 %collective-permute-start.4 = (bf16[64,4096]{1,0:T(8,128)(2,1)S(1)}, bf16[64,4096]{1,0:T(8,128)(2,1)S(1)}, u32[]{:S(2)}, u32[]{:S(2)}) collective-permute-start(bf16[64,4096]{1,0:T(8,128)(2,1)S(1)} %get-tuple-element.35), channel_id=1, source_target_pairs={{0,12},{1,13},{2,14},{3,15},{64,76},{65,77},{66,78},{67,79},{128,1... | collective-permute-start | bytes 1572872 | tf_op jit(solution)/shard_map/ppermute | solution.py:47
  31.1 7.0 %collective-permute-done.6.refs_0_ = bf16[64,4096]{1,0:T(8,128)(2,1)S(1)} collective-permute-done((bf16[64,4096]{1,0:T(8,128)(2,1)S(1)}, bf16[64,4096]{1,0:T(8,128)(2,1)S(1)}, u32[]{:S(2)}, u32[]{:S(2)}) %collective-permute-start.6) | collective-permute-done | bytes 524320 | tf_op jit(solution)/shard_map/ppermute | solution.py:47
  38.1 1.6 %collective-permute-start.5 = (bf16[64,4096]{1,0:T(8,128)(2,1)S(1)}, bf16[64,4096]{1,0:T(8,128)(2,1)S(1)}, u32[]{:S(2)}, u32[]{:S(2)}) collective-permute-start(bf16[64,4096]{1,0:T(8,128)(2,1)S(1)} %get-tuple-element.36), channel_id=1, source_target_pairs={{0,4},{1,5},{2,6},{3,7},{64,68},{65,69},{66,70},{67,71},{128,132},... | collective-permute-start | bytes 1572872 | tf_op jit(solution)/shard_map/ppermute | solution.py:47
  39.7 9.7 %collective-permute-done.7.refs_1_ = bf16[64,4096]{1,0:T(8,128)(2,1)S(1)} collective-permute-done((bf16[64,4096]{1,0:T(8,128)(2,1)S(1)}, bf16[64,4096]{1,0:T(8,128)(2,1)S(1)}, u32[]{:S(2)}, u32[]{:S(2)}) %collective-permute-start.7) | collective-permute-done | bytes 524320 | tf_op jit(solution)/shard_map/ppermute | solution.py:47
  49.4 0.0 collective-permute-done.3.refs_3_
  49.4 3.3 %experts.4 = (bf16[64,4096]{1,0:T(8,128)(2,1)S(1)}, bf16[64,4096]{1,0:T(8,128)(2,1)S(1)}) custom-call(bf16[64,4096]{1,0:T(8,128)(2,1)S(1)} %collective-permute-done.6.refs_0_, bf16[64,4096]{1,0:T(8,128)(2,1)S(1)} %collective-permute-done.7.refs_1_, bf16[36864,128]{1,0:T(8,128)(2,1)S(1)} %get-tuple-element.34.refs_2_, ...), custom_call_target="tpu_custom_call" | custom-call | bytes 12582912 | tf_op jit(solution)/shard_map/experts/pallas_call | solution.py:320
  52.7 1.2 %collective-permute-start.9 = (bf16[64,4096]{1,0:T(8,128)(2,1)S(1)}, bf16[64,4096]{1,0:T(8,128)(2,1)S(1)}, u32[]{:S(2)}, u32[]{:S(2)}) collective-permute-start(bf16[64,4096]{1,0:T(8,128)(2,1)S(1)} %get-tuple-element.42), channel_id=1, source_target_pairs={{0,194},{1,3},{2,0},{3,65},{64,2},{65,67},{66,64},{67,129},{128,66... | collective-permute-start | bytes 1572872 | tf_op jit(solution)/shard_map/ppermute | solution.py:47
  54.0 4.9 %collective-permute-done.4.refs_6_.refs_1_ = bf16[64,4096]{1,0:T(8,128)(2,1)S(1)} collective-permute-done((bf16[64,4096]{1,0:T(8,128)(2,1)S(1)}, bf16[64,4096]{1,0:T(8,128)(2,1)S(1)}, u32[]{:S(2)}, u32[]{:S(2)}) %collective-permute-start.4) | collective-permute-done | bytes 524320 | tf_op jit(solution)/shard_map/ppermute | solution.py:47
  58.8 0.0 collective-permute-done.5.refs_1_
  58.8 4.8 %collective-permute-done.8.refs_5_.refs_0_.refs_1_ = bf16[11,64,512]{2,1,0:T(8,128)(2,1)S(1)} collective-permute-done((bf16[11,64,512]{2,1,0:T(8,128)(2,1)S(1)}, bf16[11,64,512]{2,1,0:T(8,128)(2,1)S(1)}, u32[]{:S(2)}, u32[]{:S(2)}) %collective-permute-start.8) | collective-permute-done | bytes 720928 | tf_op jit(solution)/shard_map/ppermute | solution.py:213
  63.6 3.3 %experts.5 = (bf16[64,4096]{1,0:T(8,128)(2,1)S(1)}, bf16[64,4096]{1,0:T(8,128)(2,1)S(1)}) custom-call(bf16[64,4096]{1,0:T(8,128)(2,1)S(1)} %collective-permute-done.1.refs_1_.refs_0_, bf16[64,4096]{1,0:T(8,128)(2,1)S(1)} %collective-permute-done.5.refs_1_, bf16[36864,128]{1,0:T(8,128)(2,1)S(1)} %get-tuple-element.34.refs_2_, ...), custom_call_target="tpu_custom_call" | custom-call | bytes 12582912 | tf_op jit(solution)/shard_map/experts/pallas_call | solution.py:320
  66.9 1.7 %collective-permute-start.11 = (bf16[64,4096]{1,0:T(8,128)(2,1)S(1)}, bf16[64,4096]{1,0:T(8,128)(2,1)S(1)}, u32[]{:S(2)}, u32[]{:S(2)}) collective-permute-start(bf16[64,4096]{1,0:T(8,128)(2,1)S(1)} %get-tuple-element.45), channel_id=1, source_target_pairs={{0,194},{1,3},{2,0},{3,65},{64,2},{65,67},{66,64},{67,129},{128,66... | collective-permute-start | bytes 1572872 | tf_op jit(solution)/shard_map/ppermute | solution.py:47
  68.6 3.3 %experts.6 = (bf16[64,4096]{1,0:T(8,128)(2,1)S(1)}, bf16[64,4096]{1,0:T(8,128)(2,1)S(1)}) custom-call(bf16[64,4096]{1,0:T(8,128)(2,1)S(1)} %collective-permute-done.2.refs_2_.refs_1_.refs_0_, bf16[64,4096]{1,0:T(8,128)(2,1)S(1)} %collective-permute-done.4.refs_6_.refs_1_, bf16[36864,128]{1,0:T(8,128)(2,1)S(1)} %get-tuple-element.34.refs_2_, ...), custom_call_target="tpu_custom_call" | custom-call | bytes 12582912 | tf_op jit(solution)/shard_map/experts/pallas_call | solution.py:320
  72.0 0.1 collective-permute-start.14
  72.1 0.0 collective-permute-done.9.b
  72.1 0.1 add.4.refs_5_
  72.2 1.2 %collective-permute-start.13 = (bf16[64,4096]{1,0:T(8,128)(2,1)S(1)}, bf16[64,4096]{1,0:T(8,128)(2,1)S(1)}, u32[]{:S(2)}, u32[]{:S(2)}) collective-permute-start(bf16[64,4096]{1,0:T(8,128)(2,1)S(1)} %add.4.refs_5_), channel_id=1, source_target_pairs={{0,8},{1,9},{2,10},{3,11},{64,72},{65,73},{66,74},{67,75},{128,136... | collective-permute-start | bytes 1572872 | tf_op jit(solution)/shard_map/ppermute | solution.py:47
  73.4 3.3 %experts.7 = (bf16[64,4096]{1,0:T(8,128)(2,1)S(1)}, bf16[64,4096]{1,0:T(8,128)(2,1)S(1)}) custom-call(bf16[64,4096]{1,0:T(8,128)(2,1)S(1)} %get-tuple-element.28.refs_0_, bf16[64,4096]{1,0:T(8,128)(2,1)S(1)} %get-tuple-element.33.refs_0_.refs_1_, bf16[36864,128]{1,0:T(8,128)(2,1)S(1)} %get-tuple-element.34.refs_2_, ...), custom_call_target="tpu_custom_call" | custom-call | bytes 12582912 | tf_op jit(solution)/shard_map/experts/pallas_call | solution.py:320
  76.8 0.1 collective-permute-start.10
  76.8 0.0 collective-permute-done.11.b
  76.9 0.1 add.6
  77.0 2.7 %collective-permute-start.12 = (bf16[64,4096]{1,0:T(8,128)(2,1)S(1)}, bf16[64,4096]{1,0:T(8,128)(2,1)S(1)}, u32[]{:S(2)}, u32[]{:S(2)}) collective-permute-start(bf16[64,4096]{1,0:T(8,128)(2,1)S(1)} %add.6), channel_id=1, source_target_pairs={{0,12},{1,13},{2,14},{3,15},{64,76},{65,77},{66,78},{67,79},{128,1... | collective-permute-start | bytes 1572872 | tf_op jit(solution)/shard_map/ppermute | solution.py:47
  79.7 2.1 %collective-permute-done.14.b = bf16[64,4096]{1,0:T(8,128)(2,1)S(1)} collective-permute-done((bf16[64,4096]{1,0:T(8,128)(2,1)S(1)}, bf16[64,4096]{1,0:T(8,128)(2,1)S(1)}, u32[]{:S(2)}, u32[]{:S(2)}) %collective-permute-start.14) | collective-permute-done | bytes 524320 | tf_op jit(solution)/shard_map/ppermute | solution.py:47
  81.8 0.1 add.7
  81.9 1.2 %collective-permute-start.15 = (bf16[64,4096]{1,0:T(8,128)(2,1)S(1)}, bf16[64,4096]{1,0:T(8,128)(2,1)S(1)}, u32[]{:S(2)}, u32[]{:S(2)}) collective-permute-start(bf16[64,4096]{1,0:T(8,128)(2,1)S(1)} %add.7), channel_id=1, source_target_pairs={{0,4},{1,5},{2,6},{3,7},{64,68},{65,69},{66,70},{67,71},{128,132},... | collective-permute-start | bytes 1572872 | tf_op jit(solution)/shard_map/ppermute | solution.py:47
  83.1 0.6 leave.3
  83.7 1.3 %collective-permute-start.16 = (bf16[5,64,512]{2,1,0:T(8,128)(2,1)S(1)}, bf16[5,64,512]{2,1,0:T(8,128)(2,1)S(1)}, u32[]{:S(2)}, u32[]{:S(2)}) collective-permute-start(bf16[5,64,512]{2,1,0:T(8,128)(2,1)S(1)} %leave.3), channel_id=1, source_target_pairs={{0,128},{16,144},{32,160},{48,176},{64,192},{80,208},{96,224},{112... | collective-permute-start | bytes 983048 | tf_op jit(solution)/shard_map/ppermute | solution.py:213
  85.0 2.4 %collective-permute-done.10.b = bf16[64,4096]{1,0:T(8,128)(2,1)S(1)} collective-permute-done((bf16[64,4096]{1,0:T(8,128)(2,1)S(1)}, bf16[64,4096]{1,0:T(8,128)(2,1)S(1)}, u32[]{:S(2)}, u32[]{:S(2)}) %collective-permute-start.10) | collective-permute-done | bytes 524320 | tf_op jit(solution)/shard_map/ppermute | solution.py:47
  87.4 0.1 add.5.refs_0_
  87.5 8.7 %collective-permute-done.12.refs_1_ = bf16[64,4096]{1,0:T(8,128)(2,1)S(1)} collective-permute-done((bf16[64,4096]{1,0:T(8,128)(2,1)S(1)}, bf16[64,4096]{1,0:T(8,128)(2,1)S(1)}, u32[]{:S(2)}, u32[]{:S(2)}) %collective-permute-start.12) | collective-permute-done | bytes 524320 | tf_op jit(solution)/shard_map/ppermute | solution.py:47
  96.3 0.8 collective-permute-done.15.refs_3_
  97.1 2.3 %bring_home.1 = (bf16[128,4096]{1,0:T(8,128)(2,1)}, f32[8,128]{1,0:T(8,128)S(1)}) custom-call(bf16[256,128]{1,0:T(8,128)(2,1)S(1)} %get-tuple-element.26.refs_0_.onehot, bf16[64,4096]{1,0:T(8,128)(2,1)S(1)} %add.5.refs_0_, bf16[64,4096]{1,0:T(8,128)(2,1)S(1)} %collective-permute-done.12.refs_1_, bf16[64,4096]{1,0:T(8,128)(2,1)S(1)} %collective-permute-done.13.refs_2_, ...), custom_call_target="tpu_custom_call" | custom-call | tf_op jit(solution)/shard_map/bring_home/pallas_call | solution.py:367
  99.4 4.8 %collective-permute-done.16.refs_2_ = bf16[5,64,512]{2,1,0:T(8,128)(2,1)S(1)} collective-permute-done((bf16[5,64,512]{2,1,0:T(8,128)(2,1)S(1)}, bf16[5,64,512]{2,1,0:T(8,128)(2,1)S(1)}, u32[]{:S(2)}, u32[]{:S(2)}) %collective-permute-start.16) | collective-permute-done | bytes 327712 | tf_op jit(solution)/shard_map/ppermute | solution.py:213
  104.2 1.0 land.1
  (11 shorter events, 0.1 us)
Async XLA Ops:
  0.6 9.0 %copy-start.3 = (bf16[1,1,4,8192]{3,2,1,0:T(4,128)(2,1)S(1)}, bf16[1,1,4,8192]{3,2,1,0:T(4,128)(2,1)}, u32[]{:S(2)}) copy-start(bf16[1,1,4,8192]{3,2,1,0:T(4,128)(2,1)} %param.9) | copy-start | bytes 196612
  0.6 9.0 %copy-start = (bf16[1,1,2,16,64,512]{5,4,3,2,1,0:T(8,128)(2,1)S(1)}, bf16[1,1,2,16,64,512]{5,4,3,2,1,0:T(8,128)(2,1)}, u32[]{:S(2)}) copy-start(bf16[1,1,2,16,64,512]{5,4,3,2,1,0:T(8,128)(2,1)} %param.10) | copy-start | bytes 6291460
  0.7 9.0 %copy-start.1 = (s32[1,1,4]{2,1,0:T(1,128)S(1)}, s32[1,1,4]{2,1,0:T(1,128)}, u32[]{:S(2)}) copy-start(s32[1,1,4]{2,1,0:T(1,128)} %param.11) | copy-start | bytes 52
  0.7 9.0 %copy-start.2 = (s32[1,1,16]{2,1,0:T(1,128)S(1)}, s32[1,1,16]{2,1,0:T(1,128)}, u32[]{:S(2)}) copy-start(s32[1,1,16]{2,1,0:T(1,128)} %param.12) | copy-start | bytes 196
  5.2 44.1 %collective-permute-start.3 = (bf16[36864,128]{1,0:T(8,128)(2,1)S(1)}, bf16[36864,128]{1,0:T(8,128)(2,1)S(1)}, u32[]{:S(2)}, u32[]{:S(2)}) collective-permute-start(bf16[36864,128]{1,0:T(8,128)(2,1)S(1)} %get-tuple-element.34.refs_2_), channel_id=1, source_target_pairs={{0,1},{1,0},{2,3},{3,2},{64,65},{65,64},{66,67},{67,66},{128,129},... | collective-permute-start | bytes 28311560 | tf_op jit(solution)/shard_map/ppermute | solution.py:47
  5.3 19.1 %collective-permute-start = (bf16[144,4096]{1,0:T(8,128)(2,1)S(1)}, bf16[144,4096]{1,0:T(8,128)(2,1)S(1)}, u32[]{:S(2)}, u32[]{:S(2)}) collective-permute-start(bf16[144,4096]{1,0:T(8,128)(2,1)S(1)} %get-tuple-element.29), channel_id=1, source_target_pairs={{0,2},{1,195},{2,64},{3,1},{64,66},{65,3},{66,128},{67,65},{128,13... | collective-permute-start | bytes 3538952 | tf_op jit(solution)/shard_map/ppermute | solution.py:47
  6.4 15.2 %collective-permute-start.1 = (bf16[64,4096]{1,0:T(8,128)(2,1)S(1)}, bf16[64,4096]{1,0:T(8,128)(2,1)S(1)}, u32[]{:S(2)}, u32[]{:S(2)}) collective-permute-start(bf16[64,4096]{1,0:T(8,128)(2,1)S(1)} %get-tuple-element.31), channel_id=1, source_target_pairs={{0,4},{1,5},{2,6},{3,7},{64,68},{65,69},{66,70},{67,71},{128,132},... | collective-permute-start | bytes 1572872 | tf_op jit(solution)/shard_map/ppermute | solution.py:47
  7.9 13.7 %collective-permute-start.2 = (bf16[64,4096]{1,0:T(8,128)(2,1)S(1)}, bf16[64,4096]{1,0:T(8,128)(2,1)S(1)}, u32[]{:S(2)}, u32[]{:S(2)}) collective-permute-start(bf16[64,4096]{1,0:T(8,128)(2,1)S(1)} %get-tuple-element.32), channel_id=1, source_target_pairs={{0,12},{1,13},{2,14},{3,15},{64,76},{65,77},{66,78},{67,79},{128,1... | collective-permute-start | bytes 1572872 | tf_op jit(solution)/shard_map/ppermute | solution.py:47
  21.6 16.5 %collective-permute-start.6 = (bf16[64,4096]{1,0:T(8,128)(2,1)S(1)}, bf16[64,4096]{1,0:T(8,128)(2,1)S(1)}, u32[]{:S(2)}, u32[]{:S(2)}) collective-permute-start(bf16[64,4096]{1,0:T(8,128)(2,1)S(1)} %hold.1), channel_id=1, source_target_pairs={{0,8},{1,9},{2,10},{3,11},{64,72},{65,73},{66,74},{67,75},{128,136... | collective-permute-start | bytes 1572872 | tf_op jit(solution)/shard_map/ppermute | solution.py:47
  26.0 37.6 %collective-permute-start.8 = (bf16[11,64,512]{2,1,0:T(8,128)(2,1)S(1)}, bf16[11,64,512]{2,1,0:T(8,128)(2,1)S(1)}, u32[]{:S(2)}, u32[]{:S(2)}) collective-permute-start(bf16[11,64,512]{2,1,0:T(8,128)(2,1)S(1)} %leave.2), channel_id=1, source_target_pairs={{0,128},{16,144},{32,160},{48,176},{64,192},{80,208},{96,224},{112... | collective-permute-start | bytes 2162696 | tf_op jit(solution)/shard_map/ppermute | solution.py:213
  27.3 22.1 %collective-permute-start.7 = (bf16[64,4096]{1,0:T(8,128)(2,1)S(1)}, bf16[64,4096]{1,0:T(8,128)(2,1)S(1)}, u32[]{:S(2)}, u32[]{:S(2)}) collective-permute-start(bf16[64,4096]{1,0:T(8,128)(2,1)S(1)} %get-tuple-element.38), channel_id=1, source_target_pairs={{0,8},{1,9},{2,10},{3,11},{64,72},{65,73},{66,74},{67,75},{128,136... | collective-permute-start | bytes 1572872 | tf_op jit(solution)/shard_map/ppermute | solution.py:47
  28.2 30.7 %collective-permute-start.4 = (bf16[64,4096]{1,0:T(8,128)(2,1)S(1)}, bf16[64,4096]{1,0:T(8,128)(2,1)S(1)}, u32[]{:S(2)}, u32[]{:S(2)}) collective-permute-start(bf16[64,4096]{1,0:T(8,128)(2,1)S(1)} %get-tuple-element.35), channel_id=1, source_target_pairs={{0,12},{1,13},{2,14},{3,15},{64,76},{65,77},{66,78},{67,79},{128,1... | collective-permute-start | bytes 1572872 | tf_op jit(solution)/shard_map/ppermute | solution.py:47
  38.1 20.7 %collective-permute-start.5 = (bf16[64,4096]{1,0:T(8,128)(2,1)S(1)}, bf16[64,4096]{1,0:T(8,128)(2,1)S(1)}, u32[]{:S(2)}, u32[]{:S(2)}) collective-permute-start(bf16[64,4096]{1,0:T(8,128)(2,1)S(1)} %get-tuple-element.36), channel_id=1, source_target_pairs={{0,4},{1,5},{2,6},{3,7},{64,68},{65,69},{66,70},{67,71},{128,132},... | collective-permute-start | bytes 1572872 | tf_op jit(solution)/shard_map/ppermute | solution.py:47
  52.7 19.3 %collective-permute-start.9 = (bf16[64,4096]{1,0:T(8,128)(2,1)S(1)}, bf16[64,4096]{1,0:T(8,128)(2,1)S(1)}, u32[]{:S(2)}, u32[]{:S(2)}) collective-permute-start(bf16[64,4096]{1,0:T(8,128)(2,1)S(1)} %get-tuple-element.42), channel_id=1, source_target_pairs={{0,194},{1,3},{2,0},{3,65},{64,2},{65,67},{66,64},{67,129},{128,66... | collective-permute-start | bytes 1572872 | tf_op jit(solution)/shard_map/ppermute | solution.py:47
  66.9 9.9 %collective-permute-start.11 = (bf16[64,4096]{1,0:T(8,128)(2,1)S(1)}, bf16[64,4096]{1,0:T(8,128)(2,1)S(1)}, u32[]{:S(2)}, u32[]{:S(2)}) collective-permute-start(bf16[64,4096]{1,0:T(8,128)(2,1)S(1)} %get-tuple-element.45), channel_id=1, source_target_pairs={{0,194},{1,3},{2,0},{3,65},{64,2},{65,67},{66,64},{67,129},{128,66... | collective-permute-start | bytes 1572872 | tf_op jit(solution)/shard_map/ppermute | solution.py:47
  72.0 9.8 %collective-permute-start.14 = (bf16[64,4096]{1,0:T(8,128)(2,1)S(1)}, bf16[64,4096]{1,0:T(8,128)(2,1)S(1)}, u32[]{:S(2)}, u32[]{:S(2)}) collective-permute-start(bf16[64,4096]{1,0:T(8,128)(2,1)S(1)} %get-tuple-element.46), channel_id=1, source_target_pairs={{0,194},{1,3},{2,0},{3,65},{64,2},{65,67},{66,64},{67,129},{128,66... | collective-permute-start | bytes 1572872 | tf_op jit(solution)/shard_map/ppermute | solution.py:47
  72.2 24.1 %collective-permute-start.13 = (bf16[64,4096]{1,0:T(8,128)(2,1)S(1)}, bf16[64,4096]{1,0:T(8,128)(2,1)S(1)}, u32[]{:S(2)}, u32[]{:S(2)}) collective-permute-start(bf16[64,4096]{1,0:T(8,128)(2,1)S(1)} %add.4.refs_5_), channel_id=1, source_target_pairs={{0,8},{1,9},{2,10},{3,11},{64,72},{65,73},{66,74},{67,75},{128,136... | collective-permute-start | bytes 1572872 | tf_op jit(solution)/shard_map/ppermute | solution.py:47
  76.8 10.7 %collective-permute-start.10 = (bf16[64,4096]{1,0:T(8,128)(2,1)S(1)}, bf16[64,4096]{1,0:T(8,128)(2,1)S(1)}, u32[]{:S(2)}, u32[]{:S(2)}) collective-permute-start(bf16[64,4096]{1,0:T(8,128)(2,1)S(1)} %get-tuple-element.44), channel_id=1, source_target_pairs={{0,194},{1,3},{2,0},{3,65},{64,2},{65,67},{66,64},{67,129},{128,66... | collective-permute-start | bytes 1572872 | tf_op jit(solution)/shard_map/ppermute | solution.py:47
  77.0 19.3 %collective-permute-start.12 = (bf16[64,4096]{1,0:T(8,128)(2,1)S(1)}, bf16[64,4096]{1,0:T(8,128)(2,1)S(1)}, u32[]{:S(2)}, u32[]{:S(2)}) collective-permute-start(bf16[64,4096]{1,0:T(8,128)(2,1)S(1)} %add.6), channel_id=1, source_target_pairs={{0,12},{1,13},{2,14},{3,15},{64,76},{65,77},{66,78},{67,79},{128,1... | collective-permute-start | bytes 1572872 | tf_op jit(solution)/shard_map/ppermute | solution.py:47
  81.9 15.2 %collective-permute-start.15 = (bf16[64,4096]{1,0:T(8,128)(2,1)S(1)}, bf16[64,4096]{1,0:T(8,128)(2,1)S(1)}, u32[]{:S(2)}, u32[]{:S(2)}) collective-permute-start(bf16[64,4096]{1,0:T(8,128)(2,1)S(1)} %add.7), channel_id=1, source_target_pairs={{0,4},{1,5},{2,6},{3,7},{64,68},{65,69},{66,70},{67,71},{128,132},... | collective-permute-start | bytes 1572872 | tf_op jit(solution)/shard_map/ppermute | solution.py:47
  83.7 20.5 %collective-permute-start.16 = (bf16[5,64,512]{2,1,0:T(8,128)(2,1)S(1)}, bf16[5,64,512]{2,1,0:T(8,128)(2,1)S(1)}, u32[]{:S(2)}, u32[]{:S(2)}) collective-permute-start(bf16[5,64,512]{2,1,0:T(8,128)(2,1)S(1)} %leave.3), channel_id=1, source_target_pairs={{0,128},{16,144},{32,160},{48,176},{64,192},{80,208},{96,224},{112... | collective-permute-start | bytes 983048 | tf_op jit(solution)/shard_map/ppermute | solution.py:213
